TPU v7x, 512 devices: a whole 4x8x8 slice. The times are simulated.
512 devices in a mesh: side: 2 (over core), grp: 8 (over y), dev: 32 (over x, z).
Axes of the slice: x: 4, y: 8, z: 8, core: 2. Of those that a mesh axis runs over, the one named last changes fastest.
Arguments:
- tokens: bfloat16 [1024, 7168], P(('side', 'grp', 'dev')), may hold values from -6 to 6
- expert_ids: int32 [1024, 8], P(('side', 'grp', 'dev')), may hold values from 0 to 31, all different within a row; in each aligned block of 64 rows (0 to 63, 64 to 127, ...) at most 32 rows name the same one
- route_weights: bfloat16 [1024, 8], P(('side', 'grp', 'dev')), may hold values from 0.19921875 to 1.5
- w_gate: bfloat16 [32, 7168, 2048], P('dev', None, ('side', 'grp')), may hold values from -0.0625 to 0.0625
- w_down: bfloat16 [32, 2048, 7168], P('dev', None, ('side', 'grp')), may hold values from -0.125 to 0.125
Outputs:
- mixed: bfloat16 [1024, 7168], P(('side', 'grp', 'dev'))
Inputs may be any that keep to these rules, and one draw needn't show every extreme that they name: `expert_ids`: each token names 8 different experts. In each aligned block of 64 tokens (the tokens of one group of devices along dev) no expert is named by more than 32 tokens, and in some block one expert is named by exactly 32.
All inputs are finite; a program needn't handle non-finite values.
Results may differ from a plain program's by a relative error of at most 0.0075.
Values may be sent and summed in bfloat16 or wider, within the bound.
No kernel may reach another device: no remote copies, remote signals or barrier semaphores. Data moves between devices by JAX's collectives and lax.ppermute only.
A program may use at most 64 MiB of HBM per device.

v0:
```python
import jax
import jax.numpy as jnp
from jax import lax
from jax.sharding import PartitionSpec as P

CAP = 32


def rms_rows(tokens):
    values = tokens.astype(jnp.float32)
    scale = lax.rsqrt(jnp.mean(values * values, axis=1, keepdims=True) + 1e-06)
    return (values * scale).astype(jnp.bfloat16)


def on_device(tokens, expert_ids, route_weights, w_gate, w_down):
    normed = rms_rows(tokens)
    group_rows, group_weights, group_ids = (
        lax.all_gather(normed, "dev", axis=0, tiled=True),
        lax.all_gather(route_weights, "dev", axis=0, tiled=True),
        lax.all_gather(expert_ids, "dev", axis=0, tiled=True),
    )
    expert = lax.axis_index("dev")
    match = group_ids == expert
    hit = jnp.any(match, axis=1)
    hit_int = hit.astype(jnp.int32)
    slot = jnp.cumsum(hit_int) - hit_int
    placed = (slot[None, :] == jnp.arange(CAP, dtype=jnp.int32)[:, None]) & hit[None, :]
    slot_input = jnp.dot(
        placed.astype(jnp.bfloat16), group_rows, preferred_element_type=jnp.float32
    ).astype(jnp.bfloat16)
    gate_slab = w_gate[0]
    down_slab = w_down[0]
    gate = jnp.dot(
        lax.all_gather(slot_input, ("side", "grp"), axis=0, tiled=True),
        gate_slab,
        preferred_element_type=jnp.float32,
    )
    hidden = jax.nn.silu(gate).astype(jnp.bfloat16)
    columns = jnp.dot(
        lax.all_gather(hidden, ("side", "grp"), axis=1, tiled=True),
        down_slab,
        preferred_element_type=jnp.float32,
    ).astype(jnp.bfloat16)
    expert_out = lax.all_to_all(columns, ("side", "grp"), split_axis=0, concat_axis=1, tiled=True)
    row_weight = jnp.sum(jnp.where(match, group_weights.astype(jnp.float32), 0.0), axis=1)
    combine_matrix = placed.T.astype(jnp.float32) * row_weight[:, None]
    output_values = expert_out.astype(jnp.float32)
    mixed = lax.psum_scatter(
        jnp.dot(combine_matrix, output_values, precision=lax.Precision.HIGHEST),
        "dev",
        scatter_dimension=0,
        tiled=True,
    )
    return mixed.astype(jnp.bfloat16)


def solution(mesh):
    in_specs = (
        P(("side", "grp", "dev"), None),
        P(("side", "grp", "dev"), None),
        P(("side", "grp", "dev"), None),
        P("dev", None, ("side", "grp")),
        P("dev", None, ("side", "grp")),
    )
    out_specs = P(("side", "grp", "dev"), None)
    return jax.shard_map(
        on_device, mesh=mesh, in_specs=in_specs, out_specs=out_specs, check_vma=False
    )
```

profile of v0, /device:TPU:16, one launch (start us, length us, event | category | flops | bytes accessed | tf_op | source)
XLA Modules:
  0.0 433.0 jit_solution(8307281467319152819)
XLA Ops:
  6.5 0.0 copy-start
  6.5 0.0 all-gather.6.cloned.1.call-start
  6.5 1.1 fusion.9
  7.6 0.8 fusion.15
  8.4 49.0 %all-gather = s32[32,2,8]{2,1,0:T(2,128)S(1)} all-gather(s32[1,2,8]{2,1,0:T(2,128)} %bitcast.24), channel_id=1, replica_groups=mesh['side'=2,'grp'=8,'dev'=32] {'dev'}, dimensions={0}, use_global_device_ids=true | all-gather | bytes 2112 | tf_op jit(solution)/shard_map/all_gather | solution.py:20
  57.4 0.6 fusion.24
  58.1 0.1 reshape.59
  58.2 0.1 copy.10
  58.3 0.1 reduce-window.8
  58.4 0.1 reduce.2
  58.5 49.0 %all-gather.2 = bf16[32,2,7168]{2,1,0:T(2,128)(2,1)S(1)} all-gather(bf16[1,2,7168]{2,1,0:T(2,128)(2,1)S(1)} %fusion.15), channel_id=1, replica_groups=mesh['side'=2,'grp'=8,'dev'=32] {'dev'}, dimensions={0}, use_global_device_ids=true | all-gather | bytes 946176 | tf_op jit(solution)/shard_map/all_gather | solution.py:18
  107.5 1.3 reshape.55
  108.8 2.2 convolution_convert_fusion
  111.0 0.0 all-gather.6.cloned.1.call-update
  111.0 0.0 all-gather.8.cloned.1.call-start
  111.1 48.1 %all-gather.6.cloned.1.call-done = bf16[512,7168]{1,0:T(8,128)(2,1)} async-done(((bf16[32,7168]{1,0:T(8,128)(2,1)}), bf16[512,7168]{1,0:T(8,128)(2,1)}) %all-gather.6.cloned.1.call-update) | async-done | bytes 7340048 | tf_op jit(solution)/shard_map/all_gather | solution.py:34
  159.2 6.3 %multiply_convert_fusion = bf16[512,128]{1,0:T(8,128)(2,1)} fusion(bf16[512,7168]{1,0:T(8,128)(2,1)} %all-gather.6.cloned.1.call-done, bf16[1,7168,128]{2,1,0:T(8,128)(2,1)} %param.8), kind=kOutput, calls=%fused_computation.6 | convolution fusion | flops 939851776 | bytes 9306112 | tf_op jit(solution)/shard_map/dot_general | solution.py:33
  165.5 0.0 all-gather.8.cloned.1.call-update
  165.5 42.9 %all-gather.8.cloned.1.call-done = bf16[512,2048]{1,0:T(8,128)(2,1)} async-done(((bf16[512,128]{1,0:T(8,128)(2,1)}), bf16[512,2048]{1,0:T(8,128)(2,1)}) %all-gather.8.cloned.1.call-update) | async-done | bytes 2097168 | tf_op jit(solution)/shard_map/all_gather | solution.py:40
  208.5 0.0 copy-done
  208.5 2.7 fusion.4
  211.2 0.0 copy-start.1
  211.2 1.0 copy.11
  212.2 6.0 %all-to-all-start = ((bf16[16,32,448]{2,1,0:T(8,128)(2,1)}), bf16[16,32,448]{2,1,0:T(8,128)(2,1)S(1)}, u32[]{:S(2)}, u32[]{:S(2)}) async-start(bf16[16,32,448]{2,1,0:T(8,128)(2,1)} %bitcast.6), calls=%async_computation | async-start | bytes 1048576 | tf_op jit(solution)/shard_map/all_to_all | solution.py:44
  218.2 0.0 copy-done.1
  218.2 40.6 %all-gather.1 = bf16[32,2,8]{2,1,0:T(2,128)(2,1)S(1)} all-gather(bf16[1,2,8]{2,1,0:T(2,128)(2,1)S(1)} %bitcast.25), channel_id=1, replica_groups=mesh['side'=2,'grp'=8,'dev'=32] {'dev'}, dimensions={0}, use_global_device_ids=true | all-gather | bytes 1056 | tf_op jit(solution)/shard_map/all_gather | solution.py:19
  258.8 0.1 select_reduce_fusion
  258.9 0.1 reshape.62
  259.1 1.3 dynamic-slice
  261.0 0.0 all-to-all-done
  261.0 0.3 copy.12
  261.3 0.6 all_to_all.17
  261.9 2.2 fusion.11
  264.1 161.4 %all-reduce.2 = bf16[64,7168]{1,0:T(8,128)(2,1)S(1)} all-reduce(f32[64,7168]{1,0:T(8,128)} %fusion.11), channel_id=2, replica_groups=mesh['side'=2,'grp'=8,'dev'=32] {'dev'}, use_global_device_ids=true, to_apply=%region_4.5.clone | all-reduce | flops 458752 | bytes 2752512
  425.5 0.6 dynamic-slice_convert_fusion
  (3 shorter events, 0.0 us)
Async XLA Ops:
  6.5 202.0 %copy-start = (bf16[1,2048,448]{1,2,0:T(8,128)(2,1)S(1)}, bf16[1,2048,448]{1,2,0:T(8,128)(2,1)}, u32[]{:S(2)}) copy-start(bf16[1,2048,448]{1,2,0:T(8,128)(2,1)} %param.9) | copy-start | bytes 5505028
  6.5 152.7 %all-gather.6.cloned.1.call-start = ((), (), s32[]{:S(2)}) async-start(), calls=%async_computation.1 | async-start | bytes 7798784 | tf_op jit(solution)/shard_map/all_gather | solution.py:34
  111.0 97.5 %all-gather.8.cloned.1.call-start = ((), (), s32[]{:S(2)}) async-start(), calls=%async_computation.2 | async-start | bytes 2228224 | tf_op jit(solution)/shard_map/all_gather | solution.py:40
  211.2 7.0 %copy-start.1 = (bf16[2,8]{1,0:T(2,128)(2,1)S(1)}, bf16[2,8]{1,0:T(2,128)(2,1)}, u32[]{:S(2)}) copy-start(bf16[2,8]{1,0:T(2,128)(2,1)} %param.7) | copy-start | bytes 100
  212.2 48.7 %all-to-all-start = ((bf16[16,32,448]{2,1,0:T(8,128)(2,1)}), bf16[16,32,448]{2,1,0:T(8,128)(2,1)S(1)}, u32[]{:S(2)}, u32[]{:S(2)}) async-start(bf16[16,32,448]{2,1,0:T(8,128)(2,1)} %bitcast.6), calls=%async_computation | async-start | bytes 1048576 | tf_op jit(solution)/shard_map/all_to_all | solution.py:44
Sparse Core Ops, SparseCore 0:
  111.2 48.0 all-gather.5
  165.7 42.7 all-gather.7
where the time goes:
time: 434 us; the launch traced here: 433 us
  blocking collectives  300 us (69%)
  waiting for transfers between devices  91.1 us (21%)
  between operations  14.1 us (3%)
  matrix products  13.4 us (3%)
  starting transfers between devices  6.01 us (1%)
  local copies, waits for them, and re-layouts  5.41 us (1%)
    unnamed x1, blocking collectives  161 us
    all_gather x1, blocking collectives, on_device(): lax.all_gather(normed, 'dev', axis=0, tiled=True)  49 us
    all_gather x1, blocking collectives, on_device(): lax.all_gather(expert_ids, 'dev', axis=0, tiled=True)  49 us
    all_gather x1, waiting for transfers between devices, on_device(): lax.all_gather(slot_input, ('side', 'grp'), axis=0, tiled=True)  48.1 us
    all_gather x1, waiting for transfers between devices, on_device(): lax.all_gather(hidden, ('side', 'grp'), axis=1, tiled=True)  42.9 us
    all_gather x1, blocking collectives, on_device(): lax.all_gather(route_weights, 'dev', axis=0, tiled=True)  40.6 us
  transfers between devices with their start and end apart: 3, of which 2 were waited for; matrix products, arithmetic and copies ran while one was open for 0% of the time, Pallas kernels for 0%

commit v1 on v0

v1 whole, which is shorter than its diff:
```python
import jax
import jax.numpy as jnp
from jax import lax
from jax.sharding import Mesh, PartitionSpec as P

CAP = 32
TOPK = 8
TAIL = 128


def rms_rows(tokens):
    values = tokens.astype(jnp.float32)
    scale = lax.rsqrt(jnp.mean(values * values, axis=1, keepdims=True) + 1e-06)
    return (values * scale).astype(jnp.bfloat16)


def side_by_side(own, side):
    other = lax.ppermute(own, "side", [(0, 1), (1, 0)])
    first = jnp.where(side == 0, own, other)
    second = jnp.where(side == 0, other, own)
    return jnp.concatenate([first, second], axis=1)


def on_device(tokens, expert_ids, route_weights, w_gate, w_down):
    bf16, f32, i32 = jnp.bfloat16, jnp.float32, jnp.int32
    rows, width = tokens.shape
    n_side, n_grp = lax.axis_size("side"), lax.axis_size("grp")
    n_x, n_z = lax.axis_size("x"), lax.axis_size("z")
    n_dev = n_x * n_z
    side = lax.axis_index("side")
    dev = lax.axis_index("x") * n_z + lax.axis_index("z")
    unit = w_gate.shape[2]

    gate_slab = jnp.pad(side_by_side(w_gate[0], side), ((0, TAIL), (0, 0)))
    down_slab = side_by_side(w_down[0], side)
    down_slab = (
        down_slab.reshape(n_side, n_grp, unit, -1)
        .transpose(1, 0, 2, 3)
        .reshape(n_side * n_grp * unit, -1)
    )

    place = (dev * rows + jnp.arange(rows, dtype=i32)).astype(bf16)
    tail = jnp.concatenate([expert_ids.astype(bf16), route_weights, place[:, None]], axis=1)
    sent = jnp.concatenate(
        [rms_rows(tokens), jnp.pad(tail, ((0, 0), (0, TAIL - 2 * TOPK - 1)))], axis=1
    )
    by_z = lax.all_to_all(
        jnp.broadcast_to(sent[None], (n_z,) + sent.shape), "z", split_axis=0, concat_axis=0, tiled=True
    ).reshape(n_z * rows, -1)
    packed = lax.all_gather(by_z, "x", axis=0, tiled=True)

    group = n_dev * rows
    hit = jnp.any(packed[:, width : width + TOPK].astype(i32) == dev, axis=1)
    before = jnp.arange(group)[:, None] < jnp.arange(group)[None, :]
    slot = jnp.sum((before & hit[:, None]).astype(i32), axis=0)
    placed = (slot[None, :] == jnp.arange(CAP, dtype=i32)[:, None]) & hit[None, :]
    slot_input = jnp.dot(placed.astype(bf16), packed, preferred_element_type=f32).astype(bf16)
    inputs = lax.all_gather(slot_input, "grp", axis=0, tiled=True)

    hidden = jax.nn.silu(jnp.dot(inputs, gate_slab, preferred_element_type=f32)).astype(bf16)
    columns = jnp.dot(
        lax.all_gather(hidden, "grp", axis=1, tiled=True), down_slab, preferred_element_type=f32
    ).astype(bf16)

    slots = n_grp * CAP
    notes = inputs[:, width:]
    ids = notes[:, :TOPK].astype(i32)
    weight = jnp.sum(
        jnp.where(ids == dev, notes[:, TOPK : 2 * TOPK].astype(f32), 0.0), axis=1
    ).astype(bf16)
    place = notes[:, 2 * TOPK].astype(i32)
    of_group = jnp.arange(slots, dtype=i32) // CAP
    target = (place // rows) * (n_grp * rows) + of_group * rows + place % rows
    combine = jnp.where(
        jnp.arange(n_grp * group, dtype=i32)[:, None] == target[None, :],
        weight[None, :],
        jnp.zeros((), bf16),
    )
    weighted = jnp.dot(combine, columns, preferred_element_type=f32).astype(bf16)
    over_x = lax.all_to_all(
        weighted.reshape(n_x, n_z * n_grp * rows, -1), "x", split_axis=0, concat_axis=0, tiled=True
    )
    total_x = jnp.sum(over_x.astype(f32), axis=0).astype(bf16)
    over_zy = lax.all_to_all(
        total_x.reshape(n_z * n_grp, rows, -1), ("z", "grp"), split_axis=0, concat_axis=0, tiled=True
    )
    total = jnp.sum(over_zy.reshape(n_z, n_grp, rows, -1).astype(f32), axis=0).astype(bf16)
    mixed = total.reshape(n_grp, rows, n_side, -1).transpose(1, 2, 0, 3)
    return mixed.reshape(rows, width)


def solution(mesh):
    side, grp, dev = mesh.devices.shape
    n_z = 8
    fine = Mesh(mesh.devices.reshape(side, grp, dev // n_z, n_z), ("side", "grp", "x", "z"))
    row_axes = ("side", "grp", "x", "z")
    in_specs = (
        P(row_axes, None),
        P(row_axes, None),
        P(row_axes, None),
        P(("x", "z"), None, ("side", "grp")),
        P(("x", "z"), None, ("side", "grp")),
    )
    return jax.shard_map(
        on_device, mesh=fine, in_specs=in_specs, out_specs=P(row_axes, None), check_vma=False
    )
```

time: 434 us -> 194 us (0.45)
  the two profiles are of different devices: /device:TPU:16 before, /device:TPU:8 now
where the time goes in v1:
time: 194 us; the launch traced here: 193 us
  blocking collectives  74.8 us (39%)
  waiting for transfers between devices  67.6 us (35%)
  between operations  13.5 us (7%)
  other arithmetic  12.7 us (7%)
  local copies, waits for them, and re-layouts  10.2 us (5%)
  matrix products  9.94 us (5%)
  starting transfers between devices  4.37 us (2%)
    all_gather x1, waiting for transfers between devices, on_device(): inputs = lax.all_gather(slot_input, 'grp', axis=0, tiled=True)  37.7 us
    all_gather x1, waiting for transfers between devices, on_device(): lax.all_gather(hidden, 'grp', axis=1, tiled=True)  28.4 us
    all_to_all x1, blocking collectives, on_device(): lax.all_to_all(total_x.reshape(n_z * n_grp, rows, -1), ('z', 'grp'), spli...  24.1 us
    all_to_all x1, blocking collectives, on_device(): lax.all_to_all(jnp.broadcast_to(sent[None], (n_z,) + sent.shape), 'z', sp...  21.4 us
    all_gather x1, blocking collectives, on_device(): packed = lax.all_gather(by_z, 'x', axis=0, tiled=True)  15.1 us
    all_to_all x1, blocking collectives, on_device(): lax.all_to_all(weighted.reshape(n_x, n_z * n_grp * rows, -1), 'x', split_...  14.2 us
    select_n x2, other arithmetic, side_by_side(): first = jnp.where(side == 0, own, other)  5.47 us
    dot_general x1, matrix products, on_device(): jnp.dot(inputs, gate_slab, preferred_element_type=f32)  4.98 us
  transfers between devices with their start and end apart: 4, of which 3 were waited for; matrix products, arithmetic and copies ran while one was open for 12% of the time, Pallas kernels for 0%

profile of v1, /device:TPU:8, one launch (start us, length us, event | category | flops | bytes accessed | tf_op | source)
XLA Modules:
  0.0 193.0 jit_solution(14789038502782183104)
XLA Ops:
  6.5 0.0 copy-start
  6.5 0.0 all-gather.3.cloned.1.call-start
  6.5 0.8 convert_element_type.71
  7.4 0.9 fusion.17
  8.3 0.8 fusion.18
  9.1 0.7 fusion.32
  9.9 0.1 broadcast_in_dim.14
  10.0 21.4 %all_to_all.15 = bf16[8,2,7296]{2,1,0:T(2,128)(2,1)S(1)} all-to-all(bf16[8,2,7296]{2,1,0:T(2,128)(2,1)S(1)} %broadcast_in_dim.14), channel_id=1, replica_groups=mesh['side'=2,'grp'=8,'x'=4,'z'=8] {'z'}, dimensions={0} | all-to-all | bytes 466944 | tf_op jit(solution)/shard_map/all_to_all | solution.py:47
  31.4 0.1 reshape.99
  31.5 15.1 %all_gather.9 = bf16[64,7296]{1,0:T(8,128)(2,1)S(1)} all-gather(bf16[16,7296]{1,0:T(8,128)(2,1)S(1)} %reshape.99), channel_id=1, replica_groups=mesh['side'=2,'grp'=8,'x'=4,'z'=8] {'x'}, dimensions={0}, use_global_device_ids=true | all-gather | bytes 1167360 | tf_op jit(solution)/shard_map/all_gather | solution.py:50
  46.6 0.1 copy.63
  46.7 0.1 convert_reduce_fusion.1
  46.8 1.1 convolution_convert_fusion
  47.9 0.0 all-gather.3.cloned.1.call-update
  47.9 0.0 all-gather.5.cloned.1.call-start
  47.9 0.0 copy-done
  47.9 1.9 collective-permute-start
  49.9 2.4 %collective-permute-start.1 = (bf16[2048,448]{0,1:T(8,128)(2,1)}, bf16[2048,448]{0,1:T(8,128)(2,1)}, u32[]{:S(2)}, u32[]{:S(2)}) collective-permute-start(bf16[2048,448]{0,1:T(8,128)(2,1)} %bitcast.2), channel_id=1, source_target_pairs={{0,256},{256,0},{1,257},{257,1},{2,258},{258,2},{3,259},{259,3},{4... | collective-permute-start | bytes 5505032 | tf_op jit(solution)/shard_map/ppermute | solution.py:18
  52.3 1.5 collective-permute-done
  53.8 3.6 %broadcast_select_fusion.1 = (bf16[7168,128]{1,0:T(8,128)(2,1)}, bf16[7168,128]{1,0:T(8,128)(2,1)}) fusion(bf16[7168,128]{1,0:T(8,128)(2,1)} %collective-permute-done, pred[]{:T(512)S(6)} %eq.56, bf16[1,7168,128]{2,1,0:T(8,128)(2,1)S(1)} %copy-done), kind=kLoop, calls=%fused_computation.14 | loop fusion | flops 1835008 | bytes 7340033 | tf_op jit(solution)/shard_map/jit(_where)/select_n | solution.py:19
  57.4 37.7 %all-gather.3.cloned.1.call-done = bf16[256,7296]{1,0:T(8,128)(2,1)} async-done(((bf16[32,7296]{1,0:T(8,128)(2,1)}), bf16[256,7296]{1,0:T(8,128)(2,1)}) %all-gather.3.cloned.1.call-update) | async-done | bytes 3735568 | tf_op jit(solution)/shard_map/all_gather | solution.py:58
  95.1 5.0 %multiply_convert_fusion = bf16[256,256]{1,0:T(8,128)(2,1)} fusion(bf16[256,7296]{1,0:T(8,128)(2,1)} %all-gather.3.cloned.1.call-done, bf16[7168,128]{1,0:T(8,128)(2,1)} %get-tuple-element.8, bf16[7168,128]{1,0:T(8,128)(2,1)} %get-tuple-element.7), kind=kOutput, calls=%fused_computation.19 | convolution fusion | flops 969703424 | bytes 7536640 | tf_op jit(solution)/shard_map/dot_general | solution.py:60
  100.0 0.0 all-gather.5.cloned.1.call-update
  100.1 2.8 %copy.51 = bf16[1,2048,448]{2,1,0:T(8,128)(2,1)S(1)} copy(bf16[1,2048,448]{1,2,0:T(8,128)(2,1)} %param.9) | data formatting | bytes 3670016 | tf_op args[4]
  102.9 0.0 collective-permute-done.1
  102.9 3.9 %copy.53 = bf16[2048,448]{1,0:T(8,128)(2,1)} copy(bf16[2048,448]{0,1:T(8,128)(2,1)} %collective-permute-done.1) | data formatting | bytes 3670016 | tf_op jit(solution)/shard_map/ppermute | solution.py:18
  106.8 1.9 bitcast_select_fusion
  108.6 1.2 pad_maximum_fusion
  109.9 2.2 %copy.55 = bf16[8,2,128,896]{3,2,1,0:T(8,128)(2,1)} copy(bf16[8,2,128,896]{3,2,0,1:T(8,128)(2,1)S(1)} %bitcast.21) | data formatting | bytes 7340032 | tf_op jit(solution)/shard_map/transpose | solution.py:38
  112.1 1.0 convert_reduce_fusion
  113.1 1.1 select_reduce_fusion
  114.3 28.4 %all-gather.5.cloned.1.call-done = bf16[256,2048]{1,0:T(8,128)(2,1)} async-done(((bf16[256,256]{1,0:T(8,128)(2,1)}), bf16[256,2048]{1,0:T(8,128)(2,1)}) %all-gather.5.cloned.1.call-update) | async-done | bytes 1048592 | tf_op jit(solution)/shard_map/all_gather | solution.py:62
  142.7 3.9 %convolution_convert_fusion.1 = bf16[512,896]{1,0:T(8,128)(2,1)S(1)} fusion(bf16[256,2048]{1,0:T(8,128)(2,1)} %all-gather.5.cloned.1.call-done, bf16[2048,896]{1,0:T(8,128)(2,1)} %bitcast.22, s32[256]{0:T(256)S(1)} %fusion.25, bf16[256]{0:T(256)(128)(2,1)S(1)} %select_reduce_fusion), kind=kOutput, calls=%fused_computation.15 | convolution fusion | flops 1175355392 | bytes 5637632 | tf_op jit(solution)/shard_map/dot_general | solution.py:79
  146.6 14.2 %all_to_all.16 = bf16[4,128,896]{2,1,0:T(8,128)(2,1)S(1)} all-to-all(bf16[4,128,896]{2,1,0:T(8,128)(2,1)S(1)} %bitcast.24), channel_id=1, replica_groups=mesh['side'=2,'grp'=8,'x'=4,'z'=8] {'x'}, dimensions={0} | all-to-all | bytes 1835008 | tf_op jit(solution)/shard_map/all_to_all | solution.py:80
  160.8 0.1 reduce_sum.54
  160.9 0.1 reshape.103
  161.0 24.1 %all_to_all.17 = bf16[64,2,896]{2,1,0:T(2,128)(2,1)S(1)} all-to-all(bf16[64,2,896]{2,1,0:T(2,128)(2,1)S(1)} %reshape.103), channel_id=1, replica_groups=mesh['side'=2,'grp'=8,'x'=4,'z'=8] {'z','grp'}, dimensions={0} | all-to-all | bytes 458752 | tf_op jit(solution)/shard_map/all_to_all | solution.py:84
  185.1 0.2 reduce_sum.55
  185.3 0.1 reshape.109
  185.5 0.7 reshape.106
  (7 shorter events, 0.1 us)
Async XLA Ops:
  6.5 41.4 %copy-start = (bf16[1,7168,128]{2,1,0:T(8,128)(2,1)S(1)}, bf16[1,7168,128]{2,1,0:T(8,128)(2,1)}, u32[]{:S(2)}) copy-start(bf16[1,7168,128]{2,1,0:T(8,128)(2,1)} %param.8) | copy-start | bytes 5505028
  6.5 88.5 %all-gather.3.cloned.1.call-start = ((), (), s32[]{:S(2)}) async-start(), calls=%async_computation.3 | async-start | bytes 4202496 | tf_op jit(solution)/shard_map/all_gather | solution.py:58
  47.9 94.8 %all-gather.5.cloned.1.call-start = ((), (), s32[]{:S(2)}) async-start(), calls=%async_computation.4 | async-start | bytes 1179648 | tf_op jit(solution)/shard_map/all_gather | solution.py:62
  47.9 5.8 %collective-permute-start = (bf16[7168,128]{1,0:T(8,128)(2,1)S(1)}, bf16[7168,128]{1,0:T(8,128)(2,1)}, u32[]{:S(2)}, u32[]{:S(2)}) collective-permute-start(bf16[7168,128]{1,0:T(8,128)(2,1)S(1)} %bitcast.23), channel_id=1, source_target_pairs={{0,256},{256,0},{1,257},{257,1},{2,258},{258,2},{3,259},{259,3},{4... | collective-permute-start | bytes 5505032 | tf_op jit(solution)/shard_map/ppermute | solution.py:18
  49.9 53.0 %collective-permute-start.1 = (bf16[2048,448]{0,1:T(8,128)(2,1)}, bf16[2048,448]{0,1:T(8,128)(2,1)}, u32[]{:S(2)}, u32[]{:S(2)}) collective-permute-start(bf16[2048,448]{0,1:T(8,128)(2,1)} %bitcast.2), channel_id=1, source_target_pairs={{0,256},{256,0},{1,257},{257,1},{2,258},{258,2},{3,259},{259,3},{4... | collective-permute-start | bytes 5505032 | tf_op jit(solution)/shard_map/ppermute | solution.py:18
Sparse Core Ops, SparseCore 0:
  48.0 46.9 all-gather.2
  100.2 42.4 all-gather.4

commit v2 on v1

v2 whole, which is shorter than its diff:
```python
import functools

import jax
import jax.numpy as jnp
from jax import lax
from jax.experimental import pallas as pl
from jax.experimental.pallas import tpu as pltpu
from jax.sharding import Mesh, PartitionSpec as P

CAP = 32
TOPK = 8
TAIL = 128
SHIFT = 64
SPOT = 32


def rms_rows(tokens):
    values = tokens.astype(jnp.float32)
    scale = lax.rsqrt(jnp.mean(values * values, axis=1, keepdims=True) + 1e-06)
    return (values * scale).astype(jnp.bfloat16)


def side_by_side(own, side, axis):
    other = lax.ppermute(own, "side", [(0, 1), (1, 0)])
    first = jnp.where(side == 0, own, other)
    second = jnp.where(side == 0, other, own)
    return jnp.concatenate([first, second], axis=axis)


def down_kernel(n_grp, n_side, unit, rows, near, where_ref, near_ref, far_ref, slab_ref, *refs):
    *tails, out_ref, hidden_ref, notes_ref = refs
    grp, dev = where_ref[0], where_ref[1]
    for g in range(n_grp):
        for j in range(n_grp):
            d = (j - g) % n_grp
            for k in range(n_side):
                units = slice(k * unit, (k + 1) * unit)
                if d in near:
                    start = near.index(d) * CAP
                    block = near_ref[g, start : start + CAP, units]
                else:
                    block = far_ref[g, :, units]
                at = (k * n_grp + g) * unit
                hidden_ref[j * CAP : (j + 1) * CAP, at : at + unit] = block
    for d in range(n_grp):
        j = lax.rem(grp + d, n_grp)
        notes_ref[pl.ds(pl.multiple_of(j * CAP, CAP), CAP), :] = tails[d][...]
    columns = lax.dot_general(
        hidden_ref[...], slab_ref[...], (((1,), (1,)), ((), ())), preferred_element_type=jnp.float32
    ).astype(jnp.bfloat16)
    slots, tokens = hidden_ref.shape[0], out_ref.shape[0]
    notes = notes_ref[...].astype(jnp.float32)
    lane = lax.broadcasted_iota(jnp.int32, notes.shape, 1)
    mine = (lane < TOPK) & (notes.astype(jnp.int32) == dev)
    weight = jnp.sum(jnp.where(mine, pltpu.roll(notes, SHIFT, 1), 0.0), axis=1, keepdims=True)
    place = jnp.sum(jnp.where(lane == SPOT, notes, 0.0), axis=1, keepdims=True).astype(jnp.int32)
    shift = rows.bit_length() - 1
    of_group = lax.broadcasted_iota(jnp.int32, (slots, 1), 0) // CAP
    target = (place >> shift) * (n_grp * rows) + of_group * rows + (place & (rows - 1))
    combine = jnp.where(
        lax.broadcasted_iota(jnp.int32, (slots, tokens), 1) == target, weight, 0.0
    ).astype(jnp.bfloat16)
    out_ref[...] = lax.dot_general(
        combine, columns, (((0,), (0,)), ((), ())), preferred_element_type=jnp.float32
    ).astype(jnp.bfloat16)


def on_device(tokens, expert_ids, route_weights, w_gate, w_down):
    bf16, f32, i32 = jnp.bfloat16, jnp.float32, jnp.int32
    rows, width = tokens.shape
    n_side, n_grp = lax.axis_size("side"), lax.axis_size("grp")
    n_x, n_z = lax.axis_size("x"), lax.axis_size("z")
    n_dev = n_x * n_z
    side = lax.axis_index("side")
    dev = lax.axis_index("x") * n_z + lax.axis_index("z")
    unit = w_gate.shape[2]

    gate_slab = jnp.pad(side_by_side(w_gate[0], side, 1), ((0, TAIL), (0, 0)))
    down_slab = side_by_side(w_down[0].T, side, 0)

    place = (dev * rows + jnp.arange(rows, dtype=i32)).astype(bf16)
    tail = jnp.concatenate(
        [
            jnp.pad(expert_ids.astype(bf16), ((0, 0), (0, SPOT - TOPK))),
            jnp.pad(place[:, None], ((0, 0), (0, SHIFT - SPOT - 1))),
            jnp.pad(route_weights, ((0, 0), (0, TAIL - SHIFT - TOPK))),
        ],
        axis=1,
    )
    sent = jnp.concatenate([rms_rows(tokens), tail], axis=1)
    by_z = lax.all_to_all(
        jnp.broadcast_to(sent[None], (n_z,) + sent.shape), "z", split_axis=0, concat_axis=0, tiled=True
    ).reshape(n_z * rows, -1)
    packed = lax.all_gather(by_z, "x", axis=0, tiled=True)

    group = n_dev * rows
    hit = jnp.any(packed[:, width : width + TOPK].astype(i32) == dev, axis=1)
    before = jnp.arange(group)[:, None] < jnp.arange(group)[None, :]
    slot = jnp.sum((before & hit[:, None]).astype(i32), axis=0)
    placed = (slot[None, :] == jnp.arange(CAP, dtype=i32)[:, None]) & hit[None, :]
    slot_input = jnp.dot(placed.astype(bf16), packed, preferred_element_type=f32).astype(bf16)

    def silu_gate(block):
        return jax.nn.silu(jnp.dot(block, gate_slab, preferred_element_type=f32)).astype(bf16)

    up = [(i, (i + 1) % n_grp) for i in range(n_grp)]
    down = [(i, (i - 1) % n_grp) for i in range(n_grp)]
    half = CAP // 2
    blocks = {0: slot_input}
    hidden = [silu_gate(slot_input)]
    near = [0]
    below = above = slot_input
    for step in range(1, n_grp // 2):
        below = lax.ppermute(below, "grp", up)
        above = lax.ppermute(above, "grp", down)
        blocks[n_grp - step], blocks[step] = below, above
        near += [n_grp - step, step]
        hidden.append(silu_gate(jnp.concatenate([below, above], axis=0)))
    last = [lax.ppermute(below[:half], "grp", up), lax.ppermute(above[half:], "grp", down)]
    got_near = lax.all_gather(jnp.concatenate(hidden, axis=0), "grp", axis=0, tiled=True)
    got_near, *last = lax.optimization_barrier((got_near, *last))
    far = n_grp // 2
    blocks[far] = jnp.concatenate(last, axis=0)
    hidden_far = silu_gate(blocks[far])
    got_far = lax.all_to_all(
        jnp.broadcast_to(hidden_far[None], (n_grp,) + hidden_far.shape),
        "grp",
        split_axis=0,
        concat_axis=0,
        tiled=True,
    )
    slots = n_grp * CAP
    weighted = pl.pallas_call(
        functools.partial(down_kernel, n_grp, n_side, unit, rows, near),
        out_shape=jax.ShapeDtypeStruct((n_grp * group, down_slab.shape[0]), bf16),
        in_specs=[pl.BlockSpec(memory_space=pltpu.SMEM)]
        + [pl.BlockSpec(memory_space=pltpu.VMEM)] * (3 + n_grp),
        out_specs=pl.BlockSpec(memory_space=pltpu.VMEM),
        scratch_shapes=[
            pltpu.VMEM((slots, down_slab.shape[1]), bf16),
            pltpu.VMEM((slots, TAIL), bf16),
        ],
        compiler_params=pltpu.CompilerParams(vmem_limit_bytes=40 * 2**20),
    )(
        jnp.stack([lax.axis_index("grp"), dev]).astype(i32),
        got_near.reshape(n_grp, len(near) * CAP, -1),
        got_far,
        down_slab,
        *[blocks[d][:, width:] for d in range(n_grp)],
    )
    parts = lax.all_to_all(
        weighted.reshape(n_dev * n_grp, rows, -1), ("x", "z", "grp"), split_axis=0, concat_axis=0, tiled=True
    )
    total = jnp.sum(parts.reshape(n_dev, n_grp, rows, -1).astype(f32), axis=0).astype(bf16)
    mixed = total.reshape(n_grp, rows, n_side, -1).transpose(1, 2, 0, 3)
    return mixed.reshape(rows, width)


def solution(mesh):
    side, grp, dev = mesh.devices.shape
    n_z = 8
    fine = Mesh(mesh.devices.reshape(side, grp, dev // n_z, n_z), ("side", "grp", "x", "z"))
    row_axes = ("side", "grp", "x", "z")
    in_specs = (
        P(row_axes, None),
        P(row_axes, None),
        P(row_axes, None),
        P(("x", "z"), None, ("side", "grp")),
        P(("x", "z"), None, ("side", "grp")),
    )
    return jax.shard_map(
        on_device, mesh=fine, in_specs=in_specs, out_specs=P(row_axes, None), check_vma=False
    )
```

time: 194 us -> 184 us (0.948)
  the two profiles are of different devices: /device:TPU:8 before, /device:TPU:16 now
where the time goes in v2:
time: 184 us; the launch traced here: 183 us
  blocking collectives  78.7 us (43%)
  starting transfers between devices  43.8 us (24%)
  waiting for transfers between devices  26.6 us (14%)
  other arithmetic  14 us (8%)
  local copies, waits for them, and re-layouts  10.2 us (6%)
  matrix products  7.6 us (4%)
  Pallas kernels  2.13 us (1%)
    all_to_all x1, blocking collectives, on_device(): lax.all_to_all(weighted.reshape(n_dev * n_grp, rows, -1), ('x', 'z', 'grp...  34 us
    all_gather x1, blocking collectives, on_device(): lax.all_gather(jnp.concatenate(hidden, axis=0), 'grp', axis=0, tiled=True)  29.7 us
    all_gather x1, blocking collectives, on_device(): packed = lax.all_gather(by_z, 'x', axis=0, tiled=True)  15.1 us
    ppermute x3, waiting for transfers between devices, on_device(): below = lax.ppermute(below, 'grp', up)  13.7 us
    all_to_all x1, starting transfers between devices, on_device(): lax.all_to_all(jnp.broadcast_to(sent[None], (n_z,) + sent.shape), 'z', sp...  10.3 us
    all_to_all x1, waiting for transfers between devices, on_device(): lax.all_to_all(jnp.broadcast_to(sent[None], (n_z,) + sent.shape), 'z', sp...  9.34 us
    ppermute x3, starting transfers between devices, on_device(): below = lax.ppermute(below, 'grp', up)  9.03 us
    ppermute x3, starting transfers between devices, on_device(): above = lax.ppermute(above, 'grp', down)  7.84 us
  transfers between devices with their start and end apart: 12, of which 6 were waited for; matrix products, arithmetic and copies ran while one was open for 12% of the time, Pallas kernels for 0%

profile of v2, /device:TPU:16, one launch (start us, length us, event | category | flops | bytes accessed | tf_op | source)
XLA Modules:
  0.0 183.3 jit_solution(14741557407942382951)
XLA Ops:
  0.0 1.1 fusion.21
  1.1 0.8 fusion.22
  1.9 0.7 convert_element_type.56
  2.6 0.7 pad.18
  3.4 0.8 broadcast_in_dim.4
  4.2 10.3 %all-to-all-start = ((bf16[8,2,7296]{2,1,0:T(2,128)(2,1)}), bf16[8,2,7296]{2,1,0:T(2,128)(2,1)S(1)}, u32[]{:S(2)}, u32[]{:S(2)}) async-start(bf16[8,2,7296]{2,1,0:T(2,128)(2,1)} %broadcast_in_dim.4), calls=%async_computation | async-start | bytes 466944 | tf_op jit(solution)/shard_map/all_to_all | solution.py:91
  14.5 1.9 %collective-permute-start = (bf16[7168,128]{1,0:T(8,128)(2,1)}, bf16[7168,128]{1,0:T(8,128)(2,1)}, u32[]{:S(2)}, u32[]{:S(2)}) collective-permute-start(bf16[7168,128]{1,0:T(8,128)(2,1)} %bitcast.26), channel_id=1, source_target_pairs={{0,256},{256,0},{1,257},{257,1},{2,258},{258,2},{3,259},{259,3},{4... | collective-permute-start | bytes 5505032 | tf_op jit(solution)/shard_map/ppermute | solution.py:24
  16.4 9.3 %all-to-all-done = bf16[8,2,7296]{2,1,0:T(2,128)(2,1)S(1)} async-done(((bf16[8,2,7296]{2,1,0:T(2,128)(2,1)}), bf16[8,2,7296]{2,1,0:T(2,128)(2,1)S(1)}, u32[]{:S(2)}, u32[]{:S(2)}) %all-to-all-start) | async-done | bytes 233504 | tf_op jit(solution)/shard_map/all_to_all | solution.py:91
  25.9 15.1 %all_gather.6 = bf16[64,7296]{1,0:T(8,128)(2,1)S(1)} all-gather(bf16[16,7296]{1,0:T(8,128)(2,1)S(1)} %reshape.41), channel_id=1, replica_groups=mesh['side'=2,'grp'=8,'x'=4,'z'=8] {'x'}, dimensions={0}, use_global_device_ids=true | all-gather | bytes 1167360 | tf_op jit(solution)/shard_map/all_gather | solution.py:94
  41.2 0.3 convolution_convert_fusion
  41.4 3.5 %collective-permute-start.1 = (bf16[32,7296]{1,0:T(8,128)(2,1)S(1)}, bf16[32,7296]{1,0:T(8,128)(2,1)}, u32[]{:S(2)}, u32[]{:S(2)}) collective-permute-start(bf16[32,7296]{1,0:T(8,128)(2,1)S(1)} %convolution_convert_fusion), channel_id=1, source_target_pairs={{0,32},{32,64},{64,96},{96,128},{128,160},{160,192},{192,224},{224... | collective-permute-start | bytes 1400840 | tf_op jit(solution)/shard_map/ppermute | solution.py:114
  44.9 2.4 %collective-permute-start.2 = (bf16[32,7296]{1,0:T(8,128)(2,1)S(1)}, bf16[32,7296]{1,0:T(8,128)(2,1)S(1)}, u32[]{:S(2)}, u32[]{:S(2)}) collective-permute-start(bf16[32,7296]{1,0:T(8,128)(2,1)S(1)} %convolution_convert_fusion), channel_id=1, source_target_pairs={{0,224},{32,0},{64,32},{96,64},{128,96},{160,128},{192,160},{224,1... | collective-permute-start | bytes 1400840 | tf_op jit(solution)/shard_map/ppermute | solution.py:115
  47.3 6.2 %collective-permute-done.1 = bf16[32,7296]{1,0:T(8,128)(2,1)} collective-permute-done((bf16[32,7296]{1,0:T(8,128)(2,1)S(1)}, bf16[32,7296]{1,0:T(8,128)(2,1)}, u32[]{:S(2)}, u32[]{:S(2)}) %collective-permute-start.1) | collective-permute-done | bytes 466976 | tf_op jit(solution)/shard_map/ppermute | solution.py:114
  53.5 3.0 %collective-permute-start.3 = (bf16[32,7296]{1,0:T(8,128)(2,1)}, bf16[32,7296]{1,0:T(8,128)(2,1)}, u32[]{:S(2)}, u32[]{:S(2)}) collective-permute-start(bf16[32,7296]{1,0:T(8,128)(2,1)} %collective-permute-done.1), channel_id=1, source_target_pairs={{0,32},{32,64},{64,96},{96,128},{128,160},{160,192},{192,224},{224... | collective-permute-start | bytes 1400840 | tf_op jit(solution)/shard_map/ppermute | solution.py:114
  56.5 0.2 collective-permute-done.2
  56.7 2.7 %collective-permute-start.4 = (bf16[32,7296]{1,0:T(8,128)(2,1)S(1)}, bf16[32,7296]{1,0:T(8,128)(2,1)}, u32[]{:S(2)}, u32[]{:S(2)}) collective-permute-start(bf16[32,7296]{1,0:T(8,128)(2,1)S(1)} %collective-permute-done.2), channel_id=1, source_target_pairs={{0,224},{32,0},{64,32},{96,64},{128,96},{160,128},{192,160},{224,1... | collective-permute-start | bytes 1400840 | tf_op jit(solution)/shard_map/ppermute | solution.py:115
  59.4 7.5 %collective-permute-done.3 = bf16[32,7296]{1,0:T(8,128)(2,1)} collective-permute-done((bf16[32,7296]{1,0:T(8,128)(2,1)}, bf16[32,7296]{1,0:T(8,128)(2,1)}, u32[]{:S(2)}, u32[]{:S(2)}) %collective-permute-start.3) | collective-permute-done | bytes 466976 | tf_op jit(solution)/shard_map/ppermute | solution.py:114
  66.9 2.6 %collective-permute-start.5 = (bf16[32,7296]{1,0:T(8,128)(2,1)}, bf16[32,7296]{1,0:T(8,128)(2,1)S(1)}, u32[]{:S(2)}, u32[]{:S(2)}) collective-permute-start(bf16[32,7296]{1,0:T(8,128)(2,1)} %collective-permute-done.3), channel_id=1, source_target_pairs={{0,32},{32,64},{64,96},{96,128},{128,160},{160,192},{192,224},{224... | collective-permute-start | bytes 1400840 | tf_op jit(solution)/shard_map/ppermute | solution.py:114
  69.5 0.5 collective-permute-done.4
  70.0 2.8 %collective-permute-start.6 = (bf16[32,7296]{1,0:T(8,128)(2,1)}, bf16[32,7296]{1,0:T(8,128)(2,1)}, u32[]{:S(2)}, u32[]{:S(2)}) collective-permute-start(bf16[32,7296]{1,0:T(8,128)(2,1)} %collective-permute-done.4), channel_id=1, source_target_pairs={{0,224},{32,0},{64,32},{96,64},{128,96},{160,128},{192,160},{224,1... | collective-permute-start | bytes 1400840 | tf_op jit(solution)/shard_map/ppermute | solution.py:115
  72.8 1.9 %collective-permute-start.9 = (bf16[448,2048]{1,0:T(8,128)(2,1)}, bf16[448,2048]{1,0:T(8,128)(2,1)}, u32[]{:S(2)}, u32[]{:S(2)}) collective-permute-start(bf16[448,2048]{1,0:T(8,128)(2,1)} %bitcast.27), channel_id=1, source_target_pairs={{0,256},{256,0},{1,257},{257,1},{2,258},{258,2},{3,259},{259,3},{4... | collective-permute-start | bytes 5505032 | tf_op jit(solution)/shard_map/ppermute | solution.py:24
  74.8 0.7 slice.48.refs_1_
  75.5 0.7 slice.54.refs_7_
  76.2 0.7 slice.49.refs_2_
  76.9 0.7 slice.53.refs_6_
  77.7 4.6 %collective-permute-start.7 = (bf16[16,7296]{1,0:T(8,128)(2,1)S(1)}, bf16[16,7296]{1,0:T(8,128)(2,1)S(1)}, u32[]{:S(2)}, u32[]{:S(2)}) collective-permute-start(bf16[16,7296]{1,0:T(8,128)(2,1)S(1)} %slice.45), channel_id=1, source_target_pairs={{0,32},{32,64},{64,96},{96,128},{128,160},{160,192},{192,224},{224... | collective-permute-start | bytes 700424 | tf_op jit(solution)/shard_map/ppermute | solution.py:119
  82.3 1.0 slice.46
  83.2 1.9 %collective-permute-start.8 = (bf16[16,7296]{1,0:T(8,128)(2,1)S(1)}, bf16[16,7296]{1,0:T(8,128)(2,1)S(1)}, u32[]{:S(2)}, u32[]{:S(2)}) collective-permute-start(bf16[16,7296]{1,0:T(8,128)(2,1)S(1)} %slice.46), channel_id=1, source_target_pairs={{0,224},{32,0},{64,32},{96,64},{128,96},{160,128},{192,160},{224,1... | collective-permute-start | bytes 700424 | tf_op jit(solution)/shard_map/ppermute | solution.py:119
  85.2 0.7 slice.50.refs_3_
  85.9 1.7 broadcast_select_fusion.3
  87.6 1.8 fusion.2
  89.5 1.9 %multiply_convert_fusion = bf16[64,256]{1,0:T(8,128)(2,1)S(1)} fusion(bf16[7296,256]{1,0:T(8,128)(2,1)S(1)} %fusion.2, bf16[32,7296]{1,0:T(8,128)(2,1)} %collective-permute-done.6, bf16[32,7296]{1,0:T(8,128)(2,1)S(1)} %collective-permute-done.5), kind=kOutput, calls=%fused_computation.25 | convolution fusion | flops 241025024 | bytes 4702208 | tf_op jit(solution)/shard_map/dot_general | solution.py:104
  91.3 1.9 %multiply_convert_fusion.1 = bf16[64,256]{1,0:T(8,128)(2,1)S(1)} fusion(bf16[7296,256]{1,0:T(8,128)(2,1)S(1)} %fusion.2, bf16[32,7296]{1,0:T(8,128)(2,1)} %collective-permute-done.4, bf16[32,7296]{1,0:T(8,128)(2,1)} %collective-permute-done.3), kind=kOutput, calls=%fused_computation.26 | convolution fusion | flops 241025024 | bytes 4702208 | tf_op jit(solution)/shard_map/dot_general | solution.py:104
  93.3 2.0 %multiply_convert_fusion.2 = bf16[64,256]{1,0:T(8,128)(2,1)S(1)} fusion(bf16[7296,256]{1,0:T(8,128)(2,1)S(1)} %fusion.2, bf16[32,7296]{1,0:T(8,128)(2,1)S(1)} %copy-done.4, bf16[32,7296]{1,0:T(8,128)(2,1)} %collective-permute-done.1), kind=kOutput, calls=%fused_computation.27 | convolution fusion | flops 241025024 | bytes 4702208 | tf_op jit(solution)/shard_map/dot_general | solution.py:104
  95.3 0.8 multiply_convert_fusion.4
  96.1 3.0 %broadcast_select_fusion.1 = (bf16[448,2048]{1,0:T(8,128)(2,1)S(1)}, bf16[448,2048]{1,0:T(8,128)(2,1)}) fusion(bf16[448,2048]{1,0:T(8,128)(2,1)} %collective-permute-done.9, pred[]{:T(512)S(6)} %eq.30, bf16[1,2048,448]{1,2,0:T(8,128)(2,1)S(1)} %copy-done.2), kind=kLoop, calls=%fused_computation.7 | loop fusion | flops 1835008 | bytes 7340033 | tf_op jit(solution)/shard_map/jit(_where)/select_n | solution.py:25
  99.1 29.7 %all_gather.7 = bf16[1792,256]{1,0:T(8,128)(2,1)S(1)} all-gather(bf16[224,256]{1,0:T(8,128)(2,1)S(1)} %pad_maximum_fusion.1), channel_id=1, replica_groups=mesh['side'=2,'grp'=8,'x'=4,'z'=8] {'grp'}, dimensions={0}, use_global_device_ids=true | all-gather | bytes 1032192 | tf_op jit(solution)/shard_map/all_gather | solution.py:120
  128.8 0.8 multiply_convert_fusion.3
  129.6 0.7 broadcast_in_dim.5
  130.3 6.3 %all-to-all-start.1 = ((bf16[8,32,256]{2,1,0:T(8,128)(2,1)}), bf16[8,32,256]{2,1,0:T(8,128)(2,1)S(1)}, u32[]{:S(2)}, u32[]{:S(2)}) async-start(bf16[8,32,256]{2,1,0:T(8,128)(2,1)} %broadcast_in_dim.5), calls=%async_computation.1 | async-start | bytes 262144 | tf_op jit(solution)/shard_map/all_to_all | solution.py:125
  136.6 3.8 %pad_maximum_fusion.slab_ref = bf16[896,2048]{1,0:T(8,128)(2,1)} fusion(bf16[448,2048]{1,0:T(8,128)(2,1)} %get-tuple-element.12, bf16[448,2048]{1,0:T(8,128)(2,1)S(1)} %get-tuple-element.11), kind=kLoop, calls=%fused_computation.5 | loop fusion | flops 7340032 | bytes 7340032 | tf_op jit(solution)/shard_map/concatenate | solution.py:27
  140.4 2.8 %all-to-all-done.1.far_ref = bf16[8,32,256]{2,1,0:T(8,128)(2,1)S(1)} async-done(((bf16[8,32,256]{2,1,0:T(8,128)(2,1)}), bf16[8,32,256]{2,1,0:T(8,128)(2,1)S(1)}, u32[]{:S(2)}, u32[]{:S(2)}) %all-to-all-start.1) | async-done | bytes 131104 | tf_op jit(solution)/shard_map/all_to_all | solution.py:125
  143.2 2.0 %copy-done = bf16[896,2048]{1,0:T(8,128)(2,1)S(1)} copy-done((bf16[896,2048]{1,0:T(8,128)(2,1)S(1)}, bf16[896,2048]{1,0:T(8,128)(2,1)}, u32[]{:S(2)}) %copy-start) | copy-done | bytes 3670040
  145.2 2.1 %shard_map.55 = bf16[512,896]{1,0:T(8,128)(2,1)S(1)} custom-call(s32[2]{0:T(128)S(1)} %pad_add_fusion.where_ref, bf16[8,224,256]{2,1,0:T(8,128)(2,1)S(1)} %bitcast.24, bf16[8,32,256]{2,1,0:T(8,128)(2,1)S(1)} %all-to-all-done.1.far_ref, bf16[896,2048]{1,0:T(8,128)(2,1)S(1)} %copy-done, bf16[32,128]{1,0:T(8,128)(2,1)S(1)} %slice.47.refs_0_, ...), custom_call_target="tpu_custom_call" | custom-call | tf_op jit(solution)/shard_map/pallas_call | solution.py:133
  147.3 0.3 reshape.43
  147.7 34.0 %all_to_all.15 = bf16[256,2,896]{2,1,0:T(2,128)(2,1)S(1)} all-to-all(bf16[256,2,896]{2,1,0:T(2,128)(2,1)S(1)} %reshape.43), channel_id=1, replica_groups=mesh['side'=2,'grp'=8,'x'=4,'z'=8] {'x','z','grp'}, dimensions={0} | all-to-all | bytes 1835008 | tf_op jit(solution)/shard_map/all_to_all | solution.py:151
  181.7 0.8 reduce_sum.32
  182.6 0.7 reshape.46
  (35 shorter events, 0.8 us)
Async XLA Ops:
  0.0 85.9 %copy-start.1 = (bf16[1,7168,128]{2,1,0:T(8,128)(2,1)S(1)}, bf16[1,7168,128]{2,1,0:T(8,128)(2,1)}, u32[]{:S(2)}) copy-start(bf16[1,7168,128]{2,1,0:T(8,128)(2,1)} %param.8) | copy-start | bytes 5505028
  4.2 21.6 %all-to-all-start = ((bf16[8,2,7296]{2,1,0:T(2,128)(2,1)}), bf16[8,2,7296]{2,1,0:T(2,128)(2,1)S(1)}, u32[]{:S(2)}, u32[]{:S(2)}) async-start(bf16[8,2,7296]{2,1,0:T(2,128)(2,1)} %broadcast_in_dim.4), calls=%async_computation | async-start | bytes 466944 | tf_op jit(solution)/shard_map/all_to_all | solution.py:91
  14.5 71.3 %collective-permute-start = (bf16[7168,128]{1,0:T(8,128)(2,1)}, bf16[7168,128]{1,0:T(8,128)(2,1)}, u32[]{:S(2)}, u32[]{:S(2)}) collective-permute-start(bf16[7168,128]{1,0:T(8,128)(2,1)} %bitcast.26), channel_id=1, source_target_pairs={{0,256},{256,0},{1,257},{257,1},{2,258},{258,2},{3,259},{259,3},{4... | collective-permute-start | bytes 5505032 | tf_op jit(solution)/shard_map/ppermute | solution.py:24
  41.4 12.1 %collective-permute-start.1 = (bf16[32,7296]{1,0:T(8,128)(2,1)S(1)}, bf16[32,7296]{1,0:T(8,128)(2,1)}, u32[]{:S(2)}, u32[]{:S(2)}) collective-permute-start(bf16[32,7296]{1,0:T(8,128)(2,1)S(1)} %convolution_convert_fusion), channel_id=1, source_target_pairs={{0,32},{32,64},{64,96},{96,128},{128,160},{160,192},{192,224},{224... | collective-permute-start | bytes 1400840 | tf_op jit(solution)/shard_map/ppermute | solution.py:114
  44.9 11.8 %collective-permute-start.2 = (bf16[32,7296]{1,0:T(8,128)(2,1)S(1)}, bf16[32,7296]{1,0:T(8,128)(2,1)S(1)}, u32[]{:S(2)}, u32[]{:S(2)}) collective-permute-start(bf16[32,7296]{1,0:T(8,128)(2,1)S(1)} %convolution_convert_fusion), channel_id=1, source_target_pairs={{0,224},{32,0},{64,32},{96,64},{128,96},{160,128},{192,160},{224,1... | collective-permute-start | bytes 1400840 | tf_op jit(solution)/shard_map/ppermute | solution.py:115
  53.5 13.4 %collective-permute-start.3 = (bf16[32,7296]{1,0:T(8,128)(2,1)}, bf16[32,7296]{1,0:T(8,128)(2,1)}, u32[]{:S(2)}, u32[]{:S(2)}) collective-permute-start(bf16[32,7296]{1,0:T(8,128)(2,1)} %collective-permute-done.1), channel_id=1, source_target_pairs={{0,32},{32,64},{64,96},{96,128},{128,160},{160,192},{192,224},{224... | collective-permute-start | bytes 1400840 | tf_op jit(solution)/shard_map/ppermute | solution.py:114
  56.7 2.7 %copy-start.3 = (bf16[32,7296]{1,0:T(8,128)(2,1)}, bf16[32,7296]{1,0:T(8,128)(2,1)S(1)}, u32[]{:S(2)}) copy-start(bf16[32,7296]{1,0:T(8,128)(2,1)S(1)} %collective-permute-done.2) | copy-start | bytes 1400836
  56.7 13.3 %collective-permute-start.4 = (bf16[32,7296]{1,0:T(8,128)(2,1)S(1)}, bf16[32,7296]{1,0:T(8,128)(2,1)}, u32[]{:S(2)}, u32[]{:S(2)}) collective-permute-start(bf16[32,7296]{1,0:T(8,128)(2,1)S(1)} %collective-permute-done.2), channel_id=1, source_target_pairs={{0,224},{32,0},{64,32},{96,64},{128,96},{160,128},{192,160},{224,1... | collective-permute-start | bytes 1400840 | tf_op jit(solution)/shard_map/ppermute | solution.py:115
  66.9 10.7 %collective-permute-start.5 = (bf16[32,7296]{1,0:T(8,128)(2,1)}, bf16[32,7296]{1,0:T(8,128)(2,1)S(1)}, u32[]{:S(2)}, u32[]{:S(2)}) collective-permute-start(bf16[32,7296]{1,0:T(8,128)(2,1)} %collective-permute-done.3), channel_id=1, source_target_pairs={{0,32},{32,64},{64,96},{96,128},{128,160},{160,192},{192,224},{224... | collective-permute-start | bytes 1400840 | tf_op jit(solution)/shard_map/ppermute | solution.py:114
  70.0 12.3 %collective-permute-start.6 = (bf16[32,7296]{1,0:T(8,128)(2,1)}, bf16[32,7296]{1,0:T(8,128)(2,1)}, u32[]{:S(2)}, u32[]{:S(2)}) collective-permute-start(bf16[32,7296]{1,0:T(8,128)(2,1)} %collective-permute-done.4), channel_id=1, source_target_pairs={{0,224},{32,0},{64,32},{96,64},{128,96},{160,128},{192,160},{224,1... | collective-permute-start | bytes 1400840 | tf_op jit(solution)/shard_map/ppermute | solution.py:115
  72.8 23.3 %collective-permute-start.9 = (bf16[448,2048]{1,0:T(8,128)(2,1)}, bf16[448,2048]{1,0:T(8,128)(2,1)}, u32[]{:S(2)}, u32[]{:S(2)}) collective-permute-start(bf16[448,2048]{1,0:T(8,128)(2,1)} %bitcast.27), channel_id=1, source_target_pairs={{0,256},{256,0},{1,257},{257,1},{2,258},{258,2},{3,259},{259,3},{4... | collective-permute-start | bytes 5505032 | tf_op jit(solution)/shard_map/ppermute | solution.py:24
  77.7 51.1 %collective-permute-start.7 = (bf16[16,7296]{1,0:T(8,128)(2,1)S(1)}, bf16[16,7296]{1,0:T(8,128)(2,1)S(1)}, u32[]{:S(2)}, u32[]{:S(2)}) collective-permute-start(bf16[16,7296]{1,0:T(8,128)(2,1)S(1)} %slice.45), channel_id=1, source_target_pairs={{0,32},{32,64},{64,96},{96,128},{128,160},{160,192},{192,224},{224... | collective-permute-start | bytes 700424 | tf_op jit(solution)/shard_map/ppermute | solution.py:119
  83.2 45.6 %collective-permute-start.8 = (bf16[16,7296]{1,0:T(8,128)(2,1)S(1)}, bf16[16,7296]{1,0:T(8,128)(2,1)S(1)}, u32[]{:S(2)}, u32[]{:S(2)}) collective-permute-start(bf16[16,7296]{1,0:T(8,128)(2,1)S(1)} %slice.46), channel_id=1, source_target_pairs={{0,224},{32,0},{64,32},{96,64},{128,96},{160,128},{192,160},{224,1... | collective-permute-start | bytes 700424 | tf_op jit(solution)/shard_map/ppermute | solution.py:119
  89.4 3.8 %copy-start.4 = (bf16[32,7296]{1,0:T(8,128)(2,1)S(1)}, bf16[32,7296]{1,0:T(8,128)(2,1)}, u32[]{:S(2)}) copy-start(bf16[32,7296]{1,0:T(8,128)(2,1)} %copy-done.3) | copy-start | bytes 1400836
  93.3 2.8 %copy-start.2 = (bf16[1,2048,448]{1,2,0:T(8,128)(2,1)S(1)}, bf16[1,2048,448]{1,2,0:T(8,128)(2,1)}, u32[]{:S(2)}) copy-start(bf16[1,2048,448]{1,2,0:T(8,128)(2,1)} %param.9) | copy-start | bytes 5505028
  130.3 12.9 %all-to-all-start.1 = ((bf16[8,32,256]{2,1,0:T(8,128)(2,1)}), bf16[8,32,256]{2,1,0:T(8,128)(2,1)S(1)}, u32[]{:S(2)}, u32[]{:S(2)}) async-start(bf16[8,32,256]{2,1,0:T(8,128)(2,1)} %broadcast_in_dim.5), calls=%async_computation.1 | async-start | bytes 262144 | tf_op jit(solution)/shard_map/all_to_all | solution.py:125
  143.2 2.0 %copy-start = (bf16[896,2048]{1,0:T(8,128)(2,1)S(1)}, bf16[896,2048]{1,0:T(8,128)(2,1)}, u32[]{:S(2)}) copy-start(bf16[896,2048]{1,0:T(8,128)(2,1)} %pad_maximum_fusion.slab_ref) | copy-start | bytes 11010052

commit v3 on v2

v3 whole, which is shorter than its diff:
```python
import functools

import jax
import jax.numpy as jnp
from jax import lax
from jax.experimental import pallas as pl
from jax.experimental.pallas import tpu as pltpu
from jax.sharding import Mesh, PartitionSpec as P

CAP = 32
TOPK = 8
TAIL = 128
SHIFT = 64
SPOT = 32


def send_kernel(rows, dev_ref, tokens_ref, ids_ref, weights_ref, out_ref):
    values = tokens_ref[...].astype(jnp.float32)
    width = values.shape[1]
    scale = lax.rsqrt(jnp.mean(values * values, axis=1, keepdims=True) + 1e-06)
    normed = (values * scale).astype(jnp.bfloat16)
    ids, weights = ids_ref[...].astype(jnp.float32), weights_ref[...].astype(jnp.float32)
    lane = lax.broadcasted_iota(jnp.int32, (rows, TAIL), 1)
    place = (dev_ref[0] * rows + lax.broadcasted_iota(jnp.int32, (rows, TAIL), 0)).astype(jnp.float32)
    tail = jnp.where(lane == SPOT, place, 0.0)
    for k in range(TOPK):
        tail = jnp.where(lane == k, ids[:, k : k + 1], tail)
        tail = jnp.where(lane == SHIFT + k, weights[:, k : k + 1], tail)
    tail = tail.astype(jnp.bfloat16)
    for z in range(out_ref.shape[0]):
        out_ref[z, :, :width] = normed
        out_ref[z, :, width:] = tail


def from_other_core(own):
    return lax.ppermute(own, "side", [(0, 1), (1, 0)])


def down_kernel(n_grp, n_side, unit, rows, order, where_ref, own_ref, other_ref, *refs):
    got, tails = refs[: len(order)], refs[len(order) : len(order) + n_grp]
    out_ref, hidden_ref, notes_ref, slab_ref, sems = refs[len(order) + n_grp :]
    grp, dev, side = where_ref[0], where_ref[1], where_ref[2]
    width = own_ref.shape[0]
    copies = [
        pltpu.make_async_copy(own_ref, slab_ref.at[pl.ds(pl.multiple_of(side * width, 64), width)], sems.at[0]),
        pltpu.make_async_copy(
            other_ref, slab_ref.at[pl.ds(pl.multiple_of((1 - side) * width, 64), width)], sems.at[1]
        ),
    ]
    for copy in copies:
        copy.start()
    for g in range(n_grp):
        for j in range(n_grp):
            d = (j - g) % n_grp
            for ref, distances in zip(got, order):
                if d in distances:
                    start = distances.index(d) * CAP
                    for k in range(n_side):
                        at = (k * n_grp + g) * unit
                        hidden_ref[j * CAP : (j + 1) * CAP, at : at + unit] = ref[
                            g, start : start + CAP, k * unit : (k + 1) * unit
                        ]
    for d in range(n_grp):
        j = lax.rem(grp + d, n_grp)
        notes_ref[pl.ds(pl.multiple_of(j * CAP, CAP), CAP), :] = tails[d][...]
    for copy in copies:
        copy.wait()
    columns = lax.dot_general(
        hidden_ref[...], slab_ref[...], (((1,), (1,)), ((), ())), preferred_element_type=jnp.float32
    ).astype(jnp.bfloat16)
    slots, tokens = hidden_ref.shape[0], out_ref.shape[0]
    notes = notes_ref[...].astype(jnp.float32)
    lane = lax.broadcasted_iota(jnp.int32, notes.shape, 1)
    mine = (lane < TOPK) & (notes.astype(jnp.int32) == dev)
    weight = jnp.sum(jnp.where(mine, pltpu.roll(notes, SHIFT, 1), 0.0), axis=1, keepdims=True)
    place = jnp.sum(jnp.where(lane == SPOT, notes, 0.0), axis=1, keepdims=True).astype(jnp.int32)
    shift = rows.bit_length() - 1
    of_group = lax.broadcasted_iota(jnp.int32, (slots, 1), 0) // CAP
    target = (place >> shift) * (n_grp * rows) + of_group * rows + (place & (rows - 1))
    combine = jnp.where(
        lax.broadcasted_iota(jnp.int32, (slots, tokens), 1) == target, weight, 0.0
    ).astype(jnp.bfloat16)
    out_ref[...] = lax.dot_general(
        combine, columns, (((0,), (0,)), ((), ())), preferred_element_type=jnp.float32
    ).astype(jnp.bfloat16)


def on_device(tokens, expert_ids, route_weights, w_gate, w_down):
    bf16, f32, i32 = jnp.bfloat16, jnp.float32, jnp.int32
    rows, width = tokens.shape
    n_side, n_grp = lax.axis_size("side"), lax.axis_size("grp")
    n_x, n_z = lax.axis_size("x"), lax.axis_size("z")
    n_dev = n_x * n_z
    side = lax.axis_index("side")
    dev = lax.axis_index("x") * n_z + lax.axis_index("z")
    unit = w_gate.shape[2]

    own_gate, own_down = w_gate[0], w_down[0].T
    other_gate, other_down = from_other_core(own_gate), from_other_core(own_down)

    vmem, smem = pl.BlockSpec(memory_space=pltpu.VMEM), pl.BlockSpec(memory_space=pltpu.SMEM)
    copies = pl.pallas_call(
        functools.partial(send_kernel, rows),
        out_shape=jax.ShapeDtypeStruct((n_z, rows, width + TAIL), bf16),
        in_specs=[smem, vmem, vmem, vmem],
        out_specs=vmem,
    )(dev.reshape(1).astype(i32), tokens, expert_ids, route_weights)
    by_z = lax.all_to_all(copies, "z", split_axis=0, concat_axis=0, tiled=True).reshape(n_z * rows, -1)
    packed = lax.all_gather(by_z, "x", axis=0, tiled=True)

    group = n_dev * rows
    hit = jnp.any(packed[:, width : width + TOPK].astype(i32) == dev, axis=1)
    before = jnp.arange(group)[:, None] < jnp.arange(group)[None, :]
    slot = jnp.sum((before & hit[:, None]).astype(i32), axis=0)
    placed = (slot[None, :] == jnp.arange(CAP, dtype=i32)[:, None]) & hit[None, :]
    slot_input = jnp.dot(placed.astype(bf16), packed, preferred_element_type=f32).astype(bf16)

    gate_slab = jnp.pad(
        jnp.concatenate(
            [jnp.where(side == 0, own_gate, other_gate), jnp.where(side == 0, other_gate, own_gate)], axis=1
        ),
        ((0, TAIL), (0, 0)),
    )

    def silu_gate(block):
        return jax.nn.silu(jnp.dot(block, gate_slab, preferred_element_type=f32)).astype(bf16)

    def to_all(hidden):
        return lax.all_to_all(
            jnp.broadcast_to(hidden[None], (n_grp,) + hidden.shape), "grp", split_axis=0, concat_axis=0, tiled=True
        )

    up = [(i, (i + 1) % n_grp) for i in range(n_grp)]
    down = [(i, (i - 1) % n_grp) for i in range(n_grp)]
    half, far = CAP // 2, n_grp // 2
    blocks = {0: slot_input}
    below = above = held = slot_input
    hidden, order = [[], []], [[], []]
    distances = [0]
    got_early = None
    for step in range(1, far + 1):
        if step < far:
            below = lax.ppermute(below, "grp", up)
            above = lax.ppermute(above, "grp", down)
        else:
            below, above = lax.ppermute(below[:half], "grp", up), lax.ppermute(above[half:], "grp", down)
        part = 0 if step <= far - 1 else 1
        hidden[part].append(silu_gate(held))
        order[part] += distances
        below, above, hidden[part][-1] = lax.optimization_barrier((below, above, hidden[part][-1]))
        if step == far - 1:
            got_early = to_all(jnp.concatenate(hidden[0], axis=0))
        held = jnp.concatenate([below, above], axis=0)
        distances = [far] if step == far else [n_grp - step, step]
        if step < far:
            blocks[n_grp - step], blocks[step] = below, above
    blocks[far] = held
    hidden[1].append(silu_gate(held))
    order[1] += distances
    got_late = to_all(jnp.concatenate(hidden[1], axis=0))

    slots = n_grp * CAP
    columns = n_side * own_down.shape[0]
    any_memory = pl.BlockSpec(memory_space=pl.ANY)
    weighted = pl.pallas_call(
        functools.partial(down_kernel, n_grp, n_side, unit, rows, order),
        out_shape=jax.ShapeDtypeStruct((n_grp * group, columns), bf16),
        in_specs=[smem, any_memory, any_memory] + [vmem] * (len(order) + n_grp),
        out_specs=vmem,
        scratch_shapes=[
            pltpu.VMEM((slots, own_down.shape[1]), bf16),
            pltpu.VMEM((slots, TAIL), bf16),
            pltpu.VMEM((columns, own_down.shape[1]), bf16),
            pltpu.SemaphoreType.DMA((2,)),
        ],
        compiler_params=pltpu.CompilerParams(vmem_limit_bytes=40 * 2**20),
    )(
        jnp.stack([lax.axis_index("grp"), dev, side]).astype(i32),
        own_down,
        other_down,
        got_early,
        got_late,
        *[blocks[d][:, width:] for d in range(n_grp)],
    )
    parts = lax.all_to_all(
        weighted.reshape(n_dev * n_grp, rows, -1), ("x", "z", "grp"), split_axis=0, concat_axis=0, tiled=True
    )
    total = jnp.sum(parts.reshape(n_dev, n_grp, rows, -1).astype(f32), axis=0).astype(bf16)
    mixed = total.reshape(n_grp, rows, n_side, -1).transpose(1, 2, 0, 3)
    return mixed.reshape(rows, width)


def solution(mesh):
    side, grp, dev = mesh.devices.shape
    n_z = 8
    fine = Mesh(mesh.devices.reshape(side, grp, dev // n_z, n_z), ("side", "grp", "x", "z"))
    row_axes = ("side", "grp", "x", "z")
    in_specs = (
        P(row_axes, None),
        P(row_axes, None),
        P(row_axes, None),
        P(("x", "z"), None, ("side", "grp")),
        P(("x", "z"), None, ("side", "grp")),
    )
    return jax.shard_map(
        on_device, mesh=fine, in_specs=in_specs, out_specs=P(row_axes, None), check_vma=False
    )
```

time: 184 us -> 177 us (0.962)
  blocking collectives: 78.7 us -> 48.4 us
  waiting for transfers between devices: 26.6 us -> 54 us
  other arithmetic: 14 us -> 4.68 us
  starting transfers between devices: 43.8 us -> 49.7 us
  matrix products: 7.6 us -> 4.24 us
  Pallas kernels: 2.13 us -> 5.44 us
    all_gather x1 -> x0, blocking collectives: 29.7 us -> none  [on_device(): lax.all_gather(jnp.concatenate(hidden, axis=0), 'grp', axis=0, tiled=True)]
    all_to_all x2 -> x3, waiting for transfers between devices: 12.1 us -> 26.4 us  [the longest x2 14.5 us: to_all(): lax.all_to_all(jnp.broadcast_to(hidden[None], (n_grp,) + hidden.shape), '...]
    ppermute x3, waiting for transfers between devices: 0.72 us -> 11.8 us  [on_device(): above = lax.ppermute(above, 'grp', down)]
    all_to_all x2 -> x3, starting transfers between devices: 16.6 us -> 21.5 us  [the longest x2 11.1 us: to_all(): lax.all_to_all(jnp.broadcast_to(hidden[None], (n_grp,) + hidden.shape), '...]
    concatenate x3, other arithmetic: 5.6 us -> 1.83 us  [the longest x1 1.82 us: on_device(): jnp.concatenate([jnp.where(side == 0, own_gate, other_gate), jnp.where(si...]
    ppermute x1, waiting for transfers between devices: 0.01 us -> 3.44 us  [on_device(): lax.ppermute(above[half:], 'grp', down)]
    dot_general x5, matrix products: 7.32 us -> 3.96 us  [silu_gate(): jnp.dot(block, gate_slab, preferred_element_type=f32)]
    select_n x2 -> x1, other arithmetic: 4.77 us -> 1.75 us  [on_device(): jnp.where(side == 0, own_gate, other_gate)]
  transfers between devices with their start and end apart: 12 -> 13, of which waited for: 6 -> 11; matrix products, arithmetic and copies ran while one was open for 12% -> 8% of each run, Pallas kernels for 0% -> 1%
where the time goes in v3:
time: 177 us; the launch traced here: 176 us
  waiting for transfers between devices  54 us (31%)
  starting transfers between devices  49.7 us (28%)
  blocking collectives  48.4 us (27%)
  local copies, waits for them, and re-layouts  8.99 us (5%)
  Pallas kernels  5.44 us (3%)
  other arithmetic  4.68 us (3%)
  matrix products  4.24 us (2%)
    all_to_all x1, blocking collectives, on_device(): lax.all_to_all(weighted.reshape(n_dev * n_grp, rows, -1), ('x', 'z', 'grp...  34.2 us
    all_to_all x2, waiting for transfers between devices, to_all(): lax.all_to_all(jnp.broadcast_to(hidden[None], (n_grp,) + hidden.shape), '...  14.5 us
    all_gather x1, blocking collectives, on_device(): packed = lax.all_gather(by_z, 'x', axis=0, tiled=True)  14.3 us
    all_to_all x1, waiting for transfers between devices, on_device(): lax.all_to_all(copies, 'z', split_axis=0, concat_axis=0, tiled=True)  11.9 us
    ppermute x3, waiting for transfers between devices, on_device(): above = lax.ppermute(above, 'grp', down)  11.8 us
    ppermute x3, starting transfers between devices, on_device(): below = lax.ppermute(below, 'grp', up)  11.7 us
    all_to_all x2, starting transfers between devices, to_all(): lax.all_to_all(jnp.broadcast_to(hidden[None], (n_grp,) + hidden.shape), '...  11.1 us
    ppermute x3, waiting for transfers between devices, on_device(): below = lax.ppermute(below, 'grp', up)  11.1 us
  transfers between devices with their start and end apart: 13, of which 11 were waited for; matrix products, arithmetic and copies ran while one was open for 8% of the time, Pallas kernels for 1%

profile of v3, /device:TPU:16, one launch (start us, length us, event | category | flops | bytes accessed | tf_op | source)
XLA Modules:
  0.0 175.8 jit_solution(10764275697319690301)
XLA Ops:
  0.0 2.0 %collective-permute-start.3 = (bf16[7168,128]{1,0:T(8,128)(2,1)}, bf16[7168,128]{1,0:T(8,128)(2,1)}, u32[]{:S(2)}, u32[]{:S(2)}) collective-permute-start(bf16[7168,128]{1,0:T(8,128)(2,1)} %bitcast.25), channel_id=1, source_target_pairs={{0,256},{256,0},{1,257},{257,1},{2,258},{258,2},{3,259},{259,3},{4... | collective-permute-start | bytes 5505032 | tf_op jit(solution)/shard_map/ppermute | solution.py:36
  2.1 1.6 shard_map.55
  3.7 10.3 %all-to-all-start = ((bf16[8,2,7296]{2,1,0:T(2,128)(2,1)}), bf16[8,2,7296]{2,1,0:T(2,128)(2,1)S(1)}, u32[]{:S(2)}, u32[]{:S(2)}) async-start(bf16[8,2,7296]{2,1,0:T(2,128)(2,1)} %shard_map.55), calls=%async_computation | async-start | bytes 466944 | tf_op jit(solution)/shard_map/all_to_all | solution.py:108
  14.0 11.9 %all-to-all-done = bf16[8,2,7296]{2,1,0:T(2,128)(2,1)S(1)} async-done(((bf16[8,2,7296]{2,1,0:T(2,128)(2,1)}), bf16[8,2,7296]{2,1,0:T(2,128)(2,1)S(1)}, u32[]{:S(2)}, u32[]{:S(2)}) %all-to-all-start) | async-done | bytes 233504 | tf_op jit(solution)/shard_map/all_to_all | solution.py:108
  26.0 14.3 %all_gather.3 = bf16[64,7296]{1,0:T(8,128)(2,1)S(1)} all-gather(bf16[16,7296]{1,0:T(8,128)(2,1)S(1)} %reshape.21), channel_id=1, replica_groups=mesh['side'=2,'grp'=8,'x'=4,'z'=8] {'x'}, dimensions={0}, use_global_device_ids=true | all-gather | bytes 1167360 | tf_op jit(solution)/shard_map/all_gather | solution.py:109
  40.8 3.5 %collective-permute-start.1 = (bf16[32,7296]{1,0:T(8,128)(2,1)S(1)}, bf16[32,7296]{1,0:T(8,128)(2,1)S(1)}, u32[]{:S(2)}, u32[]{:S(2)}) collective-permute-start(bf16[32,7296]{1,0:T(8,128)(2,1)S(1)} %convolution_convert_fusion), channel_id=1, source_target_pairs={{0,32},{32,64},{64,96},{96,128},{128,160},{160,192},{192,224},{224... | collective-permute-start | bytes 1400840 | tf_op jit(solution)/shard_map/ppermute | solution.py:143
  44.3 2.4 %collective-permute-start.2 = (bf16[32,7296]{1,0:T(8,128)(2,1)S(1)}, bf16[32,7296]{1,0:T(8,128)(2,1)S(1)}, u32[]{:S(2)}, u32[]{:S(2)}) collective-permute-start(bf16[32,7296]{1,0:T(8,128)(2,1)S(1)} %convolution_convert_fusion), channel_id=1, source_target_pairs={{0,224},{32,0},{64,32},{96,64},{128,96},{160,128},{192,160},{224,1... | collective-permute-start | bytes 1400840 | tf_op jit(solution)/shard_map/ppermute | solution.py:144
  46.7 1.7 broadcast_select_fusion.1
  48.4 1.8 %fusion.2 = bf16[7296,256]{1,0:T(8,128)(2,1)S(1)} fusion(bf16[7168,128]{1,0:T(8,128)(2,1)S(1)} %get-tuple-element.30, bf16[7168,128]{1,0:T(8,128)(2,1)S(1)} %get-tuple-element.29), kind=kLoop, calls=%fused_computation.4 | loop fusion | flops 13074432 | bytes 7405568 | tf_op jit(solution)/shard_map/concatenate | solution.py:119
  50.3 0.8 multiply_convert_fusion.4
  51.1 2.7 %collective-permute-done.1 = bf16[32,7296]{1,0:T(8,128)(2,1)S(1)} collective-permute-done((bf16[32,7296]{1,0:T(8,128)(2,1)S(1)}, bf16[32,7296]{1,0:T(8,128)(2,1)S(1)}, u32[]{:S(2)}, u32[]{:S(2)}) %collective-permute-start.1) | collective-permute-done | bytes 466976 | tf_op jit(solution)/shard_map/ppermute | solution.py:143
  53.7 4.3 %collective-permute-done.2 = bf16[32,7296]{1,0:T(8,128)(2,1)S(1)} collective-permute-done((bf16[32,7296]{1,0:T(8,128)(2,1)S(1)}, bf16[32,7296]{1,0:T(8,128)(2,1)S(1)}, u32[]{:S(2)}, u32[]{:S(2)}) %collective-permute-start.2) | collective-permute-done | bytes 466976 | tf_op jit(solution)/shard_map/ppermute | solution.py:144
  58.0 4.8 %collective-permute-start.4 = (bf16[32,7296]{1,0:T(8,128)(2,1)S(1)}, bf16[32,7296]{1,0:T(8,128)(2,1)S(1)}, u32[]{:S(2)}, u32[]{:S(2)}) collective-permute-start(bf16[32,7296]{1,0:T(8,128)(2,1)S(1)} %collective-permute-done.1), channel_id=1, source_target_pairs={{0,32},{32,64},{64,96},{96,128},{128,160},{160,192},{192,224},{224... | collective-permute-start | bytes 1400840 | tf_op jit(solution)/shard_map/ppermute | solution.py:143
  62.8 1.9 %collective-permute-start.5 = (bf16[32,7296]{1,0:T(8,128)(2,1)S(1)}, bf16[32,7296]{1,0:T(8,128)(2,1)S(1)}, u32[]{:S(2)}, u32[]{:S(2)}) collective-permute-start(bf16[32,7296]{1,0:T(8,128)(2,1)S(1)} %collective-permute-done.2), channel_id=1, source_target_pairs={{0,224},{32,0},{64,32},{96,64},{128,96},{160,128},{192,160},{224,1... | collective-permute-start | bytes 1400840 | tf_op jit(solution)/shard_map/ppermute | solution.py:144
  64.8 0.8 multiply_convert_fusion.2
  65.6 4.6 %collective-permute-done.4 = bf16[32,7296]{1,0:T(8,128)(2,1)S(1)} collective-permute-done((bf16[32,7296]{1,0:T(8,128)(2,1)S(1)}, bf16[32,7296]{1,0:T(8,128)(2,1)S(1)}, u32[]{:S(2)}, u32[]{:S(2)}) %collective-permute-start.4) | collective-permute-done | bytes 466976 | tf_op jit(solution)/shard_map/ppermute | solution.py:143
  70.2 4.1 %collective-permute-done.5 = bf16[32,7296]{1,0:T(8,128)(2,1)S(1)} collective-permute-done((bf16[32,7296]{1,0:T(8,128)(2,1)S(1)}, bf16[32,7296]{1,0:T(8,128)(2,1)S(1)}, u32[]{:S(2)}, u32[]{:S(2)}) %collective-permute-start.5) | collective-permute-done | bytes 466976 | tf_op jit(solution)/shard_map/ppermute | solution.py:144
  74.3 3.4 %collective-permute-start.6 = (bf16[32,7296]{1,0:T(8,128)(2,1)S(1)}, bf16[32,7296]{1,0:T(8,128)(2,1)S(1)}, u32[]{:S(2)}, u32[]{:S(2)}) collective-permute-start(bf16[32,7296]{1,0:T(8,128)(2,1)S(1)} %collective-permute-done.4), channel_id=1, source_target_pairs={{0,32},{32,64},{64,96},{96,128},{128,160},{160,192},{192,224},{224... | collective-permute-start | bytes 1400840 | tf_op jit(solution)/shard_map/ppermute | solution.py:143
  77.7 2.4 %collective-permute-start.7 = (bf16[32,7296]{1,0:T(8,128)(2,1)S(1)}, bf16[32,7296]{1,0:T(8,128)(2,1)S(1)}, u32[]{:S(2)}, u32[]{:S(2)}) collective-permute-start(bf16[32,7296]{1,0:T(8,128)(2,1)S(1)} %collective-permute-done.5), channel_id=1, source_target_pairs={{0,224},{32,0},{64,32},{96,64},{128,96},{160,128},{192,160},{224,1... | collective-permute-start | bytes 1400840 | tf_op jit(solution)/shard_map/ppermute | solution.py:144
  80.1 0.8 multiply_convert_fusion.1
  81.0 3.8 %collective-permute-done.6 = bf16[32,7296]{1,0:T(8,128)(2,1)S(1)} collective-permute-done((bf16[32,7296]{1,0:T(8,128)(2,1)S(1)}, bf16[32,7296]{1,0:T(8,128)(2,1)S(1)}, u32[]{:S(2)}, u32[]{:S(2)}) %collective-permute-start.6) | collective-permute-done | bytes 466976 | tf_op jit(solution)/shard_map/ppermute | solution.py:143
  84.8 3.4 %collective-permute-done.7 = bf16[32,7296]{1,0:T(8,128)(2,1)S(1)} collective-permute-done((bf16[32,7296]{1,0:T(8,128)(2,1)S(1)}, bf16[32,7296]{1,0:T(8,128)(2,1)S(1)}, u32[]{:S(2)}, u32[]{:S(2)}) %collective-permute-start.7) | collective-permute-done | bytes 466976 | tf_op jit(solution)/shard_map/ppermute | solution.py:144
  88.2 3.4 %collective-permute-start.8 = (bf16[16,7296]{1,0:T(8,128)(2,1)S(1)}, bf16[16,7296]{1,0:T(8,128)(2,1)S(1)}, u32[]{:S(2)}, u32[]{:S(2)}) collective-permute-start(bf16[16,7296]{1,0:T(8,128)(2,1)S(1)} %slice.34), channel_id=1, source_target_pairs={{0,32},{32,64},{64,96},{96,128},{128,160},{160,192},{192,224},{224... | collective-permute-start | bytes 700424 | tf_op jit(solution)/shard_map/ppermute | solution.py:146
  91.7 2.4 %collective-permute-start.9 = (bf16[16,7296]{1,0:T(8,128)(2,1)S(1)}, bf16[16,7296]{1,0:T(8,128)(2,1)S(1)}, u32[]{:S(2)}, u32[]{:S(2)}) collective-permute-start(bf16[16,7296]{1,0:T(8,128)(2,1)S(1)} %slice.35), channel_id=1, source_target_pairs={{0,224},{32,0},{64,32},{96,64},{128,96},{160,128},{192,160},{224,1... | collective-permute-start | bytes 700424 | tf_op jit(solution)/shard_map/ppermute | solution.py:146
  94.1 0.8 multiply_convert_fusion
  94.9 1.2 collective-permute-done.8
  96.2 3.4 %collective-permute-done.9 = bf16[16,7296]{1,0:T(8,128)(2,1)S(1)} collective-permute-done((bf16[16,7296]{1,0:T(8,128)(2,1)S(1)}, bf16[16,7296]{1,0:T(8,128)(2,1)S(1)}, u32[]{:S(2)}, u32[]{:S(2)}) %collective-permute-start.9) | collective-permute-done | bytes 233504 | tf_op jit(solution)/shard_map/ppermute | solution.py:146
  99.7 0.8 multiply_convert_fusion.3
  100.5 0.8 broadcast_in_dim.5
  101.3 4.9 %all-to-all-start.2 = ((bf16[8,96,256]{2,1,0:T(8,128)(2,1)}), bf16[8,96,256]{2,1,0:T(8,128)(2,1)S(1)}, u32[]{:S(2)}, u32[]{:S(2)}) async-start(bf16[8,96,256]{2,1,0:T(8,128)(2,1)} %broadcast_in_dim.5), calls=%async_computation.2 | async-start | bytes 786432 | tf_op jit(solution)/shard_map/all_to_all | solution.py:129
  106.1 1.9 %collective-permute-start = (bf16[448,2048]{1,0:T(8,128)(2,1)S(1)}, bf16[448,2048]{1,0:T(8,128)(2,1)}, u32[]{:S(2)}, u32[]{:S(2)}) collective-permute-start(bf16[448,2048]{1,0:T(8,128)(2,1)S(1)} %bitcast.22), channel_id=1, source_target_pairs={{0,256},{256,0},{1,257},{257,1},{2,258},{258,2},{3,259},{259,3},{4... | collective-permute-start | bytes 5505032 | tf_op jit(solution)/shard_map/ppermute | solution.py:36
  108.1 7.1 %all-to-all-done.2.refs_1_ = bf16[8,96,256]{2,1,0:T(8,128)(2,1)S(1)} async-done(((bf16[8,96,256]{2,1,0:T(8,128)(2,1)}), bf16[8,96,256]{2,1,0:T(8,128)(2,1)S(1)}, u32[]{:S(2)}, u32[]{:S(2)}) %all-to-all-start.2) | async-done | bytes 393248 | tf_op jit(solution)/shard_map/all_to_all | solution.py:129
  115.2 1.0 broadcast_in_dim.4
  116.1 6.3 %all-to-all-start.1 = ((bf16[8,160,256]{2,1,0:T(8,128)(2,1)}), bf16[8,160,256]{2,1,0:T(8,128)(2,1)S(1)}, u32[]{:S(2)}, u32[]{:S(2)}) async-start(bf16[8,160,256]{2,1,0:T(8,128)(2,1)} %broadcast_in_dim.4), calls=%async_computation.1 | async-start | bytes 1310720 | tf_op jit(solution)/shard_map/all_to_all | solution.py:129
  122.5 0.7 slice.37.refs_3_
  123.2 0.7 slice.43.refs_9_
  123.9 0.7 slice.38.refs_4_
  124.6 0.7 slice.42.refs_8_
  125.3 0.7 slice.39.refs_5_
  126.0 0.7 slice.41.refs_7_
  126.7 0.7 slice.46.refs_6_
  127.4 7.4 %all-to-all-done.1.refs_0_ = bf16[8,160,256]{2,1,0:T(8,128)(2,1)S(1)} async-done(((bf16[8,160,256]{2,1,0:T(8,128)(2,1)}), bf16[8,160,256]{2,1,0:T(8,128)(2,1)S(1)}, u32[]{:S(2)}, u32[]{:S(2)}) %all-to-all-start.1) | async-done | bytes 655392 | tf_op jit(solution)/shard_map/all_to_all | solution.py:129
  134.8 1.0 copy-done.2
  135.8 3.8 %shard_map.56 = bf16[512,896]{1,0:T(8,128)(2,1)S(1)} custom-call(s32[3]{0:T(128)S(1)} %pad_add_fusion.where_ref, bf16[448,2048]{1,0:T(8,128)(2,1)S(1)} %bitcast.23, bf16[448,2048]{1,0:T(8,128)(2,1)} %collective-permute-done.other_ref, bf16[8,160,256]{2,1,0:T(8,128)(2,1)S(1)} %all-to-all-done.1.refs_0_, bf16[8,96,256]{2,1,0:T(8,128)(2,1)S(1)} %copy-done.2, ...), custom_call_target="tpu_custom_call" | custom-call | tf_op jit(solution)/shard_map/pallas_call | solution.py:165
  139.6 0.3 reshape.22
  139.9 34.2 %all_to_all.20 = bf16[256,2,896]{2,1,0:T(2,128)(2,1)S(1)} all-to-all(bf16[256,2,896]{2,1,0:T(2,128)(2,1)S(1)} %reshape.22), channel_id=1, replica_groups=mesh['side'=2,'grp'=8,'x'=4,'z'=8] {'x','z','grp'}, dimensions={0} | all-to-all | bytes 1835008 | tf_op jit(solution)/shard_map/all_to_all | solution.py:185
  174.1 0.8 reduce_sum.22
  175.0 0.7 reshape.25
  (37 shorter events, 0.9 us)
Async XLA Ops:
  0.0 46.7 %copy-start.3 = (bf16[1,7168,128]{2,1,0:T(8,128)(2,1)S(1)}, bf16[1,7168,128]{2,1,0:T(8,128)(2,1)}, u32[]{:S(2)}) copy-start(bf16[1,7168,128]{2,1,0:T(8,128)(2,1)} %param.8) | copy-start | bytes 5505028
  0.0 46.7 %collective-permute-start.3 = (bf16[7168,128]{1,0:T(8,128)(2,1)}, bf16[7168,128]{1,0:T(8,128)(2,1)}, u32[]{:S(2)}, u32[]{:S(2)}) collective-permute-start(bf16[7168,128]{1,0:T(8,128)(2,1)} %bitcast.25), channel_id=1, source_target_pairs={{0,256},{256,0},{1,257},{257,1},{2,258},{258,2},{3,259},{259,3},{4... | collective-permute-start | bytes 5505032 | tf_op jit(solution)/shard_map/ppermute | solution.py:36
  3.7 22.2 %all-to-all-start = ((bf16[8,2,7296]{2,1,0:T(2,128)(2,1)}), bf16[8,2,7296]{2,1,0:T(2,128)(2,1)S(1)}, u32[]{:S(2)}, u32[]{:S(2)}) async-start(bf16[8,2,7296]{2,1,0:T(2,128)(2,1)} %shard_map.55), calls=%async_computation | async-start | bytes 466944 | tf_op jit(solution)/shard_map/all_to_all | solution.py:108
  40.8 12.9 %collective-permute-start.1 = (bf16[32,7296]{1,0:T(8,128)(2,1)S(1)}, bf16[32,7296]{1,0:T(8,128)(2,1)S(1)}, u32[]{:S(2)}, u32[]{:S(2)}) collective-permute-start(bf16[32,7296]{1,0:T(8,128)(2,1)S(1)} %convolution_convert_fusion), channel_id=1, source_target_pairs={{0,32},{32,64},{64,96},{96,128},{128,160},{160,192},{192,224},{224... | collective-permute-start | bytes 1400840 | tf_op jit(solution)/shard_map/ppermute | solution.py:143
  44.3 13.7 %collective-permute-start.2 = (bf16[32,7296]{1,0:T(8,128)(2,1)S(1)}, bf16[32,7296]{1,0:T(8,128)(2,1)S(1)}, u32[]{:S(2)}, u32[]{:S(2)}) collective-permute-start(bf16[32,7296]{1,0:T(8,128)(2,1)S(1)} %convolution_convert_fusion), channel_id=1, source_target_pairs={{0,224},{32,0},{64,32},{96,64},{128,96},{160,128},{192,160},{224,1... | collective-permute-start | bytes 1400840 | tf_op jit(solution)/shard_map/ppermute | solution.py:144
  53.7 27.2 %copy-start.7 = (bf16[32,7296]{1,0:T(8,128)(2,1)}, bf16[32,7296]{1,0:T(8,128)(2,1)S(1)}, u32[]{:S(2)}) copy-start(bf16[32,7296]{1,0:T(8,128)(2,1)S(1)} %collective-permute-done.1) | copy-start | bytes 1400836
  58.0 23.0 %copy-start.8 = (bf16[32,7296]{1,0:T(8,128)(2,1)}, bf16[32,7296]{1,0:T(8,128)(2,1)S(1)}, u32[]{:S(2)}) copy-start(bf16[32,7296]{1,0:T(8,128)(2,1)S(1)} %collective-permute-done.2) | copy-start | bytes 1400836
  58.0 12.2 %collective-permute-start.4 = (bf16[32,7296]{1,0:T(8,128)(2,1)S(1)}, bf16[32,7296]{1,0:T(8,128)(2,1)S(1)}, u32[]{:S(2)}, u32[]{:S(2)}) collective-permute-start(bf16[32,7296]{1,0:T(8,128)(2,1)S(1)} %collective-permute-done.1), channel_id=1, source_target_pairs={{0,32},{32,64},{64,96},{96,128},{128,160},{160,192},{192,224},{224... | collective-permute-start | bytes 1400840 | tf_op jit(solution)/shard_map/ppermute | solution.py:143
  62.8 11.4 %collective-permute-start.5 = (bf16[32,7296]{1,0:T(8,128)(2,1)S(1)}, bf16[32,7296]{1,0:T(8,128)(2,1)S(1)}, u32[]{:S(2)}, u32[]{:S(2)}) collective-permute-start(bf16[32,7296]{1,0:T(8,128)(2,1)S(1)} %collective-permute-done.2), channel_id=1, source_target_pairs={{0,224},{32,0},{64,32},{96,64},{128,96},{160,128},{192,160},{224,1... | collective-permute-start | bytes 1400840 | tf_op jit(solution)/shard_map/ppermute | solution.py:144
  70.2 24.8 %copy-start.9 = (bf16[32,7296]{1,0:T(8,128)(2,1)}, bf16[32,7296]{1,0:T(8,128)(2,1)S(1)}, u32[]{:S(2)}) copy-start(bf16[32,7296]{1,0:T(8,128)(2,1)S(1)} %collective-permute-done.4) | copy-start | bytes 1400836
  74.3 20.6 %copy-start.10 = (bf16[32,7296]{1,0:T(8,128)(2,1)}, bf16[32,7296]{1,0:T(8,128)(2,1)S(1)}, u32[]{:S(2)}) copy-start(bf16[32,7296]{1,0:T(8,128)(2,1)S(1)} %collective-permute-done.5) | copy-start | bytes 1400836
  74.3 10.5 %collective-permute-start.6 = (bf16[32,7296]{1,0:T(8,128)(2,1)S(1)}, bf16[32,7296]{1,0:T(8,128)(2,1)S(1)}, u32[]{:S(2)}, u32[]{:S(2)}) collective-permute-start(bf16[32,7296]{1,0:T(8,128)(2,1)S(1)} %collective-permute-done.4), channel_id=1, source_target_pairs={{0,32},{32,64},{64,96},{96,128},{128,160},{160,192},{192,224},{224... | collective-permute-start | bytes 1400840 | tf_op jit(solution)/shard_map/ppermute | solution.py:143
  77.7 10.5 %collective-permute-start.7 = (bf16[32,7296]{1,0:T(8,128)(2,1)S(1)}, bf16[32,7296]{1,0:T(8,128)(2,1)S(1)}, u32[]{:S(2)}, u32[]{:S(2)}) collective-permute-start(bf16[32,7296]{1,0:T(8,128)(2,1)S(1)} %collective-permute-done.5), channel_id=1, source_target_pairs={{0,224},{32,0},{64,32},{96,64},{128,96},{160,128},{192,160},{224,1... | collective-permute-start | bytes 1400840 | tf_op jit(solution)/shard_map/ppermute | solution.py:144
  84.8 15.7 %copy-start.4 = (bf16[32,7296]{1,0:T(8,128)(2,1)}, bf16[32,7296]{1,0:T(8,128)(2,1)S(1)}, u32[]{:S(2)}) copy-start(bf16[32,7296]{1,0:T(8,128)(2,1)S(1)} %collective-permute-done.6) | copy-start | bytes 1400836
  88.2 12.3 %copy-start.5 = (bf16[32,7296]{1,0:T(8,128)(2,1)}, bf16[32,7296]{1,0:T(8,128)(2,1)S(1)}, u32[]{:S(2)}) copy-start(bf16[32,7296]{1,0:T(8,128)(2,1)S(1)} %collective-permute-done.7) | copy-start | bytes 1400836
  88.2 8.0 %collective-permute-start.8 = (bf16[16,7296]{1,0:T(8,128)(2,1)S(1)}, bf16[16,7296]{1,0:T(8,128)(2,1)S(1)}, u32[]{:S(2)}, u32[]{:S(2)}) collective-permute-start(bf16[16,7296]{1,0:T(8,128)(2,1)S(1)} %slice.34), channel_id=1, source_target_pairs={{0,32},{32,64},{64,96},{96,128},{128,160},{160,192},{192,224},{224... | collective-permute-start | bytes 700424 | tf_op jit(solution)/shard_map/ppermute | solution.py:146
  91.7 8.0 %collective-permute-start.9 = (bf16[16,7296]{1,0:T(8,128)(2,1)S(1)}, bf16[16,7296]{1,0:T(8,128)(2,1)S(1)}, u32[]{:S(2)}, u32[]{:S(2)}) collective-permute-start(bf16[16,7296]{1,0:T(8,128)(2,1)S(1)} %slice.35), channel_id=1, source_target_pairs={{0,224},{32,0},{64,32},{96,64},{128,96},{160,128},{192,160},{224,1... | collective-permute-start | bytes 700424 | tf_op jit(solution)/shard_map/ppermute | solution.py:146
  94.9 11.2 %copy-start = (bf16[1,2048,448]{1,2,0:T(8,128)(2,1)S(1)}, bf16[1,2048,448]{1,2,0:T(8,128)(2,1)}, u32[]{:S(2)}) copy-start(bf16[1,2048,448]{1,2,0:T(8,128)(2,1)} %param.9) | copy-start | bytes 5505028
  99.7 16.5 %copy-start.6 = (bf16[32,7296]{1,0:T(8,128)(2,1)}, bf16[32,7296]{1,0:T(8,128)(2,1)S(1)}, u32[]{:S(2)}) copy-start(bf16[32,7296]{1,0:T(8,128)(2,1)S(1)} %constant_dynamic-update-slice_fusion) | copy-start | bytes 1400836
  101.3 13.9 %all-to-all-start.2 = ((bf16[8,96,256]{2,1,0:T(8,128)(2,1)}), bf16[8,96,256]{2,1,0:T(8,128)(2,1)S(1)}, u32[]{:S(2)}, u32[]{:S(2)}) async-start(bf16[8,96,256]{2,1,0:T(8,128)(2,1)} %broadcast_in_dim.5), calls=%async_computation.2 | async-start | bytes 786432 | tf_op jit(solution)/shard_map/all_to_all | solution.py:129
  106.1 21.3 %collective-permute-start = (bf16[448,2048]{1,0:T(8,128)(2,1)S(1)}, bf16[448,2048]{1,0:T(8,128)(2,1)}, u32[]{:S(2)}, u32[]{:S(2)}) collective-permute-start(bf16[448,2048]{1,0:T(8,128)(2,1)S(1)} %bitcast.22), channel_id=1, source_target_pairs={{0,256},{256,0},{1,257},{257,1},{2,258},{258,2},{3,259},{259,3},{4... | collective-permute-start | bytes 5505032 | tf_op jit(solution)/shard_map/ppermute | solution.py:36
  115.2 12.2 %copy-start.1 = (bf16[8,96,256]{2,1,0:T(8,128)(2,1)}, bf16[8,96,256]{2,1,0:T(8,128)(2,1)S(1)}, u32[]{:S(2)}) copy-start(bf16[8,96,256]{2,1,0:T(8,128)(2,1)S(1)} %all-to-all-done.2.refs_1_) | copy-start | bytes 1179652
  116.1 18.7 %all-to-all-start.1 = ((bf16[8,160,256]{2,1,0:T(8,128)(2,1)}), bf16[8,160,256]{2,1,0:T(8,128)(2,1)S(1)}, u32[]{:S(2)}, u32[]{:S(2)}) async-start(bf16[8,160,256]{2,1,0:T(8,128)(2,1)} %broadcast_in_dim.4), calls=%async_computation.1 | async-start | bytes 1310720 | tf_op jit(solution)/shard_map/all_to_all | solution.py:129
  134.8 1.0 copy-start.2

commit v4 on v3

--- a/solution.py
+++ b/solution.py
@@ -38,17 +38,8 @@
 
 def down_kernel(n_grp, n_side, unit, rows, order, where_ref, own_ref, other_ref, *refs):
     got, tails = refs[: len(order)], refs[len(order) : len(order) + n_grp]
-    out_ref, hidden_ref, notes_ref, slab_ref, sems = refs[len(order) + n_grp :]
+    out_ref, hidden_ref, notes_ref = refs[len(order) + n_grp :]
     grp, dev, side = where_ref[0], where_ref[1], where_ref[2]
-    width = own_ref.shape[0]
-    copies = [
-        pltpu.make_async_copy(own_ref, slab_ref.at[pl.ds(pl.multiple_of(side * width, 64), width)], sems.at[0]),
-        pltpu.make_async_copy(
-            other_ref, slab_ref.at[pl.ds(pl.multiple_of((1 - side) * width, 64), width)], sems.at[1]
-        ),
-    ]
-    for copy in copies:
-        copy.start()
     for g in range(n_grp):
         for j in range(n_grp):
             d = (j - g) % n_grp
@@ -63,11 +54,13 @@
     for d in range(n_grp):
         j = lax.rem(grp + d, n_grp)
         notes_ref[pl.ds(pl.multiple_of(j * CAP, CAP), CAP), :] = tails[d][...]
-    for copy in copies:
-        copy.wait()
-    columns = lax.dot_general(
-        hidden_ref[...], slab_ref[...], (((1,), (1,)), ((), ())), preferred_element_type=jnp.float32
-    ).astype(jnp.bfloat16)
+    own, other = [
+        lax.dot_general(
+            hidden_ref[...], slab[...], (((1,), (1,)), ((), ())), preferred_element_type=jnp.float32
+        )
+        for slab in (own_ref, other_ref)
+    ]
+    columns = [jnp.where(side == 0, own, other), jnp.where(side == 0, other, own)]
     slots, tokens = hidden_ref.shape[0], out_ref.shape[0]
     notes = notes_ref[...].astype(jnp.float32)
     lane = lax.broadcasted_iota(jnp.int32, notes.shape, 1)
@@ -80,9 +73,11 @@
     combine = jnp.where(
         lax.broadcasted_iota(jnp.int32, (slots, tokens), 1) == target, weight, 0.0
     ).astype(jnp.bfloat16)
-    out_ref[...] = lax.dot_general(
-        combine, columns, (((0,), (0,)), ((), ())), preferred_element_type=jnp.float32
-    ).astype(jnp.bfloat16)
+    width = own_ref.shape[0]
+    for k in range(n_side):
+        out_ref[:, k * width : (k + 1) * width] = lax.dot_general(
+            combine, columns[k].astype(jnp.bfloat16), (((0,), (0,)), ((), ())), preferred_element_type=jnp.float32
+        ).astype(jnp.bfloat16)
 
 
 def on_device(tokens, expert_ids, route_weights, w_gate, w_down):
@@ -96,7 +91,7 @@
     unit = w_gate.shape[2]
 
     own_gate, own_down = w_gate[0], w_down[0].T
-    other_gate, other_down = from_other_core(own_gate), from_other_core(own_down)
+    other_down = from_other_core(own_down)
 
     vmem, smem = pl.BlockSpec(memory_space=pltpu.VMEM), pl.BlockSpec(memory_space=pltpu.SMEM)
     copies = pl.pallas_call(
@@ -105,6 +100,8 @@
         in_specs=[smem, vmem, vmem, vmem],
         out_specs=vmem,
     )(dev.reshape(1).astype(i32), tokens, expert_ids, route_weights)
+    own_gate, copies = lax.optimization_barrier((own_gate, copies))
+    other_gate = from_other_core(own_gate)
     by_z = lax.all_to_all(copies, "z", split_axis=0, concat_axis=0, tiled=True).reshape(n_z * rows, -1)
     packed = lax.all_gather(by_z, "x", axis=0, tiled=True)
 
@@ -144,12 +141,17 @@
             above = lax.ppermute(above, "grp", down)
         else:
             below, above = lax.ppermute(below[:half], "grp", up), lax.ppermute(above[half:], "grp", down)
-        part = 0 if step <= far - 1 else 1
-        hidden[part].append(silu_gate(held))
+        product = silu_gate(held)
+        part = 0 if step < far else 1
+        hidden[part].append(product)
         order[part] += distances
-        below, above, hidden[part][-1] = lax.optimization_barrier((below, above, hidden[part][-1]))
         if step == far - 1:
             got_early = to_all(jnp.concatenate(hidden[0], axis=0))
+        if step < far:
+            below, product = lax.optimization_barrier((below, product))
+        else:
+            below, product, got_early = lax.optimization_barrier((below, product, got_early))
+        hidden[part][-1] = product
         held = jnp.concatenate([below, above], axis=0)
         distances = [far] if step == far else [n_grp - step, step]
         if step < far:
@@ -161,17 +163,14 @@
 
     slots = n_grp * CAP
     columns = n_side * own_down.shape[0]
-    any_memory = pl.BlockSpec(memory_space=pl.ANY)
     weighted = pl.pallas_call(
         functools.partial(down_kernel, n_grp, n_side, unit, rows, order),
         out_shape=jax.ShapeDtypeStruct((n_grp * group, columns), bf16),
-        in_specs=[smem, any_memory, any_memory] + [vmem] * (len(order) + n_grp),
+        in_specs=[smem] + [vmem] * (2 + len(order) + n_grp),
         out_specs=vmem,
         scratch_shapes=[
             pltpu.VMEM((slots, own_down.shape[1]), bf16),
             pltpu.VMEM((slots, TAIL), bf16),
-            pltpu.VMEM((columns, own_down.shape[1]), bf16),
-            pltpu.SemaphoreType.DMA((2,)),
         ],
         compiler_params=pltpu.CompilerParams(vmem_limit_bytes=40 * 2**20),
     )(

time: 177 us -> 181 us (1.023)
  waiting for transfers between devices: 54 us -> 45.8 us
  starting transfers between devices: 49.7 us -> 54.1 us
  matrix products: 4.24 us -> 8.33 us
  local copies, waits for them, and re-layouts: 8.99 us -> 12.1 us
    all_to_all x2, waiting for transfers between devices: 14.5 us -> 4.48 us  [to_all(): lax.all_to_all(jnp.broadcast_to(hidden[None], (n_grp,) + hidden.shape), '...]
    ppermute x3, waiting for transfers between devices: 11.8 us -> 20.5 us  [on_device(): above = lax.ppermute(above, 'grp', down)]
    all_to_all x2, starting transfers between devices: 11.1 us -> 16.2 us  [to_all(): lax.all_to_all(jnp.broadcast_to(hidden[None], (n_grp,) + hidden.shape), '...]
    dot_general x5, matrix products: 3.96 us -> 8.05 us  [silu_gate(): jnp.dot(block, gate_slab, preferred_element_type=f32)]
    ppermute x1, waiting for transfers between devices: 3.44 us -> 0.01 us  [on_device(): lax.ppermute(above[half:], 'grp', down)]
    ppermute x3, waiting for transfers between devices: 11.1 us -> 7.64 us  [on_device(): below = lax.ppermute(below, 'grp', up)]
    unnamed x23 -> x25, local copies, waits for them, and re-layouts: 1.05 us -> 3.5 us
  transfers between devices with their start and end apart: 13 -> 13, of which waited for: 11 -> 8; matrix products, arithmetic and copies ran while one was open for 8% -> 11% of each run, Pallas kernels for 1% -> 0%
where the time goes in v4:
time: 181 us; the launch traced here: 180 us
  starting transfers between devices  54.1 us (30%)
  blocking collectives  49.3 us (27%)
  waiting for transfers between devices  45.8 us (25%)
  local copies, waits for them, and re-layouts  12.1 us (7%)
  matrix products  8.33 us (5%)
  Pallas kernels  5.03 us (3%)
  other arithmetic  4.68 us (3%)
    all_to_all x1, blocking collectives, on_device(): lax.all_to_all(weighted.reshape(n_dev * n_grp, rows, -1), ('x', 'z', 'grp...  35.1 us
    ppermute x3, waiting for transfers between devices, on_device(): above = lax.ppermute(above, 'grp', down)  20.5 us
    all_to_all x2, starting transfers between devices, to_all(): lax.all_to_all(jnp.broadcast_to(hidden[None], (n_grp,) + hidden.shape), '...  16.2 us
    all_gather x1, blocking collectives, on_device(): packed = lax.all_gather(by_z, 'x', axis=0, tiled=True)  14.3 us
    all_to_all x1, waiting for transfers between devices, on_device(): lax.all_to_all(copies, 'z', split_axis=0, concat_axis=0, tiled=True)  11.9 us
    ppermute x3, starting transfers between devices, on_device(): below = lax.ppermute(below, 'grp', up)  10.6 us
    all_to_all x1, starting transfers between devices, on_device(): lax.all_to_all(copies, 'z', split_axis=0, concat_axis=0, tiled=True)  10.3 us
    dot_general x5, matrix products, silu_gate(): jnp.dot(block, gate_slab, preferred_element_type=f32)  8.05 us
  transfers between devices with their start and end apart: 13, of which 8 were waited for; matrix products, arithmetic and copies ran while one was open for 11% of the time, Pallas kernels for 0%

profile of v4, /device:TPU:16, one launch (start us, length us, event | category | flops | bytes accessed | tf_op | source)
XLA Modules:
  0.0 179.7 jit_solution(8722719327949315059)
XLA Ops:
  0.0 1.8 shard_map.55
  1.8 1.9 %collective-permute-start.2 = (bf16[7168,128]{1,0:T(8,128)(2,1)}, bf16[7168,128]{1,0:T(8,128)(2,1)}, u32[]{:S(2)}, u32[]{:S(2)}) collective-permute-start(bf16[7168,128]{1,0:T(8,128)(2,1)} %bitcast.23), channel_id=1, source_target_pairs={{0,256},{256,0},{1,257},{257,1},{2,258},{258,2},{3,259},{259,3},{4... | collective-permute-start | bytes 5505032 | tf_op jit(solution)/shard_map/ppermute | solution.py:36
  3.7 10.3 %all-to-all-start = ((bf16[8,2,7296]{2,1,0:T(2,128)(2,1)}), bf16[8,2,7296]{2,1,0:T(2,128)(2,1)S(1)}, u32[]{:S(2)}, u32[]{:S(2)}) async-start(bf16[8,2,7296]{2,1,0:T(2,128)(2,1)} %shard_map.55), calls=%async_computation | async-start | bytes 466944 | tf_op jit(solution)/shard_map/all_to_all | solution.py:105
  14.0 11.9 %all-to-all-done = bf16[8,2,7296]{2,1,0:T(2,128)(2,1)S(1)} async-done(((bf16[8,2,7296]{2,1,0:T(2,128)(2,1)}), bf16[8,2,7296]{2,1,0:T(2,128)(2,1)S(1)}, u32[]{:S(2)}, u32[]{:S(2)}) %all-to-all-start) | async-done | bytes 233504 | tf_op jit(solution)/shard_map/all_to_all | solution.py:105
  26.0 14.3 %all_gather.3 = bf16[64,7296]{1,0:T(8,128)(2,1)S(1)} all-gather(bf16[16,7296]{1,0:T(8,128)(2,1)S(1)} %reshape.21), channel_id=1, replica_groups=mesh['side'=2,'grp'=8,'x'=4,'z'=8] {'x'}, dimensions={0}, use_global_device_ids=true | all-gather | bytes 1167360 | tf_op jit(solution)/shard_map/all_gather | solution.py:106
  40.8 3.5 %collective-permute-start.1 = (bf16[32,7296]{1,0:T(8,128)(2,1)S(1)}, bf16[32,7296]{1,0:T(8,128)(2,1)S(1)}, u32[]{:S(2)}, u32[]{:S(2)}) collective-permute-start(bf16[32,7296]{1,0:T(8,128)(2,1)S(1)} %convolution_convert_fusion), channel_id=1, source_target_pairs={{0,32},{32,64},{64,96},{96,128},{128,160},{160,192},{192,224},{224... | collective-permute-start | bytes 1400840 | tf_op jit(solution)/shard_map/ppermute | solution.py:140
  44.3 2.4 %collective-permute-start.4 = (bf16[32,7296]{1,0:T(8,128)(2,1)S(1)}, bf16[32,7296]{1,0:T(8,128)(2,1)S(1)}, u32[]{:S(2)}, u32[]{:S(2)}) collective-permute-start(bf16[32,7296]{1,0:T(8,128)(2,1)S(1)} %convolution_convert_fusion), channel_id=1, source_target_pairs={{0,224},{32,0},{64,32},{96,64},{128,96},{160,128},{192,160},{224,1... | collective-permute-start | bytes 1400840 | tf_op jit(solution)/shard_map/ppermute | solution.py:141
  46.7 1.7 broadcast_select_fusion.1
  48.4 1.8 %fusion.2 = bf16[7296,256]{1,0:T(8,128)(2,1)S(1)} fusion(bf16[7168,128]{1,0:T(8,128)(2,1)S(1)} %get-tuple-element.26, bf16[7168,128]{1,0:T(8,128)(2,1)S(1)} %get-tuple-element.25), kind=kLoop, calls=%fused_computation.4 | loop fusion | flops 13074432 | bytes 7405568 | tf_op jit(solution)/shard_map/concatenate | solution.py:116
  50.3 0.8 multiply_convert_fusion.4
  51.1 2.7 %collective-permute-done.1 = bf16[32,7296]{1,0:T(8,128)(2,1)S(1)} collective-permute-done((bf16[32,7296]{1,0:T(8,128)(2,1)S(1)}, bf16[32,7296]{1,0:T(8,128)(2,1)S(1)}, u32[]{:S(2)}, u32[]{:S(2)}) %collective-permute-start.1) | collective-permute-done | bytes 466976 | tf_op jit(solution)/shard_map/ppermute | solution.py:140
  53.7 3.8 %collective-permute-start.3 = (bf16[32,7296]{1,0:T(8,128)(2,1)S(1)}, bf16[32,7296]{1,0:T(8,128)(2,1)S(1)}, u32[]{:S(2)}, u32[]{:S(2)}) collective-permute-start(bf16[32,7296]{1,0:T(8,128)(2,1)S(1)} %collective-permute-done.1), channel_id=1, source_target_pairs={{0,32},{32,64},{64,96},{96,128},{128,160},{160,192},{192,224},{224... | collective-permute-start | bytes 1400840 | tf_op jit(solution)/shard_map/ppermute | solution.py:140
  57.5 0.5 collective-permute-done.4
  58.0 1.9 %collective-permute-start.6 = (bf16[32,7296]{1,0:T(8,128)(2,1)S(1)}, bf16[32,7296]{1,0:T(8,128)(2,1)S(1)}, u32[]{:S(2)}, u32[]{:S(2)}) collective-permute-start(bf16[32,7296]{1,0:T(8,128)(2,1)S(1)} %collective-permute-done.4), channel_id=1, source_target_pairs={{0,224},{32,0},{64,32},{96,64},{128,96},{160,128},{192,160},{224,1... | collective-permute-start | bytes 1400840 | tf_op jit(solution)/shard_map/ppermute | solution.py:141
  59.9 0.8 multiply_convert_fusion.2
  60.7 5.0 %collective-permute-done.3 = bf16[32,7296]{1,0:T(8,128)(2,1)S(1)} collective-permute-done((bf16[32,7296]{1,0:T(8,128)(2,1)S(1)}, bf16[32,7296]{1,0:T(8,128)(2,1)S(1)}, u32[]{:S(2)}, u32[]{:S(2)}) %collective-permute-start.3) | collective-permute-done | bytes 466976 | tf_op jit(solution)/shard_map/ppermute | solution.py:140
  65.7 5.5 %collective-permute-done.6 = bf16[32,7296]{1,0:T(8,128)(2,1)S(1)} collective-permute-done((bf16[32,7296]{1,0:T(8,128)(2,1)S(1)}, bf16[32,7296]{1,0:T(8,128)(2,1)S(1)}, u32[]{:S(2)}, u32[]{:S(2)}) %collective-permute-start.6) | collective-permute-done | bytes 466976 | tf_op jit(solution)/shard_map/ppermute | solution.py:141
  71.2 0.8 multiply_convert_fusion.1
  72.0 0.9 broadcast_in_dim.4
  73.0 6.6 %all-to-all-start.1 = ((bf16[8,160,256]{2,1,0:T(8,128)(2,1)}), bf16[8,160,256]{2,1,0:T(8,128)(2,1)S(1)}, u32[]{:S(2)}, u32[]{:S(2)}) async-start(bf16[8,160,256]{2,1,0:T(8,128)(2,1)} %broadcast_in_dim.4), calls=%async_computation.1 | async-start | bytes 1310720 | tf_op jit(solution)/shard_map/all_to_all | solution.py:126
  79.5 2.5 %collective-permute-start.8 = (bf16[32,7296]{1,0:T(8,128)(2,1)}, bf16[32,7296]{1,0:T(8,128)(2,1)S(1)}, u32[]{:S(2)}, u32[]{:S(2)}) collective-permute-start(bf16[32,7296]{1,0:T(8,128)(2,1)} %copy-done.11), channel_id=1, source_target_pairs={{0,224},{32,0},{64,32},{96,64},{128,96},{160,128},{192,160},{224,1... | collective-permute-start | bytes 1400840 | tf_op jit(solution)/shard_map/ppermute | solution.py:141
  82.0 3.4 %collective-permute-start.5 = (bf16[32,7296]{1,0:T(8,128)(2,1)}, bf16[32,7296]{1,0:T(8,128)(2,1)S(1)}, u32[]{:S(2)}, u32[]{:S(2)}) collective-permute-start(bf16[32,7296]{1,0:T(8,128)(2,1)} %copy-done.10), channel_id=1, source_target_pairs={{0,32},{32,64},{64,96},{96,128},{128,160},{160,192},{192,224},{224... | collective-permute-start | bytes 1400840 | tf_op jit(solution)/shard_map/ppermute | solution.py:140
  85.4 1.9 %collective-permute-start = (bf16[448,2048]{1,0:T(8,128)(2,1)S(1)}, bf16[448,2048]{1,0:T(8,128)(2,1)}, u32[]{:S(2)}, u32[]{:S(2)}) collective-permute-start(bf16[448,2048]{1,0:T(8,128)(2,1)S(1)} %bitcast.20), channel_id=1, source_target_pairs={{0,256},{256,0},{1,257},{257,1},{2,258},{258,2},{3,259},{259,3},{4... | collective-permute-start | bytes 5505032 | tf_op jit(solution)/shard_map/ppermute | solution.py:36
  87.3 14.6 %collective-permute-done.8 = bf16[32,7296]{1,0:T(8,128)(2,1)S(1)} collective-permute-done((bf16[32,7296]{1,0:T(8,128)(2,1)}, bf16[32,7296]{1,0:T(8,128)(2,1)S(1)}, u32[]{:S(2)}, u32[]{:S(2)}) %collective-permute-start.8) | collective-permute-done | bytes 466976 | tf_op jit(solution)/shard_map/ppermute | solution.py:141
  101.9 0.8 slice.45
  102.6 2.5 %collective-permute-start.9 = (bf16[16,7296]{1,0:T(8,128)(2,1)}, bf16[16,7296]{1,0:T(8,128)(2,1)S(1)}, u32[]{:S(2)}, u32[]{:S(2)}) collective-permute-start(bf16[16,7296]{1,0:T(8,128)(2,1)} %slice.45), channel_id=1, source_target_pairs={{0,224},{32,0},{64,32},{96,64},{128,96},{160,128},{192,160},{224,1... | collective-permute-start | bytes 700424 | tf_op jit(solution)/shard_map/ppermute | solution.py:143
  105.2 4.0 %collective-permute-start.7 = (bf16[16,7296]{1,0:T(8,128)(2,1)S(1)}, bf16[16,7296]{1,0:T(8,128)(2,1)}, u32[]{:S(2)}, u32[]{:S(2)}) collective-permute-start(bf16[16,7296]{1,0:T(8,128)(2,1)S(1)} %slice.34), channel_id=1, source_target_pairs={{0,32},{32,64},{64,96},{96,128},{128,160},{160,192},{192,224},{224... | collective-permute-start | bytes 700424 | tf_op jit(solution)/shard_map/ppermute | solution.py:143
  109.2 2.9 %multiply_convert_fusion = bf16[64,256]{1,0:T(8,128)(2,1)S(1)} fusion(bf16[7296,256]{1,0:T(8,128)(2,1)} %copy-done.3, bf16[32,7296]{1,0:T(8,128)(2,1)S(1)} %collective-permute-done.8, bf16[32,7296]{1,0:T(8,128)(2,1)S(1)} %collective-permute-done.5), kind=kOutput, calls=%fused_computation.20 | convolution fusion | flops 241025024 | bytes 4702208 | tf_op jit(solution)/shard_map/dot_general | solution.py:123
  112.0 1.2 collective-permute-done.7
  113.2 1.0 constant_dynamic-update-slice_fusion.1
  114.2 0.8 copy-done.7
  115.0 2.8 %multiply_convert_fusion.3 = bf16[32,256]{1,0:T(8,128)(2,1)S(1)} fusion(bf16[32,7296]{1,0:T(8,128)(2,1)S(1)} %constant_dynamic-update-slice_fusion, bf16[7296,256]{1,0:T(8,128)(2,1)} %copy-done.3), kind=kOutput, calls=%fused_computation.24 | convolution fusion | flops 119578624 | bytes 4218880 | tf_op jit(solution)/shard_map/dot_general | solution.py:123
  117.8 0.8 broadcast_in_dim.5
  118.6 9.6 %all-to-all-start.2 = ((bf16[8,96,256]{2,1,0:T(8,128)(2,1)}), bf16[8,96,256]{2,1,0:T(8,128)(2,1)S(1)}, u32[]{:S(2)}, u32[]{:S(2)}) async-start(bf16[8,96,256]{2,1,0:T(8,128)(2,1)} %broadcast_in_dim.5), calls=%async_computation.2 | async-start | bytes 786432 | tf_op jit(solution)/shard_map/all_to_all | solution.py:126
  128.3 0.7 slice.47.refs_3_
  129.0 0.7 slice.48.refs_4_
  129.7 0.7 slice.49.refs_5_
  130.4 0.7 slice.43.refs_9_
  131.1 0.7 slice.42.refs_8_
  131.8 0.7 slice.41.refs_7_
  132.5 0.7 slice.50.refs_6_
  133.2 4.5 %all-to-all-done.2.refs_1_ = bf16[8,96,256]{2,1,0:T(8,128)(2,1)S(1)} async-done(((bf16[8,96,256]{2,1,0:T(8,128)(2,1)}), bf16[8,96,256]{2,1,0:T(8,128)(2,1)S(1)}, u32[]{:S(2)}, u32[]{:S(2)}) %all-to-all-start.2) | async-done | bytes 393248 | tf_op jit(solution)/shard_map/all_to_all | solution.py:126
  137.6 0.8 copy-done.1
  138.4 1.0 copy-done.2
  139.4 3.3 %shard_map.56 = bf16[512,896]{1,0:T(8,128)(2,1)S(1)} custom-call(s32[3]{0:T(128)S(1)} %pad_add_fusion.where_ref, bf16[448,2048]{1,0:T(8,128)(2,1)S(1)} %bitcast.21, bf16[448,2048]{1,0:T(8,128)(2,1)} %collective-permute-done.other_ref, bf16[8,160,256]{2,1,0:T(8,128)(2,1)S(1)} %all-to-all-done.1.refs_0_, bf16[8,96,256]{2,1,0:T(8,128)(2,1)S(1)} %copy-done.2, ...), custom_call_target="tpu_custom_call" | custom-call | tf_op jit(solution)/shard_map/pallas_call | solution.py:166
  143.0 35.1 %all_to_all.20 = bf16[256,2,896]{2,1,0:T(2,128)(2,1)S(1)} all-to-all(bf16[256,2,896]{2,1,0:T(2,128)(2,1)S(1)} %reshape.22), channel_id=1, replica_groups=mesh['side'=2,'grp'=8,'x'=4,'z'=8] {'x','z','grp'}, dimensions={0} | all-to-all | bytes 1835008 | tf_op jit(solution)/shard_map/all_to_all | solution.py:184
  178.1 0.8 reduce_sum.22
  179.0 0.7 reshape.25
  (39 shorter events, 1.2 us)
Async XLA Ops:
  0.0 46.7 %copy-start.4 = (bf16[1,7168,128]{2,1,0:T(8,128)(2,1)S(1)}, bf16[1,7168,128]{2,1,0:T(8,128)(2,1)}, u32[]{:S(2)}) copy-start(bf16[1,7168,128]{2,1,0:T(8,128)(2,1)} %param.8) | copy-start | bytes 5505028
  1.8 44.9 %collective-permute-start.2 = (bf16[7168,128]{1,0:T(8,128)(2,1)}, bf16[7168,128]{1,0:T(8,128)(2,1)}, u32[]{:S(2)}, u32[]{:S(2)}) collective-permute-start(bf16[7168,128]{1,0:T(8,128)(2,1)} %bitcast.23), channel_id=1, source_target_pairs={{0,256},{256,0},{1,257},{257,1},{2,258},{258,2},{3,259},{259,3},{4... | collective-permute-start | bytes 5505032 | tf_op jit(solution)/shard_map/ppermute | solution.py:36
  3.7 22.3 %all-to-all-start = ((bf16[8,2,7296]{2,1,0:T(2,128)(2,1)}), bf16[8,2,7296]{2,1,0:T(2,128)(2,1)S(1)}, u32[]{:S(2)}, u32[]{:S(2)}) async-start(bf16[8,2,7296]{2,1,0:T(2,128)(2,1)} %shard_map.55), calls=%async_computation | async-start | bytes 466944 | tf_op jit(solution)/shard_map/all_to_all | solution.py:105
  40.8 12.9 %collective-permute-start.1 = (bf16[32,7296]{1,0:T(8,128)(2,1)S(1)}, bf16[32,7296]{1,0:T(8,128)(2,1)S(1)}, u32[]{:S(2)}, u32[]{:S(2)}) collective-permute-start(bf16[32,7296]{1,0:T(8,128)(2,1)S(1)} %convolution_convert_fusion), channel_id=1, source_target_pairs={{0,32},{32,64},{64,96},{96,128},{128,160},{160,192},{192,224},{224... | collective-permute-start | bytes 1400840 | tf_op jit(solution)/shard_map/ppermute | solution.py:140
  44.3 13.7 %collective-permute-start.4 = (bf16[32,7296]{1,0:T(8,128)(2,1)S(1)}, bf16[32,7296]{1,0:T(8,128)(2,1)S(1)}, u32[]{:S(2)}, u32[]{:S(2)}) collective-permute-start(bf16[32,7296]{1,0:T(8,128)(2,1)S(1)} %convolution_convert_fusion), channel_id=1, source_target_pairs={{0,224},{32,0},{64,32},{96,64},{128,96},{160,128},{192,160},{224,1... | collective-permute-start | bytes 1400840 | tf_op jit(solution)/shard_map/ppermute | solution.py:141
  50.3 20.9 %copy-start.3 = (bf16[7296,256]{1,0:T(8,128)(2,1)}, bf16[7296,256]{1,0:T(8,128)(2,1)S(1)}, u32[]{:S(2)}) copy-start(bf16[7296,256]{1,0:T(8,128)(2,1)S(1)} %fusion.2) | copy-start | bytes 11206660
  53.7 18.3 %copy-start.8 = (bf16[32,7296]{1,0:T(8,128)(2,1)}, bf16[32,7296]{1,0:T(8,128)(2,1)S(1)}, u32[]{:S(2)}) copy-start(bf16[32,7296]{1,0:T(8,128)(2,1)S(1)} %collective-permute-done.1) | copy-start | bytes 1400836
  53.7 12.0 %collective-permute-start.3 = (bf16[32,7296]{1,0:T(8,128)(2,1)S(1)}, bf16[32,7296]{1,0:T(8,128)(2,1)S(1)}, u32[]{:S(2)}, u32[]{:S(2)}) collective-permute-start(bf16[32,7296]{1,0:T(8,128)(2,1)S(1)} %collective-permute-done.1), channel_id=1, source_target_pairs={{0,32},{32,64},{64,96},{96,128},{128,160},{160,192},{192,224},{224... | collective-permute-start | bytes 1400840 | tf_op jit(solution)/shard_map/ppermute | solution.py:140
  58.0 14.0 %copy-start.9 = (bf16[32,7296]{1,0:T(8,128)(2,1)}, bf16[32,7296]{1,0:T(8,128)(2,1)S(1)}, u32[]{:S(2)}) copy-start(bf16[32,7296]{1,0:T(8,128)(2,1)S(1)} %collective-permute-done.4) | copy-start | bytes 1400836
  58.0 13.2 %collective-permute-start.6 = (bf16[32,7296]{1,0:T(8,128)(2,1)S(1)}, bf16[32,7296]{1,0:T(8,128)(2,1)S(1)}, u32[]{:S(2)}, u32[]{:S(2)}) collective-permute-start(bf16[32,7296]{1,0:T(8,128)(2,1)S(1)} %collective-permute-done.4), channel_id=1, source_target_pairs={{0,224},{32,0},{64,32},{96,64},{128,96},{160,128},{192,160},{224,1... | collective-permute-start | bytes 1400840 | tf_op jit(solution)/shard_map/ppermute | solution.py:141
  60.7 24.7 %copy-start = (bf16[1,2048,448]{1,2,0:T(8,128)(2,1)S(1)}, bf16[1,2048,448]{1,2,0:T(8,128)(2,1)}, u32[]{:S(2)}) copy-start(bf16[1,2048,448]{1,2,0:T(8,128)(2,1)} %param.9) | copy-start | bytes 5505028
  65.7 7.2 %copy-start.10 = (bf16[32,7296]{1,0:T(8,128)(2,1)}, bf16[32,7296]{1,0:T(8,128)(2,1)S(1)}, u32[]{:S(2)}) copy-start(bf16[32,7296]{1,0:T(8,128)(2,1)S(1)} %collective-permute-done.3) | copy-start | bytes 1400836
  71.2 0.8 copy-start.11
  73.0 40.3 %all-to-all-start.1 = ((bf16[8,160,256]{2,1,0:T(8,128)(2,1)}), bf16[8,160,256]{2,1,0:T(8,128)(2,1)S(1)}, u32[]{:S(2)}, u32[]{:S(2)}) async-start(bf16[8,160,256]{2,1,0:T(8,128)(2,1)} %broadcast_in_dim.4), calls=%async_computation.1 | async-start | bytes 1310720 | tf_op jit(solution)/shard_map/all_to_all | solution.py:126
  79.5 22.3 %collective-permute-start.8 = (bf16[32,7296]{1,0:T(8,128)(2,1)}, bf16[32,7296]{1,0:T(8,128)(2,1)S(1)}, u32[]{:S(2)}, u32[]{:S(2)}) collective-permute-start(bf16[32,7296]{1,0:T(8,128)(2,1)} %copy-done.11), channel_id=1, source_target_pairs={{0,224},{32,0},{64,32},{96,64},{128,96},{160,128},{192,160},{224,1... | collective-permute-start | bytes 1400840 | tf_op jit(solution)/shard_map/ppermute | solution.py:141
  82.0 23.1 %collective-permute-start.5 = (bf16[32,7296]{1,0:T(8,128)(2,1)}, bf16[32,7296]{1,0:T(8,128)(2,1)S(1)}, u32[]{:S(2)}, u32[]{:S(2)}) collective-permute-start(bf16[32,7296]{1,0:T(8,128)(2,1)} %copy-done.10), channel_id=1, source_target_pairs={{0,32},{32,64},{64,96},{96,128},{128,160},{160,192},{192,224},{224... | collective-permute-start | bytes 1400840 | tf_op jit(solution)/shard_map/ppermute | solution.py:140
  85.4 47.8 %collective-permute-start = (bf16[448,2048]{1,0:T(8,128)(2,1)S(1)}, bf16[448,2048]{1,0:T(8,128)(2,1)}, u32[]{:S(2)}, u32[]{:S(2)}) collective-permute-start(bf16[448,2048]{1,0:T(8,128)(2,1)S(1)} %bitcast.20), channel_id=1, source_target_pairs={{0,256},{256,0},{1,257},{257,1},{2,258},{258,2},{3,259},{259,3},{4... | collective-permute-start | bytes 5505032 | tf_op jit(solution)/shard_map/ppermute | solution.py:36
  101.9 10.1 %copy-start.6 = (bf16[32,7296]{1,0:T(8,128)(2,1)}, bf16[32,7296]{1,0:T(8,128)(2,1)S(1)}, u32[]{:S(2)}) copy-start(bf16[32,7296]{1,0:T(8,128)(2,1)S(1)} %collective-permute-done.8) | copy-start | bytes 1400836
  102.6 11.5 %collective-permute-start.9 = (bf16[16,7296]{1,0:T(8,128)(2,1)}, bf16[16,7296]{1,0:T(8,128)(2,1)S(1)}, u32[]{:S(2)}, u32[]{:S(2)}) collective-permute-start(bf16[16,7296]{1,0:T(8,128)(2,1)} %slice.45), channel_id=1, source_target_pairs={{0,224},{32,0},{64,32},{96,64},{128,96},{160,128},{192,160},{224,1... | collective-permute-start | bytes 700424 | tf_op jit(solution)/shard_map/ppermute | solution.py:143
  105.1 6.9 %copy-start.5 = (bf16[32,7296]{1,0:T(8,128)(2,1)}, bf16[32,7296]{1,0:T(8,128)(2,1)S(1)}, u32[]{:S(2)}) copy-start(bf16[32,7296]{1,0:T(8,128)(2,1)S(1)} %collective-permute-done.5) | copy-start | bytes 1400836
  105.2 8.1 %collective-permute-start.7 = (bf16[16,7296]{1,0:T(8,128)(2,1)S(1)}, bf16[16,7296]{1,0:T(8,128)(2,1)}, u32[]{:S(2)}, u32[]{:S(2)}) collective-permute-start(bf16[16,7296]{1,0:T(8,128)(2,1)S(1)} %slice.34), channel_id=1, source_target_pairs={{0,32},{32,64},{64,96},{96,128},{128,160},{160,192},{192,224},{224... | collective-permute-start | bytes 700424 | tf_op jit(solution)/shard_map/ppermute | solution.py:143
  114.2 0.8 copy-start.7
  118.6 19.0 %all-to-all-start.2 = ((bf16[8,96,256]{2,1,0:T(8,128)(2,1)}), bf16[8,96,256]{2,1,0:T(8,128)(2,1)S(1)}, u32[]{:S(2)}, u32[]{:S(2)}) async-start(bf16[8,96,256]{2,1,0:T(8,128)(2,1)} %broadcast_in_dim.5), calls=%async_computation.2 | async-start | bytes 786432 | tf_op jit(solution)/shard_map/all_to_all | solution.py:126
  137.6 0.8 copy-start.1
  138.4 1.0 copy-start.2

commit v5 on v4

--- a/solution.py
+++ b/solution.py
@@ -36,21 +36,17 @@
     return lax.ppermute(own, "side", [(0, 1), (1, 0)])
 
 
-def down_kernel(n_grp, n_side, unit, rows, order, where_ref, own_ref, other_ref, *refs):
-    got, tails = refs[: len(order)], refs[len(order) : len(order) + n_grp]
-    out_ref, hidden_ref, notes_ref = refs[len(order) + n_grp :]
+def down_kernel(n_grp, n_side, unit, rows, order, where_ref, own_ref, other_ref, got_ref, *refs):
+    *tails, out_ref, hidden_ref, notes_ref = refs
     grp, dev, side = where_ref[0], where_ref[1], where_ref[2]
     for g in range(n_grp):
         for j in range(n_grp):
-            d = (j - g) % n_grp
-            for ref, distances in zip(got, order):
-                if d in distances:
-                    start = distances.index(d) * CAP
-                    for k in range(n_side):
-                        at = (k * n_grp + g) * unit
-                        hidden_ref[j * CAP : (j + 1) * CAP, at : at + unit] = ref[
-                            g, start : start + CAP, k * unit : (k + 1) * unit
-                        ]
+            start = order.index((j - g) % n_grp) * CAP
+            for k in range(n_side):
+                at = (k * n_grp + g) * unit
+                hidden_ref[j * CAP : (j + 1) * CAP, at : at + unit] = got_ref[
+                    g, start : start + CAP, k * unit : (k + 1) * unit
+                ]
     for d in range(n_grp):
         j = lax.rem(grp + d, n_grp)
         notes_ref[pl.ds(pl.multiple_of(j * CAP, CAP), CAP), :] = tails[d][...]
@@ -100,8 +96,6 @@
         in_specs=[smem, vmem, vmem, vmem],
         out_specs=vmem,
     )(dev.reshape(1).astype(i32), tokens, expert_ids, route_weights)
-    own_gate, copies = lax.optimization_barrier((own_gate, copies))
-    other_gate = from_other_core(own_gate)
     by_z = lax.all_to_all(copies, "z", split_axis=0, concat_axis=0, tiled=True).reshape(n_z * rows, -1)
     packed = lax.all_gather(by_z, "x", axis=0, tiled=True)
 
@@ -112,73 +106,59 @@
     placed = (slot[None, :] == jnp.arange(CAP, dtype=i32)[:, None]) & hit[None, :]
     slot_input = jnp.dot(placed.astype(bf16), packed, preferred_element_type=f32).astype(bf16)
 
-    gate_slab = jnp.pad(
-        jnp.concatenate(
-            [jnp.where(side == 0, own_gate, other_gate), jnp.where(side == 0, other_gate, own_gate)], axis=1
-        ),
-        ((0, TAIL), (0, 0)),
-    )
-
-    def silu_gate(block):
+    def silu_gate(parts):
+        block = jnp.concatenate(parts, axis=0)
         return jax.nn.silu(jnp.dot(block, gate_slab, preferred_element_type=f32)).astype(bf16)
-
-    def to_all(hidden):
-        return lax.all_to_all(
-            jnp.broadcast_to(hidden[None], (n_grp,) + hidden.shape), "grp", split_axis=0, concat_axis=0, tiled=True
-        )
 
     up = [(i, (i + 1) % n_grp) for i in range(n_grp)]
     down = [(i, (i - 1) % n_grp) for i in range(n_grp)]
     half, far = CAP // 2, n_grp // 2
-    blocks = {0: slot_input}
-    below = above = held = slot_input
-    hidden, order = [[], []], [[], []]
-    distances = [0]
-    got_early = None
-    for step in range(1, far + 1):
-        if step < far:
-            below = lax.ppermute(below, "grp", up)
-            above = lax.ppermute(above, "grp", down)
-        else:
-            below, above = lax.ppermute(below[:half], "grp", up), lax.ppermute(above[half:], "grp", down)
-        product = silu_gate(held)
-        part = 0 if step < far else 1
-        hidden[part].append(product)
-        order[part] += distances
+    below = above = slot_input
+    blocks, order, waiting, hidden = {0: slot_input}, [0], [slot_input], []
+    for step in range(1, far):
+        below = lax.ppermute(below, "grp", up)
+        above = lax.ppermute(above, "grp", down)
+        if step == 1:
+            below, own_gate = lax.optimization_barrier((below, own_gate))
+            other_gate = from_other_core(own_gate)
+            both = [jnp.where(side == 0, own_gate, other_gate), jnp.where(side == 0, other_gate, own_gate)]
+            gate_slab = jnp.pad(jnp.concatenate(both, axis=1), ((0, TAIL), (0, 0)))
         if step == far - 1:
-            got_early = to_all(jnp.concatenate(hidden[0], axis=0))
-        if step < far:
+            product = silu_gate(waiting)
             below, product = lax.optimization_barrier((below, product))
-        else:
-            below, product, got_early = lax.optimization_barrier((below, product, got_early))
-        hidden[part][-1] = product
-        held = jnp.concatenate([below, above], axis=0)
-        distances = [far] if step == far else [n_grp - step, step]
-        if step < far:
-            blocks[n_grp - step], blocks[step] = below, above
-    blocks[far] = held
-    hidden[1].append(silu_gate(held))
-    order[1] += distances
-    got_late = to_all(jnp.concatenate(hidden[1], axis=0))
+            hidden.append(product)
+            waiting = []
+        blocks[n_grp - step], blocks[step] = below, above
+        order += [n_grp - step, step]
+        waiting += [below, above]
+    below, above = lax.ppermute(below[:half], "grp", up), lax.ppermute(above[half:], "grp", down)
+    product = silu_gate(waiting)
+    below, product = lax.optimization_barrier((below, product))
+    blocks[far] = jnp.concatenate([below, above], axis=0)
+    order.append(far)
+    hidden += [product, silu_gate([blocks[far]])]
+    hidden = jnp.concatenate(hidden, axis=0)
+    got = lax.all_to_all(
+        jnp.broadcast_to(hidden[None], (n_grp,) + hidden.shape), "grp", split_axis=0, concat_axis=0, tiled=True
+    )
 
     slots = n_grp * CAP
     columns = n_side * own_down.shape[0]
     weighted = pl.pallas_call(
         functools.partial(down_kernel, n_grp, n_side, unit, rows, order),
         out_shape=jax.ShapeDtypeStruct((n_grp * group, columns), bf16),
-        in_specs=[smem] + [vmem] * (2 + len(order) + n_grp),
+        in_specs=[smem] + [vmem] * (3 + n_grp),
         out_specs=vmem,
         scratch_shapes=[
             pltpu.VMEM((slots, own_down.shape[1]), bf16),
             pltpu.VMEM((slots, TAIL), bf16),
         ],
-        compiler_params=pltpu.CompilerParams(vmem_limit_bytes=40 * 2**20),
+        compiler_params=pltpu.CompilerParams(vmem_limit_bytes=16 * 2**20),
     )(
         jnp.stack([lax.axis_index("grp"), dev, side]).astype(i32),
         own_down,
         other_down,
-        got_early,
-        got_late,
+        got,
         *[blocks[d][:, width:] for d in range(n_grp)],
     )
     parts = lax.all_to_all(

time: 181 us -> 184 us (1.017)
  blocking collectives: 49.3 us -> 74.2 us
  starting transfers between devices: 54.1 us -> 39.1 us
  matrix products: 8.33 us -> 3.46 us
    all_to_all x0 -> x1, blocking collectives: none -> 21.6 us  [on_device(): lax.all_to_all(copies, 'z', split_axis=0, concat_axis=0, tiled=True)]
    all_to_all x3 -> x1, starting transfers between devices: 26.5 us -> 9.99 us  [on_device(): lax.all_to_all(jnp.broadcast_to(hidden[None], (n_grp,) + hidden.shape), '...]
    dot_general x5 -> x3, matrix products: 8.05 us -> 2.39 us  [silu_gate(): jnp.dot(block, gate_slab, preferred_element_type=f32)]
    all_to_all x1, blocking collectives: 35.1 us -> 37.5 us  [on_device(): lax.all_to_all(weighted.reshape(n_dev * n_grp, rows, -1), ('x', 'z', 'grp...]
    ppermute x3, waiting for transfers between devices: 7.64 us -> 5.52 us  [on_device(): below = lax.ppermute(below, 'grp', up)]
    unnamed x25 -> x26, local copies, waits for them, and re-layouts: 3.5 us -> 3.97 us
    all_to_all x3 -> x1, waiting for transfers between devices: 16.4 us -> 16.7 us  [on_device(): lax.all_to_all(jnp.broadcast_to(hidden[None], (n_grp,) + hidden.shape), '...]
  transfers between devices with their start and end apart: 13 -> 11, of which waited for: 8 -> 7; matrix products, arithmetic and copies ran while one was open for 11% -> 8% of each run, Pallas kernels for 0% -> 0%
where the time goes in v5:
time: 184 us; the launch traced here: 183 us
  blocking collectives  74.2 us (40%)
  waiting for transfers between devices  45.3 us (25%)
  starting transfers between devices  39.1 us (21%)
  local copies, waits for them, and re-layouts  12 us (7%)
  Pallas kernels  5.08 us (3%)
  matrix products  3.46 us (2%)
  other arithmetic  3.18 us (2%)
    all_to_all x1, blocking collectives, on_device(): lax.all_to_all(weighted.reshape(n_dev * n_grp, rows, -1), ('x', 'z', 'grp...  37.5 us
    all_to_all x1, blocking collectives, on_device(): lax.all_to_all(copies, 'z', split_axis=0, concat_axis=0, tiled=True)  21.6 us
    ppermute x3, waiting for transfers between devices, on_device(): above = lax.ppermute(above, 'grp', down)  20.3 us
    all_to_all x1, waiting for transfers between devices, on_device(): lax.all_to_all(jnp.broadcast_to(hidden[None], (n_grp,) + hidden.shape), '...  16.7 us
    all_gather x1, blocking collectives, on_device(): packed = lax.all_gather(by_z, 'x', axis=0, tiled=True)  15.1 us
    ppermute x3, starting transfers between devices, on_device(): below = lax.ppermute(below, 'grp', up)  12.3 us
    all_to_all x1, starting transfers between devices, on_device(): lax.all_to_all(jnp.broadcast_to(hidden[None], (n_grp,) + hidden.shape), '...  9.99 us
    ppermute x3, starting transfers between devices, on_device(): above = lax.ppermute(above, 'grp', down)  6.31 us
  transfers between devices with their start and end apart: 11, of which 7 were waited for; matrix products, arithmetic and copies ran while one was open for 8% of the time, Pallas kernels for 0%

profile of v5, /device:TPU:16, one launch (start us, length us, event | category | flops | bytes accessed | tf_op | source)
XLA Modules:
  0.0 182.7 jit_solution(9613266977939166237)
XLA Ops:
  0.0 1.8 shard_map.55
  1.8 21.6 %all_to_all.15 = bf16[8,2,7296]{2,1,0:T(2,128)(2,1)S(1)} all-to-all(bf16[8,2,7296]{2,1,0:T(2,128)(2,1)} %shard_map.55), channel_id=1, replica_groups=mesh['side'=2,'grp'=8,'x'=4,'z'=8] {'z'}, dimensions={0} | all-to-all | bytes 466944 | tf_op jit(solution)/shard_map/all_to_all | solution.py:99
  23.4 15.1 %all_gather.3 = bf16[64,7296]{1,0:T(8,128)(2,1)S(1)} all-gather(bf16[16,7296]{1,0:T(8,128)(2,1)S(1)} %reshape.20), channel_id=1, replica_groups=mesh['side'=2,'grp'=8,'x'=4,'z'=8] {'x'}, dimensions={0}, use_global_device_ids=true | all-gather | bytes 1167360 | tf_op jit(solution)/shard_map/all_gather | solution.py:100
  38.5 0.1 fusion.10
  38.6 0.1 convert_reduce_fusion
  38.7 1.1 constant_dynamic-update-slice_fusion.4
  39.8 3.5 %collective-permute-start.1 = (bf16[32,7296]{1,0:T(8,128)(2,1)S(1)}, bf16[32,7296]{1,0:T(8,128)(2,1)S(1)}, u32[]{:S(2)}, u32[]{:S(2)}) collective-permute-start(bf16[32,7296]{1,0:T(8,128)(2,1)S(1)} %get-tuple-element.20), channel_id=1, source_target_pairs={{0,32},{32,64},{64,96},{96,128},{128,160},{160,192},{192,224},{224... | collective-permute-start | bytes 1400840 | tf_op jit(solution)/shard_map/ppermute | solution.py:119
  43.3 1.9 %collective-permute-start = (bf16[448,2048]{1,0:T(8,128)(2,1)S(1)}, bf16[448,2048]{1,0:T(8,128)(2,1)}, u32[]{:S(2)}, u32[]{:S(2)}) collective-permute-start(bf16[448,2048]{1,0:T(8,128)(2,1)S(1)} %bitcast.18), channel_id=1, source_target_pairs={{0,256},{256,0},{1,257},{257,1},{2,258},{258,2},{3,259},{259,3},{4... | collective-permute-start | bytes 5505032 | tf_op jit(solution)/shard_map/ppermute | solution.py:36
  45.2 2.5 %collective-permute-start.4 = (bf16[32,7296]{1,0:T(8,128)(2,1)S(1)}, bf16[32,7296]{1,0:T(8,128)(2,1)S(1)}, u32[]{:S(2)}, u32[]{:S(2)}) collective-permute-start(bf16[32,7296]{1,0:T(8,128)(2,1)S(1)} %get-tuple-element.20), channel_id=1, source_target_pairs={{0,224},{32,0},{64,32},{96,64},{128,96},{160,128},{192,160},{224,1... | collective-permute-start | bytes 1400840 | tf_op jit(solution)/shard_map/ppermute | solution.py:120
  47.7 2.5 %collective-permute-done.1 = bf16[32,7296]{1,0:T(8,128)(2,1)S(1)} collective-permute-done((bf16[32,7296]{1,0:T(8,128)(2,1)S(1)}, bf16[32,7296]{1,0:T(8,128)(2,1)S(1)}, u32[]{:S(2)}, u32[]{:S(2)}) %collective-permute-start.1) | collective-permute-done | bytes 466976 | tf_op jit(solution)/shard_map/ppermute | solution.py:119
  50.2 1.9 %collective-permute-start.6 = (bf16[7168,128]{1,0:T(8,128)(2,1)}, bf16[7168,128]{1,0:T(8,128)(2,1)S(1)}, u32[]{:S(2)}, u32[]{:S(2)}) collective-permute-start(bf16[7168,128]{1,0:T(8,128)(2,1)} %bitcast.21), channel_id=1, source_target_pairs={{0,256},{256,0},{1,257},{257,1},{2,258},{258,2},{3,259},{259,3},{4... | collective-permute-start | bytes 5505032 | tf_op jit(solution)/shard_map/ppermute | solution.py:36
  52.2 3.8 %collective-permute-start.2 = (bf16[32,7296]{1,0:T(8,128)(2,1)S(1)}, bf16[32,7296]{1,0:T(8,128)(2,1)S(1)}, u32[]{:S(2)}, u32[]{:S(2)}) collective-permute-start(bf16[32,7296]{1,0:T(8,128)(2,1)S(1)} %collective-permute-done.1), channel_id=1, source_target_pairs={{0,32},{32,64},{64,96},{96,128},{128,160},{160,192},{192,224},{224... | collective-permute-start | bytes 1400840 | tf_op jit(solution)/shard_map/ppermute | solution.py:119
  56.0 0.8 constant_dynamic-update-slice_fusion.3
  56.7 4.7 %collective-permute-done.4 = bf16[32,7296]{1,0:T(8,128)(2,1)S(1)} collective-permute-done((bf16[32,7296]{1,0:T(8,128)(2,1)S(1)}, bf16[32,7296]{1,0:T(8,128)(2,1)S(1)}, u32[]{:S(2)}, u32[]{:S(2)}) %collective-permute-start.4) | collective-permute-done | bytes 466976 | tf_op jit(solution)/shard_map/ppermute | solution.py:120
  61.4 1.9 %collective-permute-start.5 = (bf16[32,7296]{1,0:T(8,128)(2,1)S(1)}, bf16[32,7296]{1,0:T(8,128)(2,1)S(1)}, u32[]{:S(2)}, u32[]{:S(2)}) collective-permute-start(bf16[32,7296]{1,0:T(8,128)(2,1)S(1)} %collective-permute-done.4), channel_id=1, source_target_pairs={{0,224},{32,0},{64,32},{96,64},{128,96},{160,128},{192,160},{224,1... | collective-permute-start | bytes 1400840 | tf_op jit(solution)/shard_map/ppermute | solution.py:120
  63.3 0.8 constant_dynamic-update-slice_fusion.2
  64.1 3.0 %collective-permute-done.2 = bf16[32,7296]{1,0:T(8,128)(2,1)S(1)} collective-permute-done((bf16[32,7296]{1,0:T(8,128)(2,1)S(1)}, bf16[32,7296]{1,0:T(8,128)(2,1)S(1)}, u32[]{:S(2)}, u32[]{:S(2)}) %collective-permute-start.2) | collective-permute-done | bytes 466976 | tf_op jit(solution)/shard_map/ppermute | solution.py:119
  67.2 5.0 %collective-permute-start.3 = (bf16[32,7296]{1,0:T(8,128)(2,1)S(1)}, bf16[32,7296]{1,0:T(8,128)(2,1)S(1)}, u32[]{:S(2)}, u32[]{:S(2)}) collective-permute-start(bf16[32,7296]{1,0:T(8,128)(2,1)S(1)} %collective-permute-done.2), channel_id=1, source_target_pairs={{0,32},{32,64},{64,96},{96,128},{128,160},{160,192},{192,224},{224... | collective-permute-start | bytes 1400840 | tf_op jit(solution)/shard_map/ppermute | solution.py:119
  72.1 4.7 %collective-permute-done.5 = bf16[32,7296]{1,0:T(8,128)(2,1)S(1)} collective-permute-done((bf16[32,7296]{1,0:T(8,128)(2,1)S(1)}, bf16[32,7296]{1,0:T(8,128)(2,1)S(1)}, u32[]{:S(2)}, u32[]{:S(2)}) %collective-permute-start.5) | collective-permute-done | bytes 466976 | tf_op jit(solution)/shard_map/ppermute | solution.py:120
  76.8 1.9 %collective-permute-start.8 = (bf16[32,7296]{1,0:T(8,128)(2,1)S(1)}, bf16[32,7296]{1,0:T(8,128)(2,1)S(1)}, u32[]{:S(2)}, u32[]{:S(2)}) collective-permute-start(bf16[32,7296]{1,0:T(8,128)(2,1)S(1)} %collective-permute-done.5), channel_id=1, source_target_pairs={{0,224},{32,0},{64,32},{96,64},{128,96},{160,128},{192,160},{224,1... | collective-permute-start | bytes 1400840 | tf_op jit(solution)/shard_map/ppermute | solution.py:120
  78.7 0.8 constant_dynamic-update-slice_fusion.1
  79.5 0.8 constant_dynamic-update-slice_fusion
  80.3 11.0 %collective-permute-done.8 = bf16[32,7296]{1,0:T(8,128)(2,1)S(1)} collective-permute-done((bf16[32,7296]{1,0:T(8,128)(2,1)S(1)}, bf16[32,7296]{1,0:T(8,128)(2,1)S(1)}, u32[]{:S(2)}, u32[]{:S(2)}) %collective-permute-start.8) | collective-permute-done | bytes 466976 | tf_op jit(solution)/shard_map/ppermute | solution.py:120
  91.4 1.9 %collective-permute-start.9 = (bf16[16,7296]{1,0:T(8,128)(2,1)S(1)}, bf16[16,7296]{1,0:T(8,128)(2,1)S(1)}, u32[]{:S(2)}, u32[]{:S(2)}) collective-permute-start(bf16[16,7296]{1,0:T(8,128)(2,1)S(1)} %slice.45), channel_id=1, source_target_pairs={{0,224},{32,0},{64,32},{96,64},{128,96},{160,128},{192,160},{224,1... | collective-permute-start | bytes 700424 | tf_op jit(solution)/shard_map/ppermute | solution.py:134
  93.3 0.2 broadcast_select_fusion.1
  93.6 1.8 fusion.2
  95.4 0.8 multiply_convert_fusion
  96.3 4.9 %collective-permute-start.7 = (bf16[16,7296]{1,0:T(8,128)(2,1)S(1)}, bf16[16,7296]{1,0:T(8,128)(2,1)S(1)}, u32[]{:S(2)}, u32[]{:S(2)}) collective-permute-start(bf16[16,7296]{1,0:T(8,128)(2,1)S(1)} %slice.34), channel_id=1, source_target_pairs={{0,32},{32,64},{64,96},{96,128},{128,160},{160,192},{192,224},{224... | collective-permute-start | bytes 700424 | tf_op jit(solution)/shard_map/ppermute | solution.py:134
  101.2 0.8 multiply_convert_fusion.1
  102.0 2.7 %collective-permute-done.7 = bf16[16,7296]{1,0:T(8,128)(2,1)S(1)} collective-permute-done((bf16[16,7296]{1,0:T(8,128)(2,1)S(1)}, bf16[16,7296]{1,0:T(8,128)(2,1)S(1)}, u32[]{:S(2)}, u32[]{:S(2)}) %collective-permute-start.7) | collective-permute-done | bytes 233504 | tf_op jit(solution)/shard_map/ppermute | solution.py:134
  104.8 0.8 multiply_convert_fusion.2
  105.6 1.0 broadcast_in_dim.2
  106.6 10.0 %all-to-all-start.1 = ((bf16[8,256,256]{2,1,0:T(8,128)(2,1)}), bf16[8,256,256]{2,1,0:T(8,128)(2,1)S(1)}, u32[]{:S(2)}, u32[]{:S(2)}) async-start(bf16[8,256,256]{2,1,0:T(8,128)(2,1)} %broadcast_in_dim.2), calls=%async_computation.1 | async-start | bytes 2097152 | tf_op jit(solution)/shard_map/all_to_all | solution.py:141
  116.7 0.7 slice.46.refs_0_
  117.4 0.7 slice.43.refs_7_
  118.1 0.7 slice.47.refs_1_
  118.8 0.7 slice.51.refs_6_
  119.5 0.7 slice.48.refs_2_
  120.2 0.7 slice.49.refs_3_
  120.9 0.7 slice.50.refs_4_
  121.6 16.7 %all-to-all-done.1.got_ref = bf16[8,256,256]{2,1,0:T(8,128)(2,1)S(1)} async-done(((bf16[8,256,256]{2,1,0:T(8,128)(2,1)}), bf16[8,256,256]{2,1,0:T(8,128)(2,1)S(1)}, u32[]{:S(2)}, u32[]{:S(2)}) %all-to-all-start.1) | async-done | bytes 1048608 | tf_op jit(solution)/shard_map/all_to_all | solution.py:141
  138.3 1.5 copy-done.1
  139.8 3.3 %shard_map.56 = bf16[512,896]{1,0:T(8,128)(2,1)S(1)} custom-call(s32[3]{0:T(128)S(1)} %pad_add_fusion.where_ref, bf16[448,2048]{1,0:T(8,128)(2,1)S(1)} %bitcast.19, bf16[448,2048]{1,0:T(8,128)(2,1)} %collective-permute-done.other_ref, bf16[8,256,256]{2,1,0:T(8,128)(2,1)S(1)} %all-to-all-done.1.got_ref, bf16[32,128]{1,0:T(8,128)(2,1)S(1)} %slice.46.refs_0_, ...), custom_call_target="tpu_custom_call" | custom-call | tf_op jit(solution)/shard_map/pallas_call | solution.py:147
  143.1 0.3 reshape.21
  143.5 37.5 %all_to_all.16 = bf16[256,2,896]{2,1,0:T(2,128)(2,1)S(1)} all-to-all(bf16[256,2,896]{2,1,0:T(2,128)(2,1)S(1)} %reshape.21), channel_id=1, replica_groups=mesh['side'=2,'grp'=8,'x'=4,'z'=8] {'x','z','grp'}, dimensions={0} | all-to-all | bytes 1835008 | tf_op jit(solution)/shard_map/all_to_all | solution.py:164
  181.0 0.8 reduce_sum.22
  181.8 0.1 reshape.25
  182.0 0.7 reshape.24
  (34 shorter events, 0.3 us)
Async XLA Ops:
  0.0 43.3 %copy-start = (bf16[1,2048,448]{1,2,0:T(8,128)(2,1)S(1)}, bf16[1,2048,448]{1,2,0:T(8,128)(2,1)}, u32[]{:S(2)}) copy-start(bf16[1,2048,448]{1,2,0:T(8,128)(2,1)} %param.9) | copy-start | bytes 5505028
  39.8 24.4 %copy-start.5 = (bf16[32,7296]{1,0:T(8,128)(2,1)}, bf16[32,7296]{1,0:T(8,128)(2,1)S(1)}, u32[]{:S(2)}) copy-start(bf16[32,7296]{1,0:T(8,128)(2,1)S(1)} %get-tuple-element.20) | copy-start | bytes 1400836
  39.8 10.4 %collective-permute-start.1 = (bf16[32,7296]{1,0:T(8,128)(2,1)S(1)}, bf16[32,7296]{1,0:T(8,128)(2,1)S(1)}, u32[]{:S(2)}, u32[]{:S(2)}) collective-permute-start(bf16[32,7296]{1,0:T(8,128)(2,1)S(1)} %get-tuple-element.20), channel_id=1, source_target_pairs={{0,32},{32,64},{64,96},{96,128},{128,160},{160,192},{192,224},{224... | collective-permute-start | bytes 1400840 | tf_op jit(solution)/shard_map/ppermute | solution.py:119
  43.3 78.3 %collective-permute-start = (bf16[448,2048]{1,0:T(8,128)(2,1)S(1)}, bf16[448,2048]{1,0:T(8,128)(2,1)}, u32[]{:S(2)}, u32[]{:S(2)}) collective-permute-start(bf16[448,2048]{1,0:T(8,128)(2,1)S(1)} %bitcast.18), channel_id=1, source_target_pairs={{0,256},{256,0},{1,257},{257,1},{2,258},{258,2},{3,259},{259,3},{4... | collective-permute-start | bytes 5505032 | tf_op jit(solution)/shard_map/ppermute | solution.py:36
  45.2 48.1 %copy-start.2 = (bf16[1,7168,128]{2,1,0:T(8,128)(2,1)S(1)}, bf16[1,7168,128]{2,1,0:T(8,128)(2,1)}, u32[]{:S(2)}) copy-start(bf16[1,7168,128]{2,1,0:T(8,128)(2,1)} %param.8) | copy-start | bytes 5505028
  45.2 16.2 %collective-permute-start.4 = (bf16[32,7296]{1,0:T(8,128)(2,1)S(1)}, bf16[32,7296]{1,0:T(8,128)(2,1)S(1)}, u32[]{:S(2)}, u32[]{:S(2)}) collective-permute-start(bf16[32,7296]{1,0:T(8,128)(2,1)S(1)} %get-tuple-element.20), channel_id=1, source_target_pairs={{0,224},{32,0},{64,32},{96,64},{128,96},{160,128},{192,160},{224,1... | collective-permute-start | bytes 1400840 | tf_op jit(solution)/shard_map/ppermute | solution.py:120
  50.2 43.3 %copy-start.6 = (bf16[32,7296]{1,0:T(8,128)(2,1)}, bf16[32,7296]{1,0:T(8,128)(2,1)S(1)}, u32[]{:S(2)}) copy-start(bf16[32,7296]{1,0:T(8,128)(2,1)S(1)} %collective-permute-done.1) | copy-start | bytes 1400836
  50.2 43.1 %collective-permute-start.6 = (bf16[7168,128]{1,0:T(8,128)(2,1)}, bf16[7168,128]{1,0:T(8,128)(2,1)S(1)}, u32[]{:S(2)}, u32[]{:S(2)}) collective-permute-start(bf16[7168,128]{1,0:T(8,128)(2,1)} %bitcast.21), channel_id=1, source_target_pairs={{0,256},{256,0},{1,257},{257,1},{2,258},{258,2},{3,259},{259,3},{4... | collective-permute-start | bytes 5505032 | tf_op jit(solution)/shard_map/ppermute | solution.py:36
  52.2 15.0 %collective-permute-start.2 = (bf16[32,7296]{1,0:T(8,128)(2,1)S(1)}, bf16[32,7296]{1,0:T(8,128)(2,1)S(1)}, u32[]{:S(2)}, u32[]{:S(2)}) collective-permute-start(bf16[32,7296]{1,0:T(8,128)(2,1)S(1)} %collective-permute-done.1), channel_id=1, source_target_pairs={{0,32},{32,64},{64,96},{96,128},{128,160},{160,192},{192,224},{224... | collective-permute-start | bytes 1400840 | tf_op jit(solution)/shard_map/ppermute | solution.py:119
  61.4 31.9 %copy-start.7 = (bf16[32,7296]{1,0:T(8,128)(2,1)}, bf16[32,7296]{1,0:T(8,128)(2,1)S(1)}, u32[]{:S(2)}) copy-start(bf16[32,7296]{1,0:T(8,128)(2,1)S(1)} %collective-permute-done.4) | copy-start | bytes 1400836
  61.4 15.4 %collective-permute-start.5 = (bf16[32,7296]{1,0:T(8,128)(2,1)S(1)}, bf16[32,7296]{1,0:T(8,128)(2,1)S(1)}, u32[]{:S(2)}, u32[]{:S(2)}) collective-permute-start(bf16[32,7296]{1,0:T(8,128)(2,1)S(1)} %collective-permute-done.4), channel_id=1, source_target_pairs={{0,224},{32,0},{64,32},{96,64},{128,96},{160,128},{192,160},{224,1... | collective-permute-start | bytes 1400840 | tf_op jit(solution)/shard_map/ppermute | solution.py:120
  67.1 26.4 %copy-start.8 = (bf16[32,7296]{1,0:T(8,128)(2,1)}, bf16[32,7296]{1,0:T(8,128)(2,1)S(1)}, u32[]{:S(2)}) copy-start(bf16[32,7296]{1,0:T(8,128)(2,1)S(1)} %collective-permute-done.2) | copy-start | bytes 1400836
  67.2 29.1 %collective-permute-start.3 = (bf16[32,7296]{1,0:T(8,128)(2,1)S(1)}, bf16[32,7296]{1,0:T(8,128)(2,1)S(1)}, u32[]{:S(2)}, u32[]{:S(2)}) collective-permute-start(bf16[32,7296]{1,0:T(8,128)(2,1)S(1)} %collective-permute-done.2), channel_id=1, source_target_pairs={{0,32},{32,64},{64,96},{96,128},{128,160},{160,192},{192,224},{224... | collective-permute-start | bytes 1400840 | tf_op jit(solution)/shard_map/ppermute | solution.py:119
  76.8 16.5 %copy-start.9 = (bf16[32,7296]{1,0:T(8,128)(2,1)}, bf16[32,7296]{1,0:T(8,128)(2,1)S(1)}, u32[]{:S(2)}) copy-start(bf16[32,7296]{1,0:T(8,128)(2,1)S(1)} %collective-permute-done.5) | copy-start | bytes 1400836
  76.8 14.5 %collective-permute-start.8 = (bf16[32,7296]{1,0:T(8,128)(2,1)S(1)}, bf16[32,7296]{1,0:T(8,128)(2,1)S(1)}, u32[]{:S(2)}, u32[]{:S(2)}) collective-permute-start(bf16[32,7296]{1,0:T(8,128)(2,1)S(1)} %collective-permute-done.5), channel_id=1, source_target_pairs={{0,224},{32,0},{64,32},{96,64},{128,96},{160,128},{192,160},{224,1... | collective-permute-start | bytes 1400840 | tf_op jit(solution)/shard_map/ppermute | solution.py:120
  91.3 9.8 %copy-start.3 = (bf16[32,7296]{1,0:T(8,128)(2,1)}, bf16[32,7296]{1,0:T(8,128)(2,1)S(1)}, u32[]{:S(2)}) copy-start(bf16[32,7296]{1,0:T(8,128)(2,1)S(1)} %collective-permute-done.8) | copy-start | bytes 1400836
  91.4 13.4 %collective-permute-start.9 = (bf16[16,7296]{1,0:T(8,128)(2,1)S(1)}, bf16[16,7296]{1,0:T(8,128)(2,1)S(1)}, u32[]{:S(2)}, u32[]{:S(2)}) collective-permute-start(bf16[16,7296]{1,0:T(8,128)(2,1)S(1)} %slice.45), channel_id=1, source_target_pairs={{0,224},{32,0},{64,32},{96,64},{128,96},{160,128},{192,160},{224,1... | collective-permute-start | bytes 700424 | tf_op jit(solution)/shard_map/ppermute | solution.py:134
  93.6 1.8 %copy-start.10 = (bf16[160,7296]{1,0:T(8,128)(2,1)S(1)}, bf16[160,7296]{1,0:T(8,128)(2,1)}, u32[]{:S(2)}) copy-start(bf16[160,7296]{1,0:T(8,128)(2,1)} %constant_dynamic-update-slice_fusion) | copy-start | bytes 7004164
  96.3 8.4 %collective-permute-start.7 = (bf16[16,7296]{1,0:T(8,128)(2,1)S(1)}, bf16[16,7296]{1,0:T(8,128)(2,1)S(1)}, u32[]{:S(2)}, u32[]{:S(2)}) collective-permute-start(bf16[16,7296]{1,0:T(8,128)(2,1)S(1)} %slice.34), channel_id=1, source_target_pairs={{0,32},{32,64},{64,96},{96,128},{128,160},{160,192},{192,224},{224... | collective-permute-start | bytes 700424 | tf_op jit(solution)/shard_map/ppermute | solution.py:134
  104.8 0.8 copy-start.4
  106.6 31.7 %all-to-all-start.1 = ((bf16[8,256,256]{2,1,0:T(8,128)(2,1)}), bf16[8,256,256]{2,1,0:T(8,128)(2,1)S(1)}, u32[]{:S(2)}, u32[]{:S(2)}) async-start(bf16[8,256,256]{2,1,0:T(8,128)(2,1)} %broadcast_in_dim.2), calls=%async_computation.1 | async-start | bytes 2097152 | tf_op jit(solution)/shard_map/all_to_all | solution.py:141
  138.3 1.5 copy-start.1

commit v6 on v5

--- a/solution.py
+++ b/solution.py
@@ -27,9 +27,9 @@
         tail = jnp.where(lane == k, ids[:, k : k + 1], tail)
         tail = jnp.where(lane == SHIFT + k, weights[:, k : k + 1], tail)
     tail = tail.astype(jnp.bfloat16)
-    for z in range(out_ref.shape[0]):
-        out_ref[z, :, :width] = normed
-        out_ref[z, :, width:] = tail
+    for d in range(out_ref.shape[0]):
+        out_ref[d, :, :width] = normed
+        out_ref[d, :, width:] = tail
 
 
 def from_other_core(own):
@@ -92,12 +92,12 @@
     vmem, smem = pl.BlockSpec(memory_space=pltpu.VMEM), pl.BlockSpec(memory_space=pltpu.SMEM)
     copies = pl.pallas_call(
         functools.partial(send_kernel, rows),
-        out_shape=jax.ShapeDtypeStruct((n_z, rows, width + TAIL), bf16),
+        out_shape=jax.ShapeDtypeStruct((n_dev, rows, width + TAIL), bf16),
         in_specs=[smem, vmem, vmem, vmem],
         out_specs=vmem,
     )(dev.reshape(1).astype(i32), tokens, expert_ids, route_weights)
-    by_z = lax.all_to_all(copies, "z", split_axis=0, concat_axis=0, tiled=True).reshape(n_z * rows, -1)
-    packed = lax.all_gather(by_z, "x", axis=0, tiled=True)
+    packed = lax.all_to_all(copies, ("x", "z"), split_axis=0, concat_axis=0, tiled=True)
+    packed = packed.reshape(n_dev * rows, -1)
 
     group = n_dev * rows
     hit = jnp.any(packed[:, width : width + TOPK].astype(i32) == dev, axis=1)
@@ -105,6 +105,10 @@
     slot = jnp.sum((before & hit[:, None]).astype(i32), axis=0)
     placed = (slot[None, :] == jnp.arange(CAP, dtype=i32)[:, None]) & hit[None, :]
     slot_input = jnp.dot(placed.astype(bf16), packed, preferred_element_type=f32).astype(bf16)
+
+    other_gate = from_other_core(own_gate)
+    both = [jnp.where(side == 0, own_gate, other_gate), jnp.where(side == 0, other_gate, own_gate)]
+    gate_slab = jnp.pad(jnp.concatenate(both, axis=1), ((0, TAIL), (0, 0)))
 
     def silu_gate(parts):
         block = jnp.concatenate(parts, axis=0)
@@ -114,30 +118,19 @@
     down = [(i, (i - 1) % n_grp) for i in range(n_grp)]
     half, far = CAP // 2, n_grp // 2
     below = above = slot_input
-    blocks, order, waiting, hidden = {0: slot_input}, [0], [slot_input], []
+    blocks, order, waiting = {0: slot_input}, [0], [slot_input]
     for step in range(1, far):
         below = lax.ppermute(below, "grp", up)
         above = lax.ppermute(above, "grp", down)
-        if step == 1:
-            below, own_gate = lax.optimization_barrier((below, own_gate))
-            other_gate = from_other_core(own_gate)
-            both = [jnp.where(side == 0, own_gate, other_gate), jnp.where(side == 0, other_gate, own_gate)]
-            gate_slab = jnp.pad(jnp.concatenate(both, axis=1), ((0, TAIL), (0, 0)))
-        if step == far - 1:
-            product = silu_gate(waiting)
-            below, product = lax.optimization_barrier((below, product))
-            hidden.append(product)
-            waiting = []
         blocks[n_grp - step], blocks[step] = below, above
         order += [n_grp - step, step]
         waiting += [below, above]
     below, above = lax.ppermute(below[:half], "grp", up), lax.ppermute(above[half:], "grp", down)
     product = silu_gate(waiting)
-    below, product = lax.optimization_barrier((below, product))
+    below, above, product = lax.optimization_barrier((below, above, product))
     blocks[far] = jnp.concatenate([below, above], axis=0)
     order.append(far)
-    hidden += [product, silu_gate([blocks[far]])]
-    hidden = jnp.concatenate(hidden, axis=0)
+    hidden = jnp.concatenate([product, silu_gate([blocks[far]])], axis=0)
     got = lax.all_to_all(
         jnp.broadcast_to(hidden[None], (n_grp,) + hidden.shape), "grp", split_axis=0, concat_axis=0, tiled=True
     )

time: 184 us -> 176 us (0.957)
  blocking collectives: 74.2 us -> 46.8 us
  waiting for transfers between devices: 45.3 us -> 57 us
  starting transfers between devices: 39.1 us -> 46.9 us
  local copies, waits for them, and re-layouts: 12 us -> 14.2 us
    all_to_all x0 -> x1, waiting for transfers between devices: none -> 22 us  [on_device(): lax.all_to_all(copies, ('x', 'z'), split_axis=0, concat_axis=0, tiled=True)]
    all_to_all x1 -> x0, blocking collectives: 21.6 us -> none  [on_device(): lax.all_to_all(copies, 'z', split_axis=0, concat_axis=0, tiled=True)]
    ppermute x3, waiting for transfers between devices: 20.3 us -> 1.23 us  [on_device(): above = lax.ppermute(above, 'grp', down)]
    all_gather x1 -> x0, blocking collectives: 15.1 us -> none  [on_device(): packed = lax.all_gather(by_z, 'x', axis=0, tiled=True)]
    all_to_all x0 -> x1, starting transfers between devices: none -> 13.3 us  [on_device(): lax.all_to_all(copies, ('x', 'z'), split_axis=0, concat_axis=0, tiled=True)]
    ppermute x3, waiting for transfers between devices: 5.52 us -> 17.1 us  [on_device(): below = lax.ppermute(below, 'grp', up)]
    all_to_all x1, blocking collectives: 37.5 us -> 46.8 us  [on_device(): lax.all_to_all(weighted.reshape(n_dev * n_grp, rows, -1), ('x', 'z', 'grp...]
    all_to_all x1, waiting for transfers between devices: 16.7 us -> 10.3 us  [on_device(): lax.all_to_all(jnp.broadcast_to(hidden[None], (n_grp,) + hidden.shape), '...]
  transfers between devices with their start and end apart: 11 -> 12, of which waited for: 7 -> 10; matrix products, arithmetic and copies ran while one was open for 8% -> 8% of each run, Pallas kernels for 0% -> 0%
where the time goes in v6:
time: 176 us; the launch traced here: 175 us
  waiting for transfers between devices  57 us (32%)
  starting transfers between devices  46.9 us (27%)
  blocking collectives  46.8 us (27%)
  local copies, waits for them, and re-layouts  14.2 us (8%)
  Pallas kernels  4.26 us (2%)
  other arithmetic  3.41 us (2%)
  matrix products  2.15 us (1%)
    all_to_all x1, blocking collectives, on_device(): lax.all_to_all(weighted.reshape(n_dev * n_grp, rows, -1), ('x', 'z', 'grp...  46.8 us
    all_to_all x1, waiting for transfers between devices, on_device(): lax.all_to_all(copies, ('x', 'z'), split_axis=0, concat_axis=0, tiled=True)  22 us
    ppermute x3, waiting for transfers between devices, on_device(): below = lax.ppermute(below, 'grp', up)  17.1 us
    all_to_all x1, starting transfers between devices, on_device(): lax.all_to_all(copies, ('x', 'z'), split_axis=0, concat_axis=0, tiled=True)  13.3 us
    all_to_all x1, waiting for transfers between devices, on_device(): lax.all_to_all(jnp.broadcast_to(hidden[None], (n_grp,) + hidden.shape), '...  10.3 us
    ppermute x3, starting transfers between devices, on_device(): below = lax.ppermute(below, 'grp', up)  9.06 us
    ppermute x3, starting transfers between devices, on_device(): above = lax.ppermute(above, 'grp', down)  7.84 us
    all_to_all x1, starting transfers between devices, on_device(): lax.all_to_all(jnp.broadcast_to(hidden[None], (n_grp,) + hidden.shape), '...  6.86 us
  transfers between devices with their start and end apart: 12, of which 10 were waited for; matrix products, arithmetic and copies ran while one was open for 8% of the time, Pallas kernels for 0%

profile of v6, /device:TPU:16, one launch (start us, length us, event | category | flops | bytes accessed | tf_op | source)
XLA Modules:
  0.0 175.0 jit_solution(8362264460941458464)
XLA Ops:
  0.0 1.9 %shard_map.55 = bf16[32,2,7296]{2,1,0:T(2,128)(2,1)} custom-call(s32[1]{0:T(128)} %bitcast.1.dev_ref, bf16[2,7168]{1,0:T(2,128)(2,1)} %tokens_ref.1, s32[2,8]{1,0:T(2,128)} %ids_ref.1, bf16[2,8]{1,0:T(2,128)(2,1)} %weights_ref.1), custom_call_target="tpu_custom_call" | custom-call | tf_op jit(solution)/shard_map/pallas_call | solution.py:93
  1.9 13.3 %all-to-all-start = ((bf16[32,2,7296]{2,1,0:T(2,128)(2,1)}), bf16[32,2,7296]{2,1,0:T(2,128)(2,1)}, u32[]{:S(2)}, u32[]{:S(2)}) async-start(bf16[32,2,7296]{2,1,0:T(2,128)(2,1)} %shard_map.55), calls=%async_computation | async-start | bytes 1867776 | tf_op jit(solution)/shard_map/all_to_all | solution.py:99
  15.2 1.9 %collective-permute-start.9 = (bf16[7168,128]{1,0:T(8,128)(2,1)}, bf16[7168,128]{1,0:T(8,128)(2,1)}, u32[]{:S(2)}, u32[]{:S(2)}) collective-permute-start(bf16[7168,128]{1,0:T(8,128)(2,1)} %bitcast.20), channel_id=1, source_target_pairs={{0,256},{256,0},{1,257},{257,1},{2,258},{258,2},{3,259},{259,3},{4... | collective-permute-start | bytes 5505032 | tf_op jit(solution)/shard_map/ppermute | solution.py:36
  17.1 2.4 %collective-permute-start = (bf16[448,2048]{1,0:T(8,128)(2,1)}, bf16[448,2048]{1,0:T(8,128)(2,1)S(1)}, u32[]{:S(2)}, u32[]{:S(2)}) collective-permute-start(bf16[448,2048]{1,0:T(8,128)(2,1)} %bitcast.17), channel_id=1, source_target_pairs={{0,256},{256,0},{1,257},{257,1},{2,258},{258,2},{3,259},{259,3},{4... | collective-permute-start | bytes 5505032 | tf_op jit(solution)/shard_map/ppermute | solution.py:36
  19.6 22.0 %all-to-all-done = bf16[32,2,7296]{2,1,0:T(2,128)(2,1)} async-done(((bf16[32,2,7296]{2,1,0:T(2,128)(2,1)}), bf16[32,2,7296]{2,1,0:T(2,128)(2,1)}, u32[]{:S(2)}, u32[]{:S(2)}) %all-to-all-start) | async-done | bytes 933920 | tf_op jit(solution)/shard_map/all_to_all | solution.py:99
  41.6 2.5 %reshape.20 = bf16[64,7296]{1,0:T(8,128)(2,1)S(1)} reshape(bf16[32,2,7296]{2,1,0:T(2,128)(2,1)} %all-to-all-done) | data formatting | bytes 1867776 | tf_op jit(solution)/shard_map/reshape | solution.py:100
  44.1 0.1 fusion.12
  44.2 0.1 convert_reduce_fusion
  44.3 0.3 constant_dynamic-update-slice_fusion.6
  44.6 3.5 %collective-permute-start.1 = (bf16[32,7296]{1,0:T(8,128)(2,1)S(1)}, bf16[32,7296]{1,0:T(8,128)(2,1)S(1)}, u32[]{:S(2)}, u32[]{:S(2)}) collective-permute-start(bf16[32,7296]{1,0:T(8,128)(2,1)S(1)} %get-tuple-element.14), channel_id=1, source_target_pairs={{0,32},{32,64},{64,96},{96,128},{128,160},{160,192},{192,224},{224... | collective-permute-start | bytes 1400840 | tf_op jit(solution)/shard_map/ppermute | solution.py:123
  48.1 2.4 %collective-permute-start.5 = (bf16[32,7296]{1,0:T(8,128)(2,1)S(1)}, bf16[32,7296]{1,0:T(8,128)(2,1)S(1)}, u32[]{:S(2)}, u32[]{:S(2)}) collective-permute-start(bf16[32,7296]{1,0:T(8,128)(2,1)S(1)} %get-tuple-element.14), channel_id=1, source_target_pairs={{0,224},{32,0},{64,32},{96,64},{128,96},{160,128},{192,160},{224,1... | collective-permute-start | bytes 1400840 | tf_op jit(solution)/shard_map/ppermute | solution.py:124
  50.5 2.3 %broadcast_select_fusion.1 = (bf16[7168,128]{1,0:T(8,128)(2,1)S(1)}, bf16[7168,128]{1,0:T(8,128)(2,1)S(1)}) fusion(bf16[7168,128]{1,0:T(8,128)(2,1)} %collective-permute-done.9, pred[]{:T(512)S(6)} %eq.28, bf16[1,7168,128]{2,1,0:T(8,128)(2,1)} %param.8), kind=kLoop, calls=%fused_computation.6 | loop fusion | flops 1835008 | bytes 7340033 | tf_op jit(solution)/shard_map/jit(_where)/select_n | solution.py:110
  52.8 3.4 %collective-permute-done.1 = bf16[32,7296]{1,0:T(8,128)(2,1)S(1)} collective-permute-done((bf16[32,7296]{1,0:T(8,128)(2,1)S(1)}, bf16[32,7296]{1,0:T(8,128)(2,1)S(1)}, u32[]{:S(2)}, u32[]{:S(2)}) %collective-permute-start.1) | collective-permute-done | bytes 466976 | tf_op jit(solution)/shard_map/ppermute | solution.py:123
  56.2 2.9 %collective-permute-start.2 = (bf16[32,7296]{1,0:T(8,128)(2,1)S(1)}, bf16[32,7296]{1,0:T(8,128)(2,1)S(1)}, u32[]{:S(2)}, u32[]{:S(2)}) collective-permute-start(bf16[32,7296]{1,0:T(8,128)(2,1)S(1)} %collective-permute-done.1), channel_id=1, source_target_pairs={{0,32},{32,64},{64,96},{96,128},{128,160},{160,192},{192,224},{224... | collective-permute-start | bytes 1400840 | tf_op jit(solution)/shard_map/ppermute | solution.py:123
  59.1 0.2 collective-permute-done.5
  59.3 2.8 %collective-permute-start.6 = (bf16[32,7296]{1,0:T(8,128)(2,1)S(1)}, bf16[32,7296]{1,0:T(8,128)(2,1)S(1)}, u32[]{:S(2)}, u32[]{:S(2)}) collective-permute-start(bf16[32,7296]{1,0:T(8,128)(2,1)S(1)} %collective-permute-done.5), channel_id=1, source_target_pairs={{0,224},{32,0},{64,32},{96,64},{128,96},{160,128},{192,160},{224,1... | collective-permute-start | bytes 1400840 | tf_op jit(solution)/shard_map/ppermute | solution.py:124
  62.2 6.7 %collective-permute-done.2 = bf16[32,7296]{1,0:T(8,128)(2,1)S(1)} collective-permute-done((bf16[32,7296]{1,0:T(8,128)(2,1)S(1)}, bf16[32,7296]{1,0:T(8,128)(2,1)S(1)}, u32[]{:S(2)}, u32[]{:S(2)}) %collective-permute-start.2) | collective-permute-done | bytes 466976 | tf_op jit(solution)/shard_map/ppermute | solution.py:123
  68.9 2.7 %collective-permute-start.3 = (bf16[32,7296]{1,0:T(8,128)(2,1)S(1)}, bf16[32,7296]{1,0:T(8,128)(2,1)S(1)}, u32[]{:S(2)}, u32[]{:S(2)}) collective-permute-start(bf16[32,7296]{1,0:T(8,128)(2,1)S(1)} %collective-permute-done.2), channel_id=1, source_target_pairs={{0,32},{32,64},{64,96},{96,128},{128,160},{160,192},{192,224},{224... | collective-permute-start | bytes 1400840 | tf_op jit(solution)/shard_map/ppermute | solution.py:123
  71.6 0.4 collective-permute-done.6
  72.1 2.7 %collective-permute-start.7 = (bf16[32,7296]{1,0:T(8,128)(2,1)S(1)}, bf16[32,7296]{1,0:T(8,128)(2,1)S(1)}, u32[]{:S(2)}, u32[]{:S(2)}) collective-permute-start(bf16[32,7296]{1,0:T(8,128)(2,1)S(1)} %collective-permute-done.6), channel_id=1, source_target_pairs={{0,224},{32,0},{64,32},{96,64},{128,96},{160,128},{192,160},{224,1... | collective-permute-start | bytes 1400840 | tf_op jit(solution)/shard_map/ppermute | solution.py:124
  74.8 7.0 %collective-permute-done.3 = bf16[32,7296]{1,0:T(8,128)(2,1)S(1)} collective-permute-done((bf16[32,7296]{1,0:T(8,128)(2,1)S(1)}, bf16[32,7296]{1,0:T(8,128)(2,1)S(1)}, u32[]{:S(2)}, u32[]{:S(2)}) %collective-permute-start.3) | collective-permute-done | bytes 466976 | tf_op jit(solution)/shard_map/ppermute | solution.py:123
  81.8 3.6 %collective-permute-start.4 = (bf16[16,7296]{1,0:T(8,128)(2,1)S(1)}, bf16[16,7296]{1,0:T(8,128)(2,1)S(1)}, u32[]{:S(2)}, u32[]{:S(2)}) collective-permute-start(bf16[16,7296]{1,0:T(8,128)(2,1)S(1)} %slice.45), channel_id=1, source_target_pairs={{0,32},{32,64},{64,96},{96,128},{128,160},{160,192},{192,224},{224... | collective-permute-start | bytes 700424 | tf_op jit(solution)/shard_map/ppermute | solution.py:128
  85.4 0.6 collective-permute-done.7
  86.0 1.9 %collective-permute-start.8 = (bf16[16,7296]{1,0:T(8,128)(2,1)S(1)}, bf16[16,7296]{1,0:T(8,128)(2,1)S(1)}, u32[]{:S(2)}, u32[]{:S(2)}) collective-permute-start(bf16[16,7296]{1,0:T(8,128)(2,1)S(1)} %slice.46), channel_id=1, source_target_pairs={{0,224},{32,0},{64,32},{96,64},{128,96},{160,128},{192,160},{224,1... | collective-permute-start | bytes 700424 | tf_op jit(solution)/shard_map/ppermute | solution.py:128
  88.1 1.1 multiply_convert_fusion
  89.2 0.6 collective-permute-done.4
  89.8 5.7 %collective-permute-done.8 = bf16[16,7296]{1,0:T(8,128)(2,1)S(1)} collective-permute-done((bf16[16,7296]{1,0:T(8,128)(2,1)S(1)}, bf16[16,7296]{1,0:T(8,128)(2,1)S(1)}, u32[]{:S(2)}, u32[]{:S(2)}) %collective-permute-start.8) | collective-permute-done | bytes 233504 | tf_op jit(solution)/shard_map/ppermute | solution.py:128
  95.5 0.8 multiply_convert_fusion.1
  96.3 1.1 broadcast_in_dim.2
  97.4 6.9 %all-to-all-start.1 = ((bf16[8,256,256]{2,1,0:T(8,128)(2,1)}), bf16[8,256,256]{2,1,0:T(8,128)(2,1)S(1)}, u32[]{:S(2)}, u32[]{:S(2)}) async-start(bf16[8,256,256]{2,1,0:T(8,128)(2,1)} %broadcast_in_dim.2), calls=%async_computation.1 | async-start | bytes 2097152 | tf_op jit(solution)/shard_map/all_to_all | solution.py:134
  104.2 0.1 pad_add_fusion.where_ref
  104.3 0.7 slice.47.refs_0_
  105.0 0.7 slice.48.refs_1_
  105.7 0.7 slice.54.refs_7_
  106.4 0.7 slice.49.refs_2_
  107.1 0.7 slice.53.refs_6_
  107.8 0.7 slice.50.refs_3_
  108.5 0.7 slice.51.refs_4_
  109.2 1.2 copy-done.1
  110.4 10.3 %all-to-all-done.1.got_ref = bf16[8,256,256]{2,1,0:T(8,128)(2,1)S(1)} async-done(((bf16[8,256,256]{2,1,0:T(8,128)(2,1)}), bf16[8,256,256]{2,1,0:T(8,128)(2,1)S(1)}, u32[]{:S(2)}, u32[]{:S(2)}) %all-to-all-start.1) | async-done | bytes 1048608 | tf_op jit(solution)/shard_map/all_to_all | solution.py:134
  120.8 1.5 copy-done
  122.3 1.5 copy-done.2
  123.8 2.3 %shard_map.56 = bf16[512,896]{1,0:T(8,128)(2,1)S(1)} custom-call(s32[3]{0:T(128)S(1)} %pad_add_fusion.where_ref, bf16[448,2048]{1,0:T(8,128)(2,1)S(1)} %bitcast.18, bf16[448,2048]{1,0:T(8,128)(2,1)S(1)} %copy-done.2, bf16[8,256,256]{2,1,0:T(8,128)(2,1)S(1)} %all-to-all-done.1.got_ref, bf16[32,128]{1,0:T(8,128)(2,1)S(1)} %slice.47.refs_0_, ...), custom_call_target="tpu_custom_call" | custom-call | tf_op jit(solution)/shard_map/pallas_call | solution.py:140
  126.1 0.3 reshape.21
  126.5 46.8 %all_to_all.15 = bf16[256,2,896]{2,1,0:T(2,128)(2,1)S(1)} all-to-all(bf16[256,2,896]{2,1,0:T(2,128)(2,1)S(1)} %reshape.21), channel_id=1, replica_groups=mesh['side'=2,'grp'=8,'x'=4,'z'=8] {'x','z','grp'}, dimensions={0} | all-to-all | bytes 1835008 | tf_op jit(solution)/shard_map/all_to_all | solution.py:157
  173.3 0.8 reduce_sum.22
  174.1 0.1 reshape.25
  174.3 0.7 reshape.24
  (32 shorter events, 0.4 us)
Async XLA Ops:
  1.9 39.7 %all-to-all-start = ((bf16[32,2,7296]{2,1,0:T(2,128)(2,1)}), bf16[32,2,7296]{2,1,0:T(2,128)(2,1)}, u32[]{:S(2)}, u32[]{:S(2)}) async-start(bf16[32,2,7296]{2,1,0:T(2,128)(2,1)} %shard_map.55), calls=%async_computation | async-start | bytes 1867776 | tf_op jit(solution)/shard_map/all_to_all | solution.py:99
  15.2 35.2 %collective-permute-start.9 = (bf16[7168,128]{1,0:T(8,128)(2,1)}, bf16[7168,128]{1,0:T(8,128)(2,1)}, u32[]{:S(2)}, u32[]{:S(2)}) collective-permute-start(bf16[7168,128]{1,0:T(8,128)(2,1)} %bitcast.20), channel_id=1, source_target_pairs={{0,256},{256,0},{1,257},{257,1},{2,258},{258,2},{3,259},{259,3},{4... | collective-permute-start | bytes 5505032 | tf_op jit(solution)/shard_map/ppermute | solution.py:36
  17.1 92.1 %collective-permute-start = (bf16[448,2048]{1,0:T(8,128)(2,1)}, bf16[448,2048]{1,0:T(8,128)(2,1)S(1)}, u32[]{:S(2)}, u32[]{:S(2)}) collective-permute-start(bf16[448,2048]{1,0:T(8,128)(2,1)} %bitcast.17), channel_id=1, source_target_pairs={{0,256},{256,0},{1,257},{257,1},{2,258},{258,2},{3,259},{259,3},{4... | collective-permute-start | bytes 5505032 | tf_op jit(solution)/shard_map/ppermute | solution.py:36
  44.6 8.2 %copy-start.4 = (bf16[32,7296]{1,0:T(8,128)(2,1)}, bf16[32,7296]{1,0:T(8,128)(2,1)S(1)}, u32[]{:S(2)}) copy-start(bf16[32,7296]{1,0:T(8,128)(2,1)S(1)} %get-tuple-element.14) | copy-start | bytes 1400836
  44.6 11.6 %collective-permute-start.1 = (bf16[32,7296]{1,0:T(8,128)(2,1)S(1)}, bf16[32,7296]{1,0:T(8,128)(2,1)S(1)}, u32[]{:S(2)}, u32[]{:S(2)}) collective-permute-start(bf16[32,7296]{1,0:T(8,128)(2,1)S(1)} %get-tuple-element.14), channel_id=1, source_target_pairs={{0,32},{32,64},{64,96},{96,128},{128,160},{160,192},{192,224},{224... | collective-permute-start | bytes 1400840 | tf_op jit(solution)/shard_map/ppermute | solution.py:123
  48.1 11.2 %collective-permute-start.5 = (bf16[32,7296]{1,0:T(8,128)(2,1)S(1)}, bf16[32,7296]{1,0:T(8,128)(2,1)S(1)}, u32[]{:S(2)}, u32[]{:S(2)}) collective-permute-start(bf16[32,7296]{1,0:T(8,128)(2,1)S(1)} %get-tuple-element.14), channel_id=1, source_target_pairs={{0,224},{32,0},{64,32},{96,64},{128,96},{160,128},{192,160},{224,1... | collective-permute-start | bytes 1400840 | tf_op jit(solution)/shard_map/ppermute | solution.py:124
  56.2 31.9 %copy-start.5 = (bf16[32,7296]{1,0:T(8,128)(2,1)}, bf16[32,7296]{1,0:T(8,128)(2,1)S(1)}, u32[]{:S(2)}) copy-start(bf16[32,7296]{1,0:T(8,128)(2,1)S(1)} %collective-permute-done.1) | copy-start | bytes 1400836
  56.2 12.7 %collective-permute-start.2 = (bf16[32,7296]{1,0:T(8,128)(2,1)S(1)}, bf16[32,7296]{1,0:T(8,128)(2,1)S(1)}, u32[]{:S(2)}, u32[]{:S(2)}) collective-permute-start(bf16[32,7296]{1,0:T(8,128)(2,1)S(1)} %collective-permute-done.1), channel_id=1, source_target_pairs={{0,32},{32,64},{64,96},{96,128},{128,160},{160,192},{192,224},{224... | collective-permute-start | bytes 1400840 | tf_op jit(solution)/shard_map/ppermute | solution.py:123
  59.3 29.9 %copy-start.6 = (bf16[32,7296]{1,0:T(8,128)(2,1)}, bf16[32,7296]{1,0:T(8,128)(2,1)S(1)}, u32[]{:S(2)}) copy-start(bf16[32,7296]{1,0:T(8,128)(2,1)S(1)} %collective-permute-done.5) | copy-start | bytes 1400836
  59.3 12.7 %collective-permute-start.6 = (bf16[32,7296]{1,0:T(8,128)(2,1)S(1)}, bf16[32,7296]{1,0:T(8,128)(2,1)S(1)}, u32[]{:S(2)}, u32[]{:S(2)}) collective-permute-start(bf16[32,7296]{1,0:T(8,128)(2,1)S(1)} %collective-permute-done.5), channel_id=1, source_target_pairs={{0,224},{32,0},{64,32},{96,64},{128,96},{160,128},{192,160},{224,1... | collective-permute-start | bytes 1400840 | tf_op jit(solution)/shard_map/ppermute | solution.py:124
  68.9 19.2 %copy-start.7 = (bf16[32,7296]{1,0:T(8,128)(2,1)}, bf16[32,7296]{1,0:T(8,128)(2,1)S(1)}, u32[]{:S(2)}) copy-start(bf16[32,7296]{1,0:T(8,128)(2,1)S(1)} %collective-permute-done.2) | copy-start | bytes 1400836
  68.9 13.0 %collective-permute-start.3 = (bf16[32,7296]{1,0:T(8,128)(2,1)S(1)}, bf16[32,7296]{1,0:T(8,128)(2,1)S(1)}, u32[]{:S(2)}, u32[]{:S(2)}) collective-permute-start(bf16[32,7296]{1,0:T(8,128)(2,1)S(1)} %collective-permute-done.2), channel_id=1, source_target_pairs={{0,32},{32,64},{64,96},{96,128},{128,160},{160,192},{192,224},{224... | collective-permute-start | bytes 1400840 | tf_op jit(solution)/shard_map/ppermute | solution.py:123
  72.1 17.1 %copy-start.8 = (bf16[32,7296]{1,0:T(8,128)(2,1)}, bf16[32,7296]{1,0:T(8,128)(2,1)S(1)}, u32[]{:S(2)}) copy-start(bf16[32,7296]{1,0:T(8,128)(2,1)S(1)} %collective-permute-done.6) | copy-start | bytes 1400836
  72.1 13.9 %collective-permute-start.7 = (bf16[32,7296]{1,0:T(8,128)(2,1)S(1)}, bf16[32,7296]{1,0:T(8,128)(2,1)S(1)}, u32[]{:S(2)}, u32[]{:S(2)}) collective-permute-start(bf16[32,7296]{1,0:T(8,128)(2,1)S(1)} %collective-permute-done.6), channel_id=1, source_target_pairs={{0,224},{32,0},{64,32},{96,64},{128,96},{160,128},{192,160},{224,1... | collective-permute-start | bytes 1400840 | tf_op jit(solution)/shard_map/ppermute | solution.py:124
  81.8 8.0 %collective-permute-start.4 = (bf16[16,7296]{1,0:T(8,128)(2,1)S(1)}, bf16[16,7296]{1,0:T(8,128)(2,1)S(1)}, u32[]{:S(2)}, u32[]{:S(2)}) collective-permute-start(bf16[16,7296]{1,0:T(8,128)(2,1)S(1)} %slice.45), channel_id=1, source_target_pairs={{0,32},{32,64},{64,96},{96,128},{128,160},{160,192},{192,224},{224... | collective-permute-start | bytes 700424 | tf_op jit(solution)/shard_map/ppermute | solution.py:128
  86.0 2.0 %copy-start.3 = (bf16[32,7296]{1,0:T(8,128)(2,1)}, bf16[32,7296]{1,0:T(8,128)(2,1)S(1)}, u32[]{:S(2)}) copy-start(bf16[32,7296]{1,0:T(8,128)(2,1)S(1)} %collective-permute-done.7) | copy-start | bytes 1400836
  86.0 9.4 %collective-permute-start.8 = (bf16[16,7296]{1,0:T(8,128)(2,1)S(1)}, bf16[16,7296]{1,0:T(8,128)(2,1)S(1)}, u32[]{:S(2)}, u32[]{:S(2)}) collective-permute-start(bf16[16,7296]{1,0:T(8,128)(2,1)S(1)} %slice.46), channel_id=1, source_target_pairs={{0,224},{32,0},{64,32},{96,64},{128,96},{160,128},{192,160},{224,1... | collective-permute-start | bytes 700424 | tf_op jit(solution)/shard_map/ppermute | solution.py:128
  95.5 0.8 copy-start.9
  97.4 23.4 %all-to-all-start.1 = ((bf16[8,256,256]{2,1,0:T(8,128)(2,1)}), bf16[8,256,256]{2,1,0:T(8,128)(2,1)S(1)}, u32[]{:S(2)}, u32[]{:S(2)}) async-start(bf16[8,256,256]{2,1,0:T(8,128)(2,1)} %broadcast_in_dim.2), calls=%async_computation.1 | async-start | bytes 2097152 | tf_op jit(solution)/shard_map/all_to_all | solution.py:134
  109.2 1.2 copy-start.1
  120.8 1.5 copy-start
  122.3 1.5 copy-start.2

commit v7 on v6

--- a/solution.py
+++ b/solution.py
@@ -154,10 +154,14 @@
         got,
         *[blocks[d][:, width:] for d in range(n_grp)],
     )
+    over_x = lax.all_to_all(
+        weighted.reshape(n_x, n_z * n_grp * rows, -1), "x", split_axis=0, concat_axis=0, tiled=True
+    )
+    total_x = jnp.sum(over_x.astype(f32), axis=0).astype(bf16)
     parts = lax.all_to_all(
-        weighted.reshape(n_dev * n_grp, rows, -1), ("x", "z", "grp"), split_axis=0, concat_axis=0, tiled=True
+        total_x.reshape(n_z * n_grp, rows, -1), ("z", "grp"), split_axis=0, concat_axis=0, tiled=True
     )
-    total = jnp.sum(parts.reshape(n_dev, n_grp, rows, -1).astype(f32), axis=0).astype(bf16)
+    total = jnp.sum(parts.reshape(n_z, n_grp, rows, -1).astype(f32), axis=0).astype(bf16)
     mixed = total.reshape(n_grp, rows, n_side, -1).transpose(1, 2, 0, 3)
     return mixed.reshape(rows, width)
 

time: 176 us -> 167 us (0.949)
  the two profiles are of different devices: /device:TPU:16 before, /device:TPU:8 now
where the time goes in v7:
time: 167 us; the launch traced here: 166 us
  waiting for transfers between devices  54.6 us (33%)
  starting transfers between devices  50.9 us (30%)
  blocking collectives  42.5 us (25%)
  local copies, waits for them, and re-layouts  7.57 us (5%)
  Pallas kernels  5.2 us (3%)
  other arithmetic  2.94 us (2%)
  matrix products  2.16 us (1%)
    all_to_all x1, blocking collectives, on_device(): lax.all_to_all(total_x.reshape(n_z * n_grp, rows, -1), ('z', 'grp'), spli...  29.9 us
    all_to_all x1, waiting for transfers between devices, on_device(): lax.all_to_all(copies, ('x', 'z'), split_axis=0, concat_axis=0, tiled=True)  22 us
    ppermute x3, waiting for transfers between devices, on_device(): below = lax.ppermute(below, 'grp', up)  15.6 us
    all_to_all x1, starting transfers between devices, on_device(): lax.all_to_all(copies, ('x', 'z'), split_axis=0, concat_axis=0, tiled=True)  13.2 us
    all_to_all x1, blocking collectives, on_device(): lax.all_to_all(weighted.reshape(n_x, n_z * n_grp * rows, -1), 'x', split_...  12.6 us
    all_to_all x1, waiting for transfers between devices, on_device(): lax.all_to_all(jnp.broadcast_to(hidden[None], (n_grp,) + hidden.shape), '...  12 us
    ppermute x3, starting transfers between devices, on_device(): below = lax.ppermute(below, 'grp', up)  11.8 us
    all_to_all x1, starting transfers between devices, on_device(): lax.all_to_all(jnp.broadcast_to(hidden[None], (n_grp,) + hidden.shape), '...  8.9 us
  transfers between devices with their start and end apart: 12, of which 7 were waited for; matrix products, arithmetic and copies ran while one was open for 7% of the time, Pallas kernels for 0%

profile of v7, /device:TPU:8, one launch (start us, length us, event | category | flops | bytes accessed | tf_op | source)
XLA Modules:
  0.0 166.2 jit_solution(13916263962991456422)
XLA Ops:
  0.0 1.9 %shard_map.55 = bf16[32,2,7296]{2,1,0:T(2,128)(2,1)} custom-call(s32[1]{0:T(128)} %bitcast.1.dev_ref, bf16[2,7168]{1,0:T(2,128)(2,1)} %tokens_ref.1, s32[2,8]{1,0:T(2,128)} %ids_ref.1, bf16[2,8]{1,0:T(2,128)(2,1)} %weights_ref.1), custom_call_target="tpu_custom_call" | custom-call | tf_op jit(solution)/shard_map/pallas_call | solution.py:93
  1.9 13.2 %all-to-all-start = ((bf16[32,2,7296]{2,1,0:T(2,128)(2,1)}), bf16[32,2,7296]{2,1,0:T(2,128)(2,1)S(1)}, u32[]{:S(2)}, u32[]{:S(2)}) async-start(bf16[32,2,7296]{2,1,0:T(2,128)(2,1)} %shard_map.55), calls=%async_computation | async-start | bytes 1867776 | tf_op jit(solution)/shard_map/all_to_all | solution.py:99
  15.1 1.9 %collective-permute-start.9 = (bf16[7168,128]{1,0:T(8,128)(2,1)}, bf16[7168,128]{1,0:T(8,128)(2,1)}, u32[]{:S(2)}, u32[]{:S(2)}) collective-permute-start(bf16[7168,128]{1,0:T(8,128)(2,1)} %bitcast.21), channel_id=1, source_target_pairs={{0,256},{256,0},{1,257},{257,1},{2,258},{258,2},{3,259},{259,3},{4... | collective-permute-start | bytes 5505032 | tf_op jit(solution)/shard_map/ppermute | solution.py:36
  17.0 2.4 %collective-permute-start = (bf16[448,2048]{1,0:T(8,128)(2,1)}, bf16[448,2048]{1,0:T(8,128)(2,1)}, u32[]{:S(2)}, u32[]{:S(2)}) collective-permute-start(bf16[448,2048]{1,0:T(8,128)(2,1)} %bitcast.19), channel_id=1, source_target_pairs={{0,256},{256,0},{1,257},{257,1},{2,258},{258,2},{3,259},{259,3},{4... | collective-permute-start | bytes 5505032 | tf_op jit(solution)/shard_map/ppermute | solution.py:36
  19.5 22.0 %all-to-all-done = bf16[32,2,7296]{2,1,0:T(2,128)(2,1)S(1)} async-done(((bf16[32,2,7296]{2,1,0:T(2,128)(2,1)}), bf16[32,2,7296]{2,1,0:T(2,128)(2,1)S(1)}, u32[]{:S(2)}, u32[]{:S(2)}) %all-to-all-start) | async-done | bytes 933920 | tf_op jit(solution)/shard_map/all_to_all | solution.py:99
  41.5 0.4 reshape.23
  41.8 0.1 fusion.12
  42.0 0.1 convert_reduce_fusion
  42.1 0.3 constant_dynamic-update-slice_fusion.6
  42.4 3.5 %collective-permute-start.1 = (bf16[32,7296]{1,0:T(8,128)(2,1)S(1)}, bf16[32,7296]{1,0:T(8,128)(2,1)S(1)}, u32[]{:S(2)}, u32[]{:S(2)}) collective-permute-start(bf16[32,7296]{1,0:T(8,128)(2,1)S(1)} %get-tuple-element.14), channel_id=1, source_target_pairs={{0,32},{32,64},{64,96},{96,128},{128,160},{160,192},{192,224},{224... | collective-permute-start | bytes 1400840 | tf_op jit(solution)/shard_map/ppermute | solution.py:123
  45.8 2.4 %collective-permute-start.5 = (bf16[32,7296]{1,0:T(8,128)(2,1)S(1)}, bf16[32,7296]{1,0:T(8,128)(2,1)S(1)}, u32[]{:S(2)}, u32[]{:S(2)}) collective-permute-start(bf16[32,7296]{1,0:T(8,128)(2,1)S(1)} %get-tuple-element.14), channel_id=1, source_target_pairs={{0,224},{32,0},{64,32},{96,64},{128,96},{160,128},{192,160},{224,1... | collective-permute-start | bytes 1400840 | tf_op jit(solution)/shard_map/ppermute | solution.py:124
  48.2 0.0 collective-permute-done.9
  48.2 2.3 %broadcast_select_fusion.1 = (bf16[7168,128]{1,0:T(8,128)(2,1)S(1)}, bf16[7168,128]{1,0:T(8,128)(2,1)S(1)}) fusion(bf16[7168,128]{1,0:T(8,128)(2,1)} %collective-permute-done.9, pred[]{:T(512)S(6)} %eq.28, bf16[1,7168,128]{2,1,0:T(8,128)(2,1)} %param.8), kind=kLoop, calls=%fused_computation.6 | loop fusion | flops 1835008 | bytes 7340033 | tf_op jit(solution)/shard_map/jit(_where)/select_n | solution.py:110
  50.5 3.0 %collective-permute-done.1 = bf16[32,7296]{1,0:T(8,128)(2,1)S(1)} collective-permute-done((bf16[32,7296]{1,0:T(8,128)(2,1)S(1)}, bf16[32,7296]{1,0:T(8,128)(2,1)S(1)}, u32[]{:S(2)}, u32[]{:S(2)}) %collective-permute-start.1) | collective-permute-done | bytes 466976 | tf_op jit(solution)/shard_map/ppermute | solution.py:123
  53.5 3.9 %collective-permute-start.2 = (bf16[32,7296]{1,0:T(8,128)(2,1)S(1)}, bf16[32,7296]{1,0:T(8,128)(2,1)S(1)}, u32[]{:S(2)}, u32[]{:S(2)}) collective-permute-start(bf16[32,7296]{1,0:T(8,128)(2,1)S(1)} %collective-permute-done.1), channel_id=1, source_target_pairs={{0,32},{32,64},{64,96},{96,128},{128,160},{160,192},{192,224},{224... | collective-permute-start | bytes 1400840 | tf_op jit(solution)/shard_map/ppermute | solution.py:123
  57.5 0.0 collective-permute-done.5
  57.5 2.1 %collective-permute-start.6 = (bf16[32,7296]{1,0:T(8,128)(2,1)S(1)}, bf16[32,7296]{1,0:T(8,128)(2,1)S(1)}, u32[]{:S(2)}, u32[]{:S(2)}) collective-permute-start(bf16[32,7296]{1,0:T(8,128)(2,1)S(1)} %collective-permute-done.5), channel_id=1, source_target_pairs={{0,224},{32,0},{64,32},{96,64},{128,96},{160,128},{192,160},{224,1... | collective-permute-start | bytes 1400840 | tf_op jit(solution)/shard_map/ppermute | solution.py:124
  59.6 6.1 %collective-permute-done.2 = bf16[32,7296]{1,0:T(8,128)(2,1)S(1)} collective-permute-done((bf16[32,7296]{1,0:T(8,128)(2,1)S(1)}, bf16[32,7296]{1,0:T(8,128)(2,1)S(1)}, u32[]{:S(2)}, u32[]{:S(2)}) %collective-permute-start.2) | collective-permute-done | bytes 466976 | tf_op jit(solution)/shard_map/ppermute | solution.py:123
  65.7 4.4 %collective-permute-start.3 = (bf16[32,7296]{1,0:T(8,128)(2,1)S(1)}, bf16[32,7296]{1,0:T(8,128)(2,1)S(1)}, u32[]{:S(2)}, u32[]{:S(2)}) collective-permute-start(bf16[32,7296]{1,0:T(8,128)(2,1)S(1)} %collective-permute-done.2), channel_id=1, source_target_pairs={{0,32},{32,64},{64,96},{96,128},{128,160},{160,192},{192,224},{224... | collective-permute-start | bytes 1400840 | tf_op jit(solution)/shard_map/ppermute | solution.py:123
  70.2 1.9 %collective-permute-start.7 = (bf16[32,7296]{1,0:T(8,128)(2,1)S(1)}, bf16[32,7296]{1,0:T(8,128)(2,1)S(1)}, u32[]{:S(2)}, u32[]{:S(2)}) collective-permute-start(bf16[32,7296]{1,0:T(8,128)(2,1)S(1)} %collective-permute-done.6), channel_id=1, source_target_pairs={{0,224},{32,0},{64,32},{96,64},{128,96},{160,128},{192,160},{224,1... | collective-permute-start | bytes 1400840 | tf_op jit(solution)/shard_map/ppermute | solution.py:124
  72.2 6.5 %collective-permute-done.3 = bf16[32,7296]{1,0:T(8,128)(2,1)S(1)} collective-permute-done((bf16[32,7296]{1,0:T(8,128)(2,1)S(1)}, bf16[32,7296]{1,0:T(8,128)(2,1)S(1)}, u32[]{:S(2)}, u32[]{:S(2)}) %collective-permute-start.3) | collective-permute-done | bytes 466976 | tf_op jit(solution)/shard_map/ppermute | solution.py:123
  78.7 4.4 %collective-permute-start.4 = (bf16[16,7296]{1,0:T(8,128)(2,1)S(1)}, bf16[16,7296]{1,0:T(8,128)(2,1)S(1)}, u32[]{:S(2)}, u32[]{:S(2)}) collective-permute-start(bf16[16,7296]{1,0:T(8,128)(2,1)S(1)} %slice.45), channel_id=1, source_target_pairs={{0,32},{32,64},{64,96},{96,128},{128,160},{160,192},{192,224},{224... | collective-permute-start | bytes 700424 | tf_op jit(solution)/shard_map/ppermute | solution.py:128
  83.1 1.9 %collective-permute-start.8 = (bf16[16,7296]{1,0:T(8,128)(2,1)S(1)}, bf16[16,7296]{1,0:T(8,128)(2,1)S(1)}, u32[]{:S(2)}, u32[]{:S(2)}) collective-permute-start(bf16[16,7296]{1,0:T(8,128)(2,1)S(1)} %slice.46), channel_id=1, source_target_pairs={{0,224},{32,0},{64,32},{96,64},{128,96},{160,128},{192,160},{224,1... | collective-permute-start | bytes 700424 | tf_op jit(solution)/shard_map/ppermute | solution.py:128
  85.2 1.1 multiply_convert_fusion
  86.4 0.6 collective-permute-done.4
  86.9 4.4 %collective-permute-done.8 = bf16[16,7296]{1,0:T(8,128)(2,1)S(1)} collective-permute-done((bf16[16,7296]{1,0:T(8,128)(2,1)S(1)}, bf16[16,7296]{1,0:T(8,128)(2,1)S(1)}, u32[]{:S(2)}, u32[]{:S(2)}) %collective-permute-start.8) | collective-permute-done | bytes 233504 | tf_op jit(solution)/shard_map/ppermute | solution.py:128
  91.4 0.8 multiply_convert_fusion.1
  92.1 0.0 copy-start
  92.2 1.1 broadcast_in_dim.2
  93.2 8.9 %all-to-all-start.1 = ((bf16[8,256,256]{2,1,0:T(8,128)(2,1)}), bf16[8,256,256]{2,1,0:T(8,128)(2,1)S(1)}, u32[]{:S(2)}, u32[]{:S(2)}) async-start(bf16[8,256,256]{2,1,0:T(8,128)(2,1)} %broadcast_in_dim.2), calls=%async_computation.1 | async-start | bytes 2097152 | tf_op jit(solution)/shard_map/all_to_all | solution.py:134
  102.1 0.1 pad_add_fusion.where_ref
  102.2 0.7 slice.47.refs_0_
  102.9 0.7 slice.48.refs_1_
  103.6 0.7 slice.54.refs_7_
  104.3 0.7 slice.49.refs_2_
  105.0 0.7 slice.53.refs_6_
  105.7 0.7 slice.50.refs_3_
  106.4 0.7 slice.51.refs_4_
  107.1 0.0 collective-permute-done.other_ref
  107.1 12.0 %all-to-all-done.1.got_ref = bf16[8,256,256]{2,1,0:T(8,128)(2,1)S(1)} async-done(((bf16[8,256,256]{2,1,0:T(8,128)(2,1)}), bf16[8,256,256]{2,1,0:T(8,128)(2,1)S(1)}, u32[]{:S(2)}, u32[]{:S(2)}) %all-to-all-start.1) | async-done | bytes 1048608 | tf_op jit(solution)/shard_map/all_to_all | solution.py:134
  119.1 3.3 %shard_map.56 = bf16[512,896]{1,0:T(8,128)(2,1)S(1)} custom-call(s32[3]{0:T(128)S(1)} %pad_add_fusion.where_ref, bf16[448,2048]{1,0:T(8,128)(2,1)S(1)} %bitcast.20, bf16[448,2048]{1,0:T(8,128)(2,1)} %collective-permute-done.other_ref, bf16[8,256,256]{2,1,0:T(8,128)(2,1)S(1)} %all-to-all-done.1.got_ref, bf16[32,128]{1,0:T(8,128)(2,1)S(1)} %slice.47.refs_0_, ...), custom_call_target="tpu_custom_call" | custom-call | tf_op jit(solution)/shard_map/pallas_call | solution.py:140
  122.4 12.6 %all_to_all.20 = bf16[4,128,896]{2,1,0:T(8,128)(2,1)S(1)} all-to-all(bf16[4,128,896]{2,1,0:T(8,128)(2,1)S(1)} %bitcast.18), channel_id=1, replica_groups=mesh['side'=2,'grp'=8,'x'=4,'z'=8] {'x'}, dimensions={0} | all-to-all | bytes 1835008 | tf_op jit(solution)/shard_map/all_to_all | solution.py:157
  135.0 0.1 reduce_sum.34
  135.1 0.1 reshape.25
  135.2 29.9 %all_to_all.21 = bf16[64,2,896]{2,1,0:T(2,128)(2,1)S(1)} all-to-all(bf16[64,2,896]{2,1,0:T(2,128)(2,1)S(1)} %reshape.25), channel_id=1, replica_groups=mesh['side'=2,'grp'=8,'x'=4,'z'=8] {'z','grp'}, dimensions={0} | all-to-all | bytes 458752 | tf_op jit(solution)/shard_map/all_to_all | solution.py:161
  165.2 0.2 reduce_sum.35
  165.4 0.1 reshape.29
  165.5 0.7 reshape.28
  (30 shorter events, 0.4 us)
Async XLA Ops:
  1.9 39.5 %all-to-all-start = ((bf16[32,2,7296]{2,1,0:T(2,128)(2,1)}), bf16[32,2,7296]{2,1,0:T(2,128)(2,1)S(1)}, u32[]{:S(2)}, u32[]{:S(2)}) async-start(bf16[32,2,7296]{2,1,0:T(2,128)(2,1)} %shard_map.55), calls=%async_computation | async-start | bytes 1867776 | tf_op jit(solution)/shard_map/all_to_all | solution.py:99
  15.1 33.1 %collective-permute-start.9 = (bf16[7168,128]{1,0:T(8,128)(2,1)}, bf16[7168,128]{1,0:T(8,128)(2,1)}, u32[]{:S(2)}, u32[]{:S(2)}) collective-permute-start(bf16[7168,128]{1,0:T(8,128)(2,1)} %bitcast.21), channel_id=1, source_target_pairs={{0,256},{256,0},{1,257},{257,1},{2,258},{258,2},{3,259},{259,3},{4... | collective-permute-start | bytes 5505032 | tf_op jit(solution)/shard_map/ppermute | solution.py:36
  17.0 90.1 %collective-permute-start = (bf16[448,2048]{1,0:T(8,128)(2,1)}, bf16[448,2048]{1,0:T(8,128)(2,1)}, u32[]{:S(2)}, u32[]{:S(2)}) collective-permute-start(bf16[448,2048]{1,0:T(8,128)(2,1)} %bitcast.19), channel_id=1, source_target_pairs={{0,256},{256,0},{1,257},{257,1},{2,258},{258,2},{3,259},{259,3},{4... | collective-permute-start | bytes 5505032 | tf_op jit(solution)/shard_map/ppermute | solution.py:36
  42.3 8.2 %copy-start.2 = (bf16[32,7296]{1,0:T(8,128)(2,1)}, bf16[32,7296]{1,0:T(8,128)(2,1)S(1)}, u32[]{:S(2)}) copy-start(bf16[32,7296]{1,0:T(8,128)(2,1)S(1)} %get-tuple-element.14) | copy-start | bytes 1400836
  42.4 11.2 %collective-permute-start.1 = (bf16[32,7296]{1,0:T(8,128)(2,1)S(1)}, bf16[32,7296]{1,0:T(8,128)(2,1)S(1)}, u32[]{:S(2)}, u32[]{:S(2)}) collective-permute-start(bf16[32,7296]{1,0:T(8,128)(2,1)S(1)} %get-tuple-element.14), channel_id=1, source_target_pairs={{0,32},{32,64},{64,96},{96,128},{128,160},{160,192},{192,224},{224... | collective-permute-start | bytes 1400840 | tf_op jit(solution)/shard_map/ppermute | solution.py:123
  45.8 11.6 %collective-permute-start.5 = (bf16[32,7296]{1,0:T(8,128)(2,1)S(1)}, bf16[32,7296]{1,0:T(8,128)(2,1)S(1)}, u32[]{:S(2)}, u32[]{:S(2)}) collective-permute-start(bf16[32,7296]{1,0:T(8,128)(2,1)S(1)} %get-tuple-element.14), channel_id=1, source_target_pairs={{0,224},{32,0},{64,32},{96,64},{128,96},{160,128},{192,160},{224,1... | collective-permute-start | bytes 1400840 | tf_op jit(solution)/shard_map/ppermute | solution.py:124
  53.5 31.7 %copy-start.3 = (bf16[32,7296]{1,0:T(8,128)(2,1)}, bf16[32,7296]{1,0:T(8,128)(2,1)S(1)}, u32[]{:S(2)}) copy-start(bf16[32,7296]{1,0:T(8,128)(2,1)S(1)} %collective-permute-done.1) | copy-start | bytes 1400836
  53.5 12.2 %collective-permute-start.2 = (bf16[32,7296]{1,0:T(8,128)(2,1)S(1)}, bf16[32,7296]{1,0:T(8,128)(2,1)S(1)}, u32[]{:S(2)}, u32[]{:S(2)}) collective-permute-start(bf16[32,7296]{1,0:T(8,128)(2,1)S(1)} %collective-permute-done.1), channel_id=1, source_target_pairs={{0,32},{32,64},{64,96},{96,128},{128,160},{160,192},{192,224},{224... | collective-permute-start | bytes 1400840 | tf_op jit(solution)/shard_map/ppermute | solution.py:123
  57.5 28.8 %copy-start.4 = (bf16[32,7296]{1,0:T(8,128)(2,1)}, bf16[32,7296]{1,0:T(8,128)(2,1)S(1)}, u32[]{:S(2)}) copy-start(bf16[32,7296]{1,0:T(8,128)(2,1)S(1)} %collective-permute-done.5) | copy-start | bytes 1400836
  57.5 12.7 %collective-permute-start.6 = (bf16[32,7296]{1,0:T(8,128)(2,1)S(1)}, bf16[32,7296]{1,0:T(8,128)(2,1)S(1)}, u32[]{:S(2)}, u32[]{:S(2)}) collective-permute-start(bf16[32,7296]{1,0:T(8,128)(2,1)S(1)} %collective-permute-done.5), channel_id=1, source_target_pairs={{0,224},{32,0},{64,32},{96,64},{128,96},{160,128},{192,160},{224,1... | collective-permute-start | bytes 1400840 | tf_op jit(solution)/shard_map/ppermute | solution.py:124
  65.7 19.5 %copy-start.5 = (bf16[32,7296]{1,0:T(8,128)(2,1)}, bf16[32,7296]{1,0:T(8,128)(2,1)S(1)}, u32[]{:S(2)}) copy-start(bf16[32,7296]{1,0:T(8,128)(2,1)S(1)} %collective-permute-done.2) | copy-start | bytes 1400836
  65.7 13.0 %collective-permute-start.3 = (bf16[32,7296]{1,0:T(8,128)(2,1)S(1)}, bf16[32,7296]{1,0:T(8,128)(2,1)S(1)}, u32[]{:S(2)}, u32[]{:S(2)}) collective-permute-start(bf16[32,7296]{1,0:T(8,128)(2,1)S(1)} %collective-permute-done.2), channel_id=1, source_target_pairs={{0,32},{32,64},{64,96},{96,128},{128,160},{160,192},{192,224},{224... | collective-permute-start | bytes 1400840 | tf_op jit(solution)/shard_map/ppermute | solution.py:123
  70.2 16.2 %copy-start.6 = (bf16[32,7296]{1,0:T(8,128)(2,1)}, bf16[32,7296]{1,0:T(8,128)(2,1)S(1)}, u32[]{:S(2)}) copy-start(bf16[32,7296]{1,0:T(8,128)(2,1)S(1)} %collective-permute-done.6) | copy-start | bytes 1400836
  70.2 12.9 %collective-permute-start.7 = (bf16[32,7296]{1,0:T(8,128)(2,1)S(1)}, bf16[32,7296]{1,0:T(8,128)(2,1)S(1)}, u32[]{:S(2)}, u32[]{:S(2)}) collective-permute-start(bf16[32,7296]{1,0:T(8,128)(2,1)S(1)} %collective-permute-done.6), channel_id=1, source_target_pairs={{0,224},{32,0},{64,32},{96,64},{128,96},{160,128},{192,160},{224,1... | collective-permute-start | bytes 1400840 | tf_op jit(solution)/shard_map/ppermute | solution.py:124
  78.7 8.2 %collective-permute-start.4 = (bf16[16,7296]{1,0:T(8,128)(2,1)S(1)}, bf16[16,7296]{1,0:T(8,128)(2,1)S(1)}, u32[]{:S(2)}, u32[]{:S(2)}) collective-permute-start(bf16[16,7296]{1,0:T(8,128)(2,1)S(1)} %slice.45), channel_id=1, source_target_pairs={{0,32},{32,64},{64,96},{96,128},{128,160},{160,192},{192,224},{224... | collective-permute-start | bytes 700424 | tf_op jit(solution)/shard_map/ppermute | solution.py:128
  83.1 2.0 %copy-start.1 = (bf16[32,7296]{1,0:T(8,128)(2,1)}, bf16[32,7296]{1,0:T(8,128)(2,1)S(1)}, u32[]{:S(2)}) copy-start(bf16[32,7296]{1,0:T(8,128)(2,1)S(1)} %collective-permute-done.7) | copy-start | bytes 1400836
  83.1 8.2 %collective-permute-start.8 = (bf16[16,7296]{1,0:T(8,128)(2,1)S(1)}, bf16[16,7296]{1,0:T(8,128)(2,1)S(1)}, u32[]{:S(2)}, u32[]{:S(2)}) collective-permute-start(bf16[16,7296]{1,0:T(8,128)(2,1)S(1)} %slice.46), channel_id=1, source_target_pairs={{0,224},{32,0},{64,32},{96,64},{128,96},{160,128},{192,160},{224,1... | collective-permute-start | bytes 700424 | tf_op jit(solution)/shard_map/ppermute | solution.py:128
  91.3 0.8 copy-start.7
  92.1 27.0 %copy-start = (bf16[1,2048,448]{1,2,0:T(8,128)(2,1)S(1)}, bf16[1,2048,448]{1,2,0:T(8,128)(2,1)}, u32[]{:S(2)}) copy-start(bf16[1,2048,448]{1,2,0:T(8,128)(2,1)} %param.9) | copy-start | bytes 5505028
  93.2 25.9 %all-to-all-start.1 = ((bf16[8,256,256]{2,1,0:T(8,128)(2,1)}), bf16[8,256,256]{2,1,0:T(8,128)(2,1)S(1)}, u32[]{:S(2)}, u32[]{:S(2)}) async-start(bf16[8,256,256]{2,1,0:T(8,128)(2,1)} %broadcast_in_dim.2), calls=%async_computation.1 | async-start | bytes 2097152 | tf_op jit(solution)/shard_map/all_to_all | solution.py:134

commit v8 on v7

--- a/solution.py
+++ b/solution.py
@@ -87,17 +87,18 @@
     unit = w_gate.shape[2]
 
     own_gate, own_down = w_gate[0], w_down[0].T
-    other_down = from_other_core(own_down)
+    other_gate = from_other_core(own_gate)
 
     vmem, smem = pl.BlockSpec(memory_space=pltpu.VMEM), pl.BlockSpec(memory_space=pltpu.SMEM)
     copies = pl.pallas_call(
         functools.partial(send_kernel, rows),
-        out_shape=jax.ShapeDtypeStruct((n_dev, rows, width + TAIL), bf16),
+        out_shape=jax.ShapeDtypeStruct((n_z, rows, width + TAIL), bf16),
         in_specs=[smem, vmem, vmem, vmem],
         out_specs=vmem,
     )(dev.reshape(1).astype(i32), tokens, expert_ids, route_weights)
-    packed = lax.all_to_all(copies, ("x", "z"), split_axis=0, concat_axis=0, tiled=True)
-    packed = packed.reshape(n_dev * rows, -1)
+    by_z = lax.all_to_all(copies, "z", split_axis=0, concat_axis=0, tiled=True).reshape(n_z * rows, -1)
+    by_z, other_gate = lax.optimization_barrier((by_z, other_gate))
+    packed = lax.all_gather(by_z, "x", axis=0, tiled=True)
 
     group = n_dev * rows
     hit = jnp.any(packed[:, width : width + TOPK].astype(i32) == dev, axis=1)
@@ -106,7 +107,6 @@
     placed = (slot[None, :] == jnp.arange(CAP, dtype=i32)[:, None]) & hit[None, :]
     slot_input = jnp.dot(placed.astype(bf16), packed, preferred_element_type=f32).astype(bf16)
 
-    other_gate = from_other_core(own_gate)
     both = [jnp.where(side == 0, own_gate, other_gate), jnp.where(side == 0, other_gate, own_gate)]
     gate_slab = jnp.pad(jnp.concatenate(both, axis=1), ((0, TAIL), (0, 0)))
 
@@ -131,6 +131,8 @@
     blocks[far] = jnp.concatenate([below, above], axis=0)
     order.append(far)
     hidden = jnp.concatenate([product, silu_gate([blocks[far]])], axis=0)
+    hidden, own_down = lax.optimization_barrier((hidden, own_down))
+    other_down = from_other_core(own_down)
     got = lax.all_to_all(
         jnp.broadcast_to(hidden[None], (n_grp,) + hidden.shape), "grp", split_axis=0, concat_axis=0, tiled=True
     )

time: 167 us -> 160 us (0.958)
  starting transfers between devices: 50.9 us -> 45.7 us
  waiting for transfers between devices: 54.6 us -> 50.6 us
  blocking collectives: 42.5 us -> 45.6 us
    ppermute x3, waiting for transfers between devices: 0.01 us -> 16.5 us  [on_device(): above = lax.ppermute(above, 'grp', down)]
    all_gather x0 -> x1, blocking collectives: none -> 14.3 us  [on_device(): packed = lax.all_gather(by_z, 'x', axis=0, tiled=True)]
    ppermute x3, waiting for transfers between devices: 15.6 us -> 1.44 us  [on_device(): below = lax.ppermute(below, 'grp', up)]
    all_to_all x1, blocking collectives: 29.9 us -> 17.6 us  [on_device(): lax.all_to_all(total_x.reshape(n_z * n_grp, rows, -1), ('z', 'grp'), spli...]
    all_to_all x1, waiting for transfers between devices: 22 us -> 11.9 us  [on_device(): lax.all_to_all(copies, 'z', split_axis=0, concat_axis=0, tiled=True)]
    ppermute x1, waiting for transfers between devices: 0.59 us -> 5.67 us  [on_device(): lax.ppermute(below[:half], 'grp', up)]
    ppermute x3, starting transfers between devices: 11.8 us -> 7.43 us  [on_device(): below = lax.ppermute(below, 'grp', up)]
    ppermute x1, waiting for transfers between devices: 4.36 us -> 0.33 us  [on_device(): lax.ppermute(above[half:], 'grp', down)]
  transfers between devices with their start and end apart: 12 -> 12, of which waited for: 7 -> 10; matrix products, arithmetic and copies ran while one was open for 7% -> 5% of each run, Pallas kernels for 0% -> 1%
where the time goes in v8:
time: 160 us; the launch traced here: 159 us
  waiting for transfers between devices  50.6 us (32%)
  starting transfers between devices  45.7 us (29%)
  blocking collectives  45.6 us (28%)
  local copies, waits for them, and re-layouts  7.31 us (5%)
  Pallas kernels  4.92 us (3%)
  other arithmetic  2.39 us (1%)
  matrix products  2.15 us (1%)
    all_to_all x1, blocking collectives, on_device(): lax.all_to_all(total_x.reshape(n_z * n_grp, rows, -1), ('z', 'grp'), spli...  17.6 us
    ppermute x3, waiting for transfers between devices, on_device(): above = lax.ppermute(above, 'grp', down)  16.5 us
    all_to_all x1, waiting for transfers between devices, on_device(): lax.all_to_all(jnp.broadcast_to(hidden[None], (n_grp,) + hidden.shape), '...  14.8 us
    all_gather x1, blocking collectives, on_device(): packed = lax.all_gather(by_z, 'x', axis=0, tiled=True)  14.3 us
    all_to_all x1, blocking collectives, on_device(): lax.all_to_all(weighted.reshape(n_x, n_z * n_grp * rows, -1), 'x', split_...  13.8 us
    all_to_all x1, waiting for transfers between devices, on_device(): lax.all_to_all(copies, 'z', split_axis=0, concat_axis=0, tiled=True)  11.9 us
    all_to_all x1, starting transfers between devices, on_device(): lax.all_to_all(copies, 'z', split_axis=0, concat_axis=0, tiled=True)  10.3 us
    ppermute x3, starting transfers between devices, on_device(): above = lax.ppermute(above, 'grp', down)  10.2 us
  transfers between devices with their start and end apart: 12, of which 10 were waited for; matrix products, arithmetic and copies ran while one was open for 5% of the time, Pallas kernels for 1%

profile of v8, /device:TPU:8, one launch (start us, length us, event | category | flops | bytes accessed | tf_op | source)
XLA Modules:
  0.0 159.1 jit_solution(3856361246894736061)
XLA Ops:
  0.0 2.0 %collective-permute-start = (bf16[7168,128]{1,0:T(8,128)(2,1)}, bf16[7168,128]{1,0:T(8,128)(2,1)}, u32[]{:S(2)}, u32[]{:S(2)}) collective-permute-start(bf16[7168,128]{1,0:T(8,128)(2,1)} %bitcast.21), channel_id=1, source_target_pairs={{0,256},{256,0},{1,257},{257,1},{2,258},{258,2},{3,259},{259,3},{4... | collective-permute-start | bytes 5505032 | tf_op jit(solution)/shard_map/ppermute | solution.py:36
  2.1 1.7 %shard_map.55 = bf16[8,2,7296]{2,1,0:T(2,128)(2,1)} custom-call(s32[1]{0:T(128)} %bitcast.1.dev_ref, bf16[2,7168]{1,0:T(2,128)(2,1)} %tokens_ref.1, s32[2,8]{1,0:T(2,128)} %ids_ref.1, bf16[2,8]{1,0:T(2,128)(2,1)} %weights_ref.1), custom_call_target="tpu_custom_call" | custom-call | tf_op jit(solution)/shard_map/pallas_call | solution.py:93
  3.7 10.3 %all-to-all-start = ((bf16[8,2,7296]{2,1,0:T(2,128)(2,1)}), bf16[8,2,7296]{2,1,0:T(2,128)(2,1)S(1)}, u32[]{:S(2)}, u32[]{:S(2)}) async-start(bf16[8,2,7296]{2,1,0:T(2,128)(2,1)} %shard_map.55), calls=%async_computation | async-start | bytes 466944 | tf_op jit(solution)/shard_map/all_to_all | solution.py:99
  14.0 11.9 %all-to-all-done = bf16[8,2,7296]{2,1,0:T(2,128)(2,1)S(1)} async-done(((bf16[8,2,7296]{2,1,0:T(2,128)(2,1)}), bf16[8,2,7296]{2,1,0:T(2,128)(2,1)S(1)}, u32[]{:S(2)}, u32[]{:S(2)}) %all-to-all-start) | async-done | bytes 233504 | tf_op jit(solution)/shard_map/all_to_all | solution.py:99
  26.0 0.1 reshape.23
  26.1 14.3 %all_gather.3 = bf16[64,7296]{1,0:T(8,128)(2,1)S(1)} all-gather(bf16[16,7296]{1,0:T(8,128)(2,1)S(1)} %reshape.23), channel_id=1, replica_groups=mesh['side'=2,'grp'=8,'x'=4,'z'=8] {'x'}, dimensions={0}, use_global_device_ids=true | all-gather | bytes 1167360 | tf_op jit(solution)/shard_map/all_gather | solution.py:101
  40.3 0.1 fusion.12
  40.4 0.1 convert_reduce_fusion
  40.5 0.3 constant_dynamic-update-slice_fusion.6
  40.8 2.4 %collective-permute-start.5 = (bf16[32,7296]{1,0:T(8,128)(2,1)S(1)}, bf16[32,7296]{1,0:T(8,128)(2,1)S(1)}, u32[]{:S(2)}, u32[]{:S(2)}) collective-permute-start(bf16[32,7296]{1,0:T(8,128)(2,1)S(1)} %get-tuple-element.22), channel_id=1, source_target_pairs={{0,224},{32,0},{64,32},{96,64},{128,96},{160,128},{192,160},{224,1... | collective-permute-start | bytes 1400840 | tf_op jit(solution)/shard_map/ppermute | solution.py:124
  43.2 3.5 %collective-permute-start.1 = (bf16[32,7296]{1,0:T(8,128)(2,1)S(1)}, bf16[32,7296]{1,0:T(8,128)(2,1)S(1)}, u32[]{:S(2)}, u32[]{:S(2)}) collective-permute-start(bf16[32,7296]{1,0:T(8,128)(2,1)S(1)} %get-tuple-element.22), channel_id=1, source_target_pairs={{0,32},{32,64},{64,96},{96,128},{128,160},{160,192},{192,224},{224... | collective-permute-start | bytes 1400840 | tf_op jit(solution)/shard_map/ppermute | solution.py:123
  46.7 1.7 %broadcast_select_fusion.1 = (bf16[7168,128]{1,0:T(8,128)(2,1)S(1)}, bf16[7168,128]{1,0:T(8,128)(2,1)S(1)}) fusion(bf16[7168,128]{1,0:T(8,128)(2,1)} %collective-permute-done, pred[]{:T(512)S(6)} %eq.28, bf16[1,7168,128]{2,1,0:T(8,128)(2,1)S(1)} %copy-done.1), kind=kLoop, calls=%fused_computation.6 | loop fusion | flops 1835008 | bytes 7340033 | tf_op jit(solution)/shard_map/jit(_where)/select_n | solution.py:110
  48.5 5.3 %collective-permute-done.5 = bf16[32,7296]{1,0:T(8,128)(2,1)S(1)} collective-permute-done((bf16[32,7296]{1,0:T(8,128)(2,1)S(1)}, bf16[32,7296]{1,0:T(8,128)(2,1)S(1)}, u32[]{:S(2)}, u32[]{:S(2)}) %collective-permute-start.5) | collective-permute-done | bytes 466976 | tf_op jit(solution)/shard_map/ppermute | solution.py:124
  53.8 3.3 %collective-permute-start.6 = (bf16[32,7296]{1,0:T(8,128)(2,1)S(1)}, bf16[32,7296]{1,0:T(8,128)(2,1)S(1)}, u32[]{:S(2)}, u32[]{:S(2)}) collective-permute-start(bf16[32,7296]{1,0:T(8,128)(2,1)S(1)} %collective-permute-done.5), channel_id=1, source_target_pairs={{0,224},{32,0},{64,32},{96,64},{128,96},{160,128},{192,160},{224,1... | collective-permute-start | bytes 1400840 | tf_op jit(solution)/shard_map/ppermute | solution.py:124
  57.1 0.5 collective-permute-done.1
  57.6 2.0 %collective-permute-start.2 = (bf16[32,7296]{1,0:T(8,128)(2,1)S(1)}, bf16[32,7296]{1,0:T(8,128)(2,1)S(1)}, u32[]{:S(2)}, u32[]{:S(2)}) collective-permute-start(bf16[32,7296]{1,0:T(8,128)(2,1)S(1)} %collective-permute-done.1), channel_id=1, source_target_pairs={{0,32},{32,64},{64,96},{96,128},{128,160},{160,192},{192,224},{224... | collective-permute-start | bytes 1400840 | tf_op jit(solution)/shard_map/ppermute | solution.py:123
  59.7 6.0 %collective-permute-done.6 = bf16[32,7296]{1,0:T(8,128)(2,1)S(1)} collective-permute-done((bf16[32,7296]{1,0:T(8,128)(2,1)S(1)}, bf16[32,7296]{1,0:T(8,128)(2,1)S(1)}, u32[]{:S(2)}, u32[]{:S(2)}) %collective-permute-start.6) | collective-permute-done | bytes 466976 | tf_op jit(solution)/shard_map/ppermute | solution.py:124
  65.7 4.5 %collective-permute-start.7 = (bf16[32,7296]{1,0:T(8,128)(2,1)S(1)}, bf16[32,7296]{1,0:T(8,128)(2,1)S(1)}, u32[]{:S(2)}, u32[]{:S(2)}) collective-permute-start(bf16[32,7296]{1,0:T(8,128)(2,1)S(1)} %collective-permute-done.6), channel_id=1, source_target_pairs={{0,224},{32,0},{64,32},{96,64},{128,96},{160,128},{192,160},{224,1... | collective-permute-start | bytes 1400840 | tf_op jit(solution)/shard_map/ppermute | solution.py:124
  70.3 0.5 collective-permute-done.2
  70.8 1.9 %collective-permute-start.3 = (bf16[32,7296]{1,0:T(8,128)(2,1)S(1)}, bf16[32,7296]{1,0:T(8,128)(2,1)S(1)}, u32[]{:S(2)}, u32[]{:S(2)}) collective-permute-start(bf16[32,7296]{1,0:T(8,128)(2,1)S(1)} %collective-permute-done.2), channel_id=1, source_target_pairs={{0,32},{32,64},{64,96},{96,128},{128,160},{160,192},{192,224},{224... | collective-permute-start | bytes 1400840 | tf_op jit(solution)/shard_map/ppermute | solution.py:123
  72.8 5.2 %collective-permute-done.7 = bf16[32,7296]{1,0:T(8,128)(2,1)S(1)} collective-permute-done((bf16[32,7296]{1,0:T(8,128)(2,1)S(1)}, bf16[32,7296]{1,0:T(8,128)(2,1)S(1)}, u32[]{:S(2)}, u32[]{:S(2)}) %collective-permute-start.7) | collective-permute-done | bytes 466976 | tf_op jit(solution)/shard_map/ppermute | solution.py:124
  78.0 4.6 %collective-permute-start.8 = (bf16[16,7296]{1,0:T(8,128)(2,1)S(1)}, bf16[16,7296]{1,0:T(8,128)(2,1)S(1)}, u32[]{:S(2)}, u32[]{:S(2)}) collective-permute-start(bf16[16,7296]{1,0:T(8,128)(2,1)S(1)} %slice.46), channel_id=1, source_target_pairs={{0,224},{32,0},{64,32},{96,64},{128,96},{160,128},{192,160},{224,1... | collective-permute-start | bytes 700424 | tf_op jit(solution)/shard_map/ppermute | solution.py:128
  82.6 0.5 collective-permute-done.3
  83.1 1.9 %collective-permute-start.4 = (bf16[16,7296]{1,0:T(8,128)(2,1)S(1)}, bf16[16,7296]{1,0:T(8,128)(2,1)S(1)}, u32[]{:S(2)}, u32[]{:S(2)}) collective-permute-start(bf16[16,7296]{1,0:T(8,128)(2,1)S(1)} %slice.45), channel_id=1, source_target_pairs={{0,32},{32,64},{64,96},{96,128},{128,160},{160,192},{192,224},{224... | collective-permute-start | bytes 700424 | tf_op jit(solution)/shard_map/ppermute | solution.py:128
  85.1 1.1 multiply_convert_fusion
  86.3 0.3 collective-permute-done.8
  86.6 5.7 %collective-permute-done.4 = bf16[16,7296]{1,0:T(8,128)(2,1)S(1)} collective-permute-done((bf16[16,7296]{1,0:T(8,128)(2,1)S(1)}, bf16[16,7296]{1,0:T(8,128)(2,1)S(1)}, u32[]{:S(2)}, u32[]{:S(2)}) %collective-permute-start.4) | collective-permute-done | bytes 233504 | tf_op jit(solution)/shard_map/ppermute | solution.py:128
  92.3 0.8 multiply_convert_fusion.1
  93.1 1.1 broadcast_in_dim.2
  94.2 7.3 %all-to-all-start.1 = ((bf16[8,256,256]{2,1,0:T(8,128)(2,1)}), bf16[8,256,256]{2,1,0:T(8,128)(2,1)S(1)}, u32[]{:S(2)}, u32[]{:S(2)}) async-start(bf16[8,256,256]{2,1,0:T(8,128)(2,1)} %broadcast_in_dim.2), calls=%async_computation.1 | async-start | bytes 2097152 | tf_op jit(solution)/shard_map/all_to_all | solution.py:136
  101.5 1.9 %collective-permute-start.9 = (bf16[448,2048]{1,0:T(8,128)(2,1)S(1)}, bf16[448,2048]{1,0:T(8,128)(2,1)}, u32[]{:S(2)}, u32[]{:S(2)}) collective-permute-start(bf16[448,2048]{1,0:T(8,128)(2,1)S(1)} %bitcast.19), channel_id=1, source_target_pairs={{0,256},{256,0},{1,257},{257,1},{2,258},{258,2},{3,259},{259,3},{4... | collective-permute-start | bytes 5505032 | tf_op jit(solution)/shard_map/ppermute | solution.py:36
  103.4 0.1 pad_add_fusion.where_ref
  103.5 0.7 slice.47.refs_0_
  104.2 0.7 slice.48.refs_1_
  104.9 0.7 slice.54.refs_7_
  105.6 0.7 slice.49.refs_2_
  106.3 0.7 slice.53.refs_6_
  107.0 0.7 slice.52.refs_5_
  107.7 0.7 slice.51.refs_4_
  108.4 14.8 %all-to-all-done.1.got_ref = bf16[8,256,256]{2,1,0:T(8,128)(2,1)S(1)} async-done(((bf16[8,256,256]{2,1,0:T(8,128)(2,1)}), bf16[8,256,256]{2,1,0:T(8,128)(2,1)S(1)}, u32[]{:S(2)}, u32[]{:S(2)}) %all-to-all-start.1) | async-done | bytes 1048608 | tf_op jit(solution)/shard_map/all_to_all | solution.py:136
  123.2 3.3 %shard_map.56 = bf16[512,896]{1,0:T(8,128)(2,1)S(1)} custom-call(s32[3]{0:T(128)S(1)} %pad_add_fusion.where_ref, bf16[448,2048]{1,0:T(8,128)(2,1)S(1)} %bitcast.20, bf16[448,2048]{1,0:T(8,128)(2,1)} %collective-permute-done.9.other_ref, bf16[8,256,256]{2,1,0:T(8,128)(2,1)S(1)} %all-to-all-done.1.got_ref, bf16[32,128]{1,0:T(8,128)(2,1)S(1)} %slice.47.refs_0_, ...), custom_call_target="tpu_custom_call" | custom-call | tf_op jit(solution)/shard_map/pallas_call | solution.py:142
  126.5 13.8 %all_to_all.20 = bf16[4,128,896]{2,1,0:T(8,128)(2,1)S(1)} all-to-all(bf16[4,128,896]{2,1,0:T(8,128)(2,1)S(1)} %bitcast.18), channel_id=1, replica_groups=mesh['side'=2,'grp'=8,'x'=4,'z'=8] {'x'}, dimensions={0} | all-to-all | bytes 1835008 | tf_op jit(solution)/shard_map/all_to_all | solution.py:159
  140.2 0.1 reduce_sum.34
  140.4 0.1 reshape.25
  140.5 17.6 %all_to_all.21 = bf16[64,2,896]{2,1,0:T(2,128)(2,1)S(1)} all-to-all(bf16[64,2,896]{2,1,0:T(2,128)(2,1)S(1)} %reshape.25), channel_id=1, replica_groups=mesh['side'=2,'grp'=8,'x'=4,'z'=8] {'z','grp'}, dimensions={0} | all-to-all | bytes 458752 | tf_op jit(solution)/shard_map/all_to_all | solution.py:163
  158.0 0.2 reduce_sum.35
  158.2 0.1 reshape.29
  158.4 0.7 reshape.28
  (33 shorter events, 0.4 us)
Async XLA Ops:
  0.0 46.7 %copy-start.1 = (bf16[1,7168,128]{2,1,0:T(8,128)(2,1)S(1)}, bf16[1,7168,128]{2,1,0:T(8,128)(2,1)}, u32[]{:S(2)}) copy-start(bf16[1,7168,128]{2,1,0:T(8,128)(2,1)} %param.8) | copy-start | bytes 5505028
  0.0 26.0 %collective-permute-start = (bf16[7168,128]{1,0:T(8,128)(2,1)}, bf16[7168,128]{1,0:T(8,128)(2,1)}, u32[]{:S(2)}, u32[]{:S(2)}) collective-permute-start(bf16[7168,128]{1,0:T(8,128)(2,1)} %bitcast.21), channel_id=1, source_target_pairs={{0,256},{256,0},{1,257},{257,1},{2,258},{258,2},{3,259},{259,3},{4... | collective-permute-start | bytes 5505032 | tf_op jit(solution)/shard_map/ppermute | solution.py:36
  3.7 22.2 %all-to-all-start = ((bf16[8,2,7296]{2,1,0:T(2,128)(2,1)}), bf16[8,2,7296]{2,1,0:T(2,128)(2,1)S(1)}, u32[]{:S(2)}, u32[]{:S(2)}) async-start(bf16[8,2,7296]{2,1,0:T(2,128)(2,1)} %shard_map.55), calls=%async_computation | async-start | bytes 466944 | tf_op jit(solution)/shard_map/all_to_all | solution.py:99
  40.8 7.6 %copy-start.3 = (bf16[32,7296]{1,0:T(8,128)(2,1)}, bf16[32,7296]{1,0:T(8,128)(2,1)S(1)}, u32[]{:S(2)}) copy-start(bf16[32,7296]{1,0:T(8,128)(2,1)S(1)} %get-tuple-element.22) | copy-start | bytes 1400836
  40.8 12.9 %collective-permute-start.5 = (bf16[32,7296]{1,0:T(8,128)(2,1)S(1)}, bf16[32,7296]{1,0:T(8,128)(2,1)S(1)}, u32[]{:S(2)}, u32[]{:S(2)}) collective-permute-start(bf16[32,7296]{1,0:T(8,128)(2,1)S(1)} %get-tuple-element.22), channel_id=1, source_target_pairs={{0,224},{32,0},{64,32},{96,64},{128,96},{160,128},{192,160},{224,1... | collective-permute-start | bytes 1400840 | tf_op jit(solution)/shard_map/ppermute | solution.py:124
  43.2 14.4 %collective-permute-start.1 = (bf16[32,7296]{1,0:T(8,128)(2,1)S(1)}, bf16[32,7296]{1,0:T(8,128)(2,1)S(1)}, u32[]{:S(2)}, u32[]{:S(2)}) collective-permute-start(bf16[32,7296]{1,0:T(8,128)(2,1)S(1)} %get-tuple-element.22), channel_id=1, source_target_pairs={{0,32},{32,64},{64,96},{96,128},{128,160},{160,192},{192,224},{224... | collective-permute-start | bytes 1400840 | tf_op jit(solution)/shard_map/ppermute | solution.py:123
  53.8 31.4 %copy-start.4 = (bf16[32,7296]{1,0:T(8,128)(2,1)}, bf16[32,7296]{1,0:T(8,128)(2,1)S(1)}, u32[]{:S(2)}) copy-start(bf16[32,7296]{1,0:T(8,128)(2,1)S(1)} %collective-permute-done.5) | copy-start | bytes 1400836
  53.8 12.0 %collective-permute-start.6 = (bf16[32,7296]{1,0:T(8,128)(2,1)S(1)}, bf16[32,7296]{1,0:T(8,128)(2,1)S(1)}, u32[]{:S(2)}, u32[]{:S(2)}) collective-permute-start(bf16[32,7296]{1,0:T(8,128)(2,1)S(1)} %collective-permute-done.5), channel_id=1, source_target_pairs={{0,224},{32,0},{64,32},{96,64},{128,96},{160,128},{192,160},{224,1... | collective-permute-start | bytes 1400840 | tf_op jit(solution)/shard_map/ppermute | solution.py:124
  57.6 27.6 %copy-start.5 = (bf16[32,7296]{1,0:T(8,128)(2,1)}, bf16[32,7296]{1,0:T(8,128)(2,1)S(1)}, u32[]{:S(2)}) copy-start(bf16[32,7296]{1,0:T(8,128)(2,1)S(1)} %collective-permute-done.1) | copy-start | bytes 1400836
  57.6 13.2 %collective-permute-start.2 = (bf16[32,7296]{1,0:T(8,128)(2,1)S(1)}, bf16[32,7296]{1,0:T(8,128)(2,1)S(1)}, u32[]{:S(2)}, u32[]{:S(2)}) collective-permute-start(bf16[32,7296]{1,0:T(8,128)(2,1)S(1)} %collective-permute-done.1), channel_id=1, source_target_pairs={{0,32},{32,64},{64,96},{96,128},{128,160},{160,192},{192,224},{224... | collective-permute-start | bytes 1400840 | tf_op jit(solution)/shard_map/ppermute | solution.py:123
  65.7 19.4 %copy-start.6 = (bf16[32,7296]{1,0:T(8,128)(2,1)}, bf16[32,7296]{1,0:T(8,128)(2,1)S(1)}, u32[]{:S(2)}) copy-start(bf16[32,7296]{1,0:T(8,128)(2,1)S(1)} %collective-permute-done.6) | copy-start | bytes 1400836
  65.7 12.2 %collective-permute-start.7 = (bf16[32,7296]{1,0:T(8,128)(2,1)S(1)}, bf16[32,7296]{1,0:T(8,128)(2,1)S(1)}, u32[]{:S(2)}, u32[]{:S(2)}) collective-permute-start(bf16[32,7296]{1,0:T(8,128)(2,1)S(1)} %collective-permute-done.6), channel_id=1, source_target_pairs={{0,224},{32,0},{64,32},{96,64},{128,96},{160,128},{192,160},{224,1... | collective-permute-start | bytes 1400840 | tf_op jit(solution)/shard_map/ppermute | solution.py:124
  70.8 15.5 %copy-start.7 = (bf16[32,7296]{1,0:T(8,128)(2,1)}, bf16[32,7296]{1,0:T(8,128)(2,1)S(1)}, u32[]{:S(2)}) copy-start(bf16[32,7296]{1,0:T(8,128)(2,1)S(1)} %collective-permute-done.2) | copy-start | bytes 1400836
  70.8 12.3 %collective-permute-start.3 = (bf16[32,7296]{1,0:T(8,128)(2,1)S(1)}, bf16[32,7296]{1,0:T(8,128)(2,1)S(1)}, u32[]{:S(2)}, u32[]{:S(2)}) collective-permute-start(bf16[32,7296]{1,0:T(8,128)(2,1)S(1)} %collective-permute-done.2), channel_id=1, source_target_pairs={{0,32},{32,64},{64,96},{96,128},{128,160},{160,192},{192,224},{224... | collective-permute-start | bytes 1400840 | tf_op jit(solution)/shard_map/ppermute | solution.py:123
  78.0 8.6 %collective-permute-start.8 = (bf16[16,7296]{1,0:T(8,128)(2,1)S(1)}, bf16[16,7296]{1,0:T(8,128)(2,1)S(1)}, u32[]{:S(2)}, u32[]{:S(2)}) collective-permute-start(bf16[16,7296]{1,0:T(8,128)(2,1)S(1)} %slice.46), channel_id=1, source_target_pairs={{0,224},{32,0},{64,32},{96,64},{128,96},{160,128},{192,160},{224,1... | collective-permute-start | bytes 700424 | tf_op jit(solution)/shard_map/ppermute | solution.py:128
  83.1 2.0 %copy-start.2 = (bf16[32,7296]{1,0:T(8,128)(2,1)}, bf16[32,7296]{1,0:T(8,128)(2,1)S(1)}, u32[]{:S(2)}) copy-start(bf16[32,7296]{1,0:T(8,128)(2,1)S(1)} %collective-permute-done.3) | copy-start | bytes 1400836
  83.1 9.2 %collective-permute-start.4 = (bf16[16,7296]{1,0:T(8,128)(2,1)S(1)}, bf16[16,7296]{1,0:T(8,128)(2,1)S(1)}, u32[]{:S(2)}, u32[]{:S(2)}) collective-permute-start(bf16[16,7296]{1,0:T(8,128)(2,1)S(1)} %slice.45), channel_id=1, source_target_pairs={{0,32},{32,64},{64,96},{96,128},{128,160},{160,192},{192,224},{224... | collective-permute-start | bytes 700424 | tf_op jit(solution)/shard_map/ppermute | solution.py:128
  92.3 0.8 copy-start.8
  93.1 8.4 %copy-start = (bf16[1,2048,448]{1,2,0:T(8,128)(2,1)S(1)}, bf16[1,2048,448]{1,2,0:T(8,128)(2,1)}, u32[]{:S(2)}) copy-start(bf16[1,2048,448]{1,2,0:T(8,128)(2,1)} %param.9) | copy-start | bytes 5505028
  94.2 29.0 %all-to-all-start.1 = ((bf16[8,256,256]{2,1,0:T(8,128)(2,1)}), bf16[8,256,256]{2,1,0:T(8,128)(2,1)S(1)}, u32[]{:S(2)}, u32[]{:S(2)}) async-start(bf16[8,256,256]{2,1,0:T(8,128)(2,1)} %broadcast_in_dim.2), calls=%async_computation.1 | async-start | bytes 2097152 | tf_op jit(solution)/shard_map/all_to_all | solution.py:136
  101.5 21.7 %collective-permute-start.9 = (bf16[448,2048]{1,0:T(8,128)(2,1)S(1)}, bf16[448,2048]{1,0:T(8,128)(2,1)}, u32[]{:S(2)}, u32[]{:S(2)}) collective-permute-start(bf16[448,2048]{1,0:T(8,128)(2,1)S(1)} %bitcast.19), channel_id=1, source_target_pairs={{0,256},{256,0},{1,257},{257,1},{2,258},{258,2},{3,259},{259,3},{4... | collective-permute-start | bytes 5505032 | tf_op jit(solution)/shard_map/ppermute | solution.py:36

commit v9 on v8

--- a/solution.py
+++ b/solution.py
@@ -34,6 +34,16 @@
 
 def from_other_core(own):
     return lax.ppermute(own, "side", [(0, 1), (1, 0)])
+
+
+def hidden_kernel(first_ref, second_ref, near_ref, slab_ref, out_ref):
+    block = jnp.concatenate([first_ref[...], second_ref[...]], axis=0)
+    gate = jnp.dot(block, slab_ref[...], preferred_element_type=jnp.float32)
+    far = jax.nn.silu(gate).astype(jnp.bfloat16)
+    near = near_ref[...]
+    for g in range(out_ref.shape[0]):
+        out_ref[g, : near.shape[0]] = near
+        out_ref[g, near.shape[0] :] = far
 
 
 def down_kernel(n_grp, n_side, unit, rows, order, where_ref, own_ref, other_ref, got_ref, *refs):
@@ -130,12 +140,16 @@
     below, above, product = lax.optimization_barrier((below, above, product))
     blocks[far] = jnp.concatenate([below, above], axis=0)
     order.append(far)
-    hidden = jnp.concatenate([product, silu_gate([blocks[far]])], axis=0)
+    hidden = pl.pallas_call(
+        hidden_kernel,
+        out_shape=jax.ShapeDtypeStruct((n_grp, n_grp * CAP, n_side * unit), bf16),
+        in_specs=[vmem] * 4,
+        out_specs=vmem,
+        compiler_params=pltpu.CompilerParams(vmem_limit_bytes=16 * 2**20),
+    )(below, above, product, gate_slab)
     hidden, own_down = lax.optimization_barrier((hidden, own_down))
     other_down = from_other_core(own_down)
-    got = lax.all_to_all(
-        jnp.broadcast_to(hidden[None], (n_grp,) + hidden.shape), "grp", split_axis=0, concat_axis=0, tiled=True
-    )
+    got = lax.all_to_all(hidden, "grp", split_axis=0, concat_axis=0, tiled=True)
 
     slots = n_grp * CAP
     columns = n_side * own_down.shape[0]

time: 160 us -> 160 us (level)
  other arithmetic: 2.39 us -> 4.2 us
  Pallas kernels: 4.92 us -> 6.7 us
  waiting for transfers between devices: 50.6 us -> 48.9 us
    ppermute x3, waiting for transfers between devices: 16.5 us -> 14.7 us  [on_device(): above = lax.ppermute(above, 'grp', down)]
    concatenate x1 -> x2, other arithmetic: 0.01 us -> 1.82 us  [the longest x1 1.82 us: on_device(): gate_slab = jnp.pad(jnp.concatenate(both, axis=1), ((0, TAIL), (0, 0)))]
    pallas_call x0 -> x1, Pallas kernels: none -> 1.78 us  [on_device(): pl.pallas_call(hidden_kernel, out_shape=jax.ShapeDtypeStruct((n_grp, n_gr...]
    slice x8 -> x7, local copies, waits for them, and re-layouts: 4.89 us -> 4.89 us  [on_device(): blocks[d][:, width:]]
  transfers between devices with their start and end apart: 12 -> 12, of which waited for: 10 -> 10; matrix products, arithmetic and copies ran while one was open for 5% -> 6% of each run, Pallas kernels for 1% -> 1%
where the time goes in v9:
time: 160 us; the launch traced here: 159 us
  waiting for transfers between devices  48.9 us (31%)
  starting transfers between devices  45.7 us (29%)
  blocking collectives  45.6 us (28%)
  Pallas kernels  6.7 us (4%)
  local copies, waits for them, and re-layouts  6.21 us (4%)
  other arithmetic  4.2 us (3%)
    all_to_all x1, blocking collectives, on_device(): lax.all_to_all(total_x.reshape(n_z * n_grp, rows, -1), ('z', 'grp'), spli...  17.6 us
    all_to_all x1, waiting for transfers between devices, on_device(): got = lax.all_to_all(hidden, 'grp', split_axis=0, concat_axis=0, tiled=True)  14.8 us
    ppermute x3, waiting for transfers between devices, on_device(): above = lax.ppermute(above, 'grp', down)  14.7 us
    all_gather x1, blocking collectives, on_device(): packed = lax.all_gather(by_z, 'x', axis=0, tiled=True)  14.3 us
    all_to_all x1, blocking collectives, on_device(): lax.all_to_all(weighted.reshape(n_x, n_z * n_grp * rows, -1), 'x', split_...  13.8 us
    all_to_all x1, waiting for transfers between devices, on_device(): lax.all_to_all(copies, 'z', split_axis=0, concat_axis=0, tiled=True)  11.9 us
    all_to_all x1, starting transfers between devices, on_device(): lax.all_to_all(copies, 'z', split_axis=0, concat_axis=0, tiled=True)  10.3 us
    ppermute x3, starting transfers between devices, on_device(): above = lax.ppermute(above, 'grp', down)  10.2 us
  transfers between devices with their start and end apart: 12, of which 10 were waited for; matrix products, arithmetic and copies ran while one was open for 6% of the time, Pallas kernels for 1%

profile of v9, /device:TPU:8, one launch (start us, length us, event | category | flops | bytes accessed | tf_op | source)
XLA Modules:
  0.0 158.9 jit_solution(13652917358706415340)
XLA Ops:
  0.0 2.0 %collective-permute-start = (bf16[7168,128]{1,0:T(8,128)(2,1)}, bf16[7168,128]{1,0:T(8,128)(2,1)}, u32[]{:S(2)}, u32[]{:S(2)}) collective-permute-start(bf16[7168,128]{1,0:T(8,128)(2,1)} %bitcast.21), channel_id=1, source_target_pairs={{0,256},{256,0},{1,257},{257,1},{2,258},{258,2},{3,259},{259,3},{4... | collective-permute-start | bytes 5505032 | tf_op jit(solution)/shard_map/ppermute | solution.py:36
  2.1 1.7 %shard_map.55 = bf16[8,2,7296]{2,1,0:T(2,128)(2,1)} custom-call(s32[1]{0:T(128)} %bitcast.1.dev_ref, bf16[2,7168]{1,0:T(2,128)(2,1)} %tokens_ref.1, s32[2,8]{1,0:T(2,128)} %ids_ref.1, bf16[2,8]{1,0:T(2,128)(2,1)} %weights_ref.1), custom_call_target="tpu_custom_call" | custom-call | tf_op jit(solution)/shard_map/pallas_call | solution.py:103
  3.7 10.3 %all-to-all-start = ((bf16[8,2,7296]{2,1,0:T(2,128)(2,1)}), bf16[8,2,7296]{2,1,0:T(2,128)(2,1)S(1)}, u32[]{:S(2)}, u32[]{:S(2)}) async-start(bf16[8,2,7296]{2,1,0:T(2,128)(2,1)} %shard_map.55), calls=%async_computation | async-start | bytes 466944 | tf_op jit(solution)/shard_map/all_to_all | solution.py:109
  14.0 11.9 %all-to-all-done = bf16[8,2,7296]{2,1,0:T(2,128)(2,1)S(1)} async-done(((bf16[8,2,7296]{2,1,0:T(2,128)(2,1)}), bf16[8,2,7296]{2,1,0:T(2,128)(2,1)S(1)}, u32[]{:S(2)}, u32[]{:S(2)}) %all-to-all-start) | async-done | bytes 233504 | tf_op jit(solution)/shard_map/all_to_all | solution.py:109
  26.0 0.1 reshape.22
  26.1 14.3 %all_gather.3 = bf16[64,7296]{1,0:T(8,128)(2,1)S(1)} all-gather(bf16[16,7296]{1,0:T(8,128)(2,1)S(1)} %reshape.22), channel_id=1, replica_groups=mesh['side'=2,'grp'=8,'x'=4,'z'=8] {'x'}, dimensions={0}, use_global_device_ids=true | all-gather | bytes 1167360 | tf_op jit(solution)/shard_map/all_gather | solution.py:111
  40.3 0.1 fusion.4
  40.4 0.1 convert_reduce_fusion
  40.5 0.3 constant_dynamic-update-slice_fusion.6
  40.8 2.4 %collective-permute-start.5 = (bf16[32,7296]{1,0:T(8,128)(2,1)S(1)}, bf16[32,7296]{1,0:T(8,128)(2,1)S(1)}, u32[]{:S(2)}, u32[]{:S(2)}) collective-permute-start(bf16[32,7296]{1,0:T(8,128)(2,1)S(1)} %get-tuple-element.22), channel_id=1, source_target_pairs={{0,224},{32,0},{64,32},{96,64},{128,96},{160,128},{192,160},{224,1... | collective-permute-start | bytes 1400840 | tf_op jit(solution)/shard_map/ppermute | solution.py:134
  43.2 3.5 %collective-permute-start.1 = (bf16[32,7296]{1,0:T(8,128)(2,1)S(1)}, bf16[32,7296]{1,0:T(8,128)(2,1)S(1)}, u32[]{:S(2)}, u32[]{:S(2)}) collective-permute-start(bf16[32,7296]{1,0:T(8,128)(2,1)S(1)} %get-tuple-element.22), channel_id=1, source_target_pairs={{0,32},{32,64},{64,96},{96,128},{128,160},{160,192},{192,224},{224... | collective-permute-start | bytes 1400840 | tf_op jit(solution)/shard_map/ppermute | solution.py:133
  46.7 1.7 %broadcast_select_fusion.1 = (bf16[7168,128]{1,0:T(8,128)(2,1)S(1)}, bf16[7168,128]{1,0:T(8,128)(2,1)S(1)}) fusion(bf16[7168,128]{1,0:T(8,128)(2,1)} %collective-permute-done, pred[]{:T(512)S(6)} %eq.28, bf16[1,7168,128]{2,1,0:T(8,128)(2,1)S(1)} %copy-done.1), kind=kLoop, calls=%fused_computation.6 | loop fusion | flops 1835008 | bytes 7340033 | tf_op jit(solution)/shard_map/jit(_where)/select_n | solution.py:120
  48.5 1.8 %fusion.2.slab_ref = bf16[7296,256]{1,0:T(8,128)(2,1)S(1)} fusion(bf16[7168,128]{1,0:T(8,128)(2,1)S(1)} %get-tuple-element.20, bf16[7168,128]{1,0:T(8,128)(2,1)S(1)} %get-tuple-element.19), kind=kLoop, calls=%fused_computation.4 | loop fusion | flops 13074432 | bytes 7405568 | tf_op jit(solution)/shard_map/concatenate | solution.py:121
  50.3 3.5 %collective-permute-done.5 = bf16[32,7296]{1,0:T(8,128)(2,1)S(1)} collective-permute-done((bf16[32,7296]{1,0:T(8,128)(2,1)S(1)}, bf16[32,7296]{1,0:T(8,128)(2,1)S(1)}, u32[]{:S(2)}, u32[]{:S(2)}) %collective-permute-start.5) | collective-permute-done | bytes 466976 | tf_op jit(solution)/shard_map/ppermute | solution.py:134
  53.8 3.3 %collective-permute-start.6 = (bf16[32,7296]{1,0:T(8,128)(2,1)S(1)}, bf16[32,7296]{1,0:T(8,128)(2,1)S(1)}, u32[]{:S(2)}, u32[]{:S(2)}) collective-permute-start(bf16[32,7296]{1,0:T(8,128)(2,1)S(1)} %collective-permute-done.5), channel_id=1, source_target_pairs={{0,224},{32,0},{64,32},{96,64},{128,96},{160,128},{192,160},{224,1... | collective-permute-start | bytes 1400840 | tf_op jit(solution)/shard_map/ppermute | solution.py:134
  57.1 0.5 collective-permute-done.1
  57.6 2.0 %collective-permute-start.2 = (bf16[32,7296]{1,0:T(8,128)(2,1)S(1)}, bf16[32,7296]{1,0:T(8,128)(2,1)S(1)}, u32[]{:S(2)}, u32[]{:S(2)}) collective-permute-start(bf16[32,7296]{1,0:T(8,128)(2,1)S(1)} %collective-permute-done.1), channel_id=1, source_target_pairs={{0,32},{32,64},{64,96},{96,128},{128,160},{160,192},{192,224},{224... | collective-permute-start | bytes 1400840 | tf_op jit(solution)/shard_map/ppermute | solution.py:133
  59.7 6.0 %collective-permute-done.6 = bf16[32,7296]{1,0:T(8,128)(2,1)S(1)} collective-permute-done((bf16[32,7296]{1,0:T(8,128)(2,1)S(1)}, bf16[32,7296]{1,0:T(8,128)(2,1)S(1)}, u32[]{:S(2)}, u32[]{:S(2)}) %collective-permute-start.6) | collective-permute-done | bytes 466976 | tf_op jit(solution)/shard_map/ppermute | solution.py:134
  65.7 4.5 %collective-permute-start.7 = (bf16[32,7296]{1,0:T(8,128)(2,1)S(1)}, bf16[32,7296]{1,0:T(8,128)(2,1)S(1)}, u32[]{:S(2)}, u32[]{:S(2)}) collective-permute-start(bf16[32,7296]{1,0:T(8,128)(2,1)S(1)} %collective-permute-done.6), channel_id=1, source_target_pairs={{0,224},{32,0},{64,32},{96,64},{128,96},{160,128},{192,160},{224,1... | collective-permute-start | bytes 1400840 | tf_op jit(solution)/shard_map/ppermute | solution.py:134
  70.3 0.5 collective-permute-done.2
  70.8 1.9 %collective-permute-start.3 = (bf16[32,7296]{1,0:T(8,128)(2,1)S(1)}, bf16[32,7296]{1,0:T(8,128)(2,1)S(1)}, u32[]{:S(2)}, u32[]{:S(2)}) collective-permute-start(bf16[32,7296]{1,0:T(8,128)(2,1)S(1)} %collective-permute-done.2), channel_id=1, source_target_pairs={{0,32},{32,64},{64,96},{96,128},{128,160},{160,192},{192,224},{224... | collective-permute-start | bytes 1400840 | tf_op jit(solution)/shard_map/ppermute | solution.py:133
  72.8 5.2 %collective-permute-done.7 = bf16[32,7296]{1,0:T(8,128)(2,1)S(1)} collective-permute-done((bf16[32,7296]{1,0:T(8,128)(2,1)S(1)}, bf16[32,7296]{1,0:T(8,128)(2,1)S(1)}, u32[]{:S(2)}, u32[]{:S(2)}) %collective-permute-start.7) | collective-permute-done | bytes 466976 | tf_op jit(solution)/shard_map/ppermute | solution.py:134
  78.0 4.6 %collective-permute-start.8 = (bf16[16,7296]{1,0:T(8,128)(2,1)S(1)}, bf16[16,7296]{1,0:T(8,128)(2,1)S(1)}, u32[]{:S(2)}, u32[]{:S(2)}) collective-permute-start(bf16[16,7296]{1,0:T(8,128)(2,1)S(1)} %slice.46), channel_id=1, source_target_pairs={{0,224},{32,0},{64,32},{96,64},{128,96},{160,128},{192,160},{224,1... | collective-permute-start | bytes 700424 | tf_op jit(solution)/shard_map/ppermute | solution.py:138
  82.6 0.5 collective-permute-done.3
  83.1 1.9 %collective-permute-start.4 = (bf16[16,7296]{1,0:T(8,128)(2,1)S(1)}, bf16[16,7296]{1,0:T(8,128)(2,1)S(1)}, u32[]{:S(2)}, u32[]{:S(2)}) collective-permute-start(bf16[16,7296]{1,0:T(8,128)(2,1)S(1)} %slice.45), channel_id=1, source_target_pairs={{0,32},{32,64},{64,96},{96,128},{128,160},{160,192},{192,224},{224... | collective-permute-start | bytes 700424 | tf_op jit(solution)/shard_map/ppermute | solution.py:138
  85.1 1.0 multiply_convert_fusion.near_ref
  86.2 0.4 collective-permute-done.8.second_ref
  86.6 5.7 %collective-permute-done.4.first_ref = bf16[16,7296]{1,0:T(8,128)(2,1)S(1)} collective-permute-done((bf16[16,7296]{1,0:T(8,128)(2,1)S(1)}, bf16[16,7296]{1,0:T(8,128)(2,1)S(1)}, u32[]{:S(2)}, u32[]{:S(2)}) %collective-permute-start.4) | collective-permute-done | bytes 233504 | tf_op jit(solution)/shard_map/ppermute | solution.py:138
  92.3 1.8 %shard_map.56 = bf16[8,256,256]{2,1,0:T(8,128)(2,1)} custom-call(bf16[16,7296]{1,0:T(8,128)(2,1)S(1)} %collective-permute-done.4.first_ref, bf16[16,7296]{1,0:T(8,128)(2,1)S(1)} %collective-permute-done.8.second_ref, bf16[224,256]{1,0:T(8,128)(2,1)S(1)} %multiply_convert_fusion.near_ref, bf16[7296,256]{1,0:T(8,128)(2,1)S(1)} %fusion.2.slab_ref), custom_call_target="tpu_custom_call" | custom-call | tf_op jit(solution)/shard_map/pallas_call | solution.py:143
  94.1 7.3 %all-to-all-start.1 = ((bf16[8,256,256]{2,1,0:T(8,128)(2,1)}), bf16[8,256,256]{2,1,0:T(8,128)(2,1)S(1)}, u32[]{:S(2)}, u32[]{:S(2)}) async-start(bf16[8,256,256]{2,1,0:T(8,128)(2,1)} %shard_map.56), calls=%async_computation.1 | async-start | bytes 2097152 | tf_op jit(solution)/shard_map/all_to_all | solution.py:152
  101.4 1.9 %collective-permute-start.9 = (bf16[448,2048]{1,0:T(8,128)(2,1)S(1)}, bf16[448,2048]{1,0:T(8,128)(2,1)}, u32[]{:S(2)}, u32[]{:S(2)}) collective-permute-start(bf16[448,2048]{1,0:T(8,128)(2,1)S(1)} %bitcast.19), channel_id=1, source_target_pairs={{0,256},{256,0},{1,257},{257,1},{2,258},{258,2},{3,259},{259,3},{4... | collective-permute-start | bytes 5505032 | tf_op jit(solution)/shard_map/ppermute | solution.py:36
  103.3 0.1 pad_add_fusion.where_ref
  103.4 0.7 slice.47.refs_0_
  104.1 0.7 slice.48.refs_1_
  104.8 0.7 slice.53.refs_7_
  105.5 0.7 slice.49.refs_2_
  106.1 0.7 slice.52.refs_6_
  106.8 0.7 slice.50.refs_3_
  107.5 0.7 slice.51.refs_5_
  108.3 14.8 %all-to-all-done.1.got_ref = bf16[8,256,256]{2,1,0:T(8,128)(2,1)S(1)} async-done(((bf16[8,256,256]{2,1,0:T(8,128)(2,1)}), bf16[8,256,256]{2,1,0:T(8,128)(2,1)S(1)}, u32[]{:S(2)}, u32[]{:S(2)}) %all-to-all-start.1) | async-done | bytes 1048608 | tf_op jit(solution)/shard_map/all_to_all | solution.py:152
  123.0 3.3 %shard_map.57 = bf16[512,896]{1,0:T(8,128)(2,1)S(1)} custom-call(s32[3]{0:T(128)S(1)} %pad_add_fusion.where_ref, bf16[448,2048]{1,0:T(8,128)(2,1)S(1)} %bitcast.20, bf16[448,2048]{1,0:T(8,128)(2,1)} %collective-permute-done.9.other_ref, bf16[8,256,256]{2,1,0:T(8,128)(2,1)S(1)} %all-to-all-done.1.got_ref, bf16[32,128]{1,0:T(8,128)(2,1)S(1)} %slice.47.refs_0_, ...), custom_call_target="tpu_custom_call" | custom-call | tf_op jit(solution)/shard_map/pallas_call | solution.py:156
  126.3 13.8 %all_to_all.20 = bf16[4,128,896]{2,1,0:T(8,128)(2,1)S(1)} all-to-all(bf16[4,128,896]{2,1,0:T(8,128)(2,1)S(1)} %bitcast.18), channel_id=1, replica_groups=mesh['side'=2,'grp'=8,'x'=4,'z'=8] {'x'}, dimensions={0} | all-to-all | bytes 1835008 | tf_op jit(solution)/shard_map/all_to_all | solution.py:173
  140.1 0.1 reduce_sum.34
  140.2 0.1 reshape.24
  140.3 17.6 %all_to_all.21 = bf16[64,2,896]{2,1,0:T(2,128)(2,1)S(1)} all-to-all(bf16[64,2,896]{2,1,0:T(2,128)(2,1)S(1)} %reshape.24), channel_id=1, replica_groups=mesh['side'=2,'grp'=8,'x'=4,'z'=8] {'z','grp'}, dimensions={0} | all-to-all | bytes 458752 | tf_op jit(solution)/shard_map/all_to_all | solution.py:177
  157.9 0.2 reduce_sum.35
  158.1 0.1 reshape.28
  158.2 0.7 reshape.27
  (30 shorter events, 0.3 us)
Async XLA Ops:
  0.0 46.7 %copy-start.1 = (bf16[1,7168,128]{2,1,0:T(8,128)(2,1)S(1)}, bf16[1,7168,128]{2,1,0:T(8,128)(2,1)}, u32[]{:S(2)}) copy-start(bf16[1,7168,128]{2,1,0:T(8,128)(2,1)} %param.8) | copy-start | bytes 5505028
  0.0 26.0 %collective-permute-start = (bf16[7168,128]{1,0:T(8,128)(2,1)}, bf16[7168,128]{1,0:T(8,128)(2,1)}, u32[]{:S(2)}, u32[]{:S(2)}) collective-permute-start(bf16[7168,128]{1,0:T(8,128)(2,1)} %bitcast.21), channel_id=1, source_target_pairs={{0,256},{256,0},{1,257},{257,1},{2,258},{258,2},{3,259},{259,3},{4... | collective-permute-start | bytes 5505032 | tf_op jit(solution)/shard_map/ppermute | solution.py:36
  3.7 22.2 %all-to-all-start = ((bf16[8,2,7296]{2,1,0:T(2,128)(2,1)}), bf16[8,2,7296]{2,1,0:T(2,128)(2,1)S(1)}, u32[]{:S(2)}, u32[]{:S(2)}) async-start(bf16[8,2,7296]{2,1,0:T(2,128)(2,1)} %shard_map.55), calls=%async_computation | async-start | bytes 466944 | tf_op jit(solution)/shard_map/all_to_all | solution.py:109
  40.8 7.6 %copy-start.4 = (bf16[32,7296]{1,0:T(8,128)(2,1)}, bf16[32,7296]{1,0:T(8,128)(2,1)S(1)}, u32[]{:S(2)}) copy-start(bf16[32,7296]{1,0:T(8,128)(2,1)S(1)} %get-tuple-element.22) | copy-start | bytes 1400836
  40.8 12.9 %collective-permute-start.5 = (bf16[32,7296]{1,0:T(8,128)(2,1)S(1)}, bf16[32,7296]{1,0:T(8,128)(2,1)S(1)}, u32[]{:S(2)}, u32[]{:S(2)}) collective-permute-start(bf16[32,7296]{1,0:T(8,128)(2,1)S(1)} %get-tuple-element.22), channel_id=1, source_target_pairs={{0,224},{32,0},{64,32},{96,64},{128,96},{160,128},{192,160},{224,1... | collective-permute-start | bytes 1400840 | tf_op jit(solution)/shard_map/ppermute | solution.py:134
  43.2 14.4 %collective-permute-start.1 = (bf16[32,7296]{1,0:T(8,128)(2,1)S(1)}, bf16[32,7296]{1,0:T(8,128)(2,1)S(1)}, u32[]{:S(2)}, u32[]{:S(2)}) collective-permute-start(bf16[32,7296]{1,0:T(8,128)(2,1)S(1)} %get-tuple-element.22), channel_id=1, source_target_pairs={{0,32},{32,64},{64,96},{96,128},{128,160},{160,192},{192,224},{224... | collective-permute-start | bytes 1400840 | tf_op jit(solution)/shard_map/ppermute | solution.py:133
  53.8 31.4 %copy-start.5 = (bf16[32,7296]{1,0:T(8,128)(2,1)}, bf16[32,7296]{1,0:T(8,128)(2,1)S(1)}, u32[]{:S(2)}) copy-start(bf16[32,7296]{1,0:T(8,128)(2,1)S(1)} %collective-permute-done.5) | copy-start | bytes 1400836
  53.8 12.0 %collective-permute-start.6 = (bf16[32,7296]{1,0:T(8,128)(2,1)S(1)}, bf16[32,7296]{1,0:T(8,128)(2,1)S(1)}, u32[]{:S(2)}, u32[]{:S(2)}) collective-permute-start(bf16[32,7296]{1,0:T(8,128)(2,1)S(1)} %collective-permute-done.5), channel_id=1, source_target_pairs={{0,224},{32,0},{64,32},{96,64},{128,96},{160,128},{192,160},{224,1... | collective-permute-start | bytes 1400840 | tf_op jit(solution)/shard_map/ppermute | solution.py:134
  57.6 27.6 %copy-start.6 = (bf16[32,7296]{1,0:T(8,128)(2,1)}, bf16[32,7296]{1,0:T(8,128)(2,1)S(1)}, u32[]{:S(2)}) copy-start(bf16[32,7296]{1,0:T(8,128)(2,1)S(1)} %collective-permute-done.1) | copy-start | bytes 1400836
  57.6 13.2 %collective-permute-start.2 = (bf16[32,7296]{1,0:T(8,128)(2,1)S(1)}, bf16[32,7296]{1,0:T(8,128)(2,1)S(1)}, u32[]{:S(2)}, u32[]{:S(2)}) collective-permute-start(bf16[32,7296]{1,0:T(8,128)(2,1)S(1)} %collective-permute-done.1), channel_id=1, source_target_pairs={{0,32},{32,64},{64,96},{96,128},{128,160},{160,192},{192,224},{224... | collective-permute-start | bytes 1400840 | tf_op jit(solution)/shard_map/ppermute | solution.py:133
  65.7 20.5 %copy-start.7 = (bf16[32,7296]{1,0:T(8,128)(2,1)}, bf16[32,7296]{1,0:T(8,128)(2,1)S(1)}, u32[]{:S(2)}) copy-start(bf16[32,7296]{1,0:T(8,128)(2,1)S(1)} %collective-permute-done.6) | copy-start | bytes 1400836
  65.7 12.2 %collective-permute-start.7 = (bf16[32,7296]{1,0:T(8,128)(2,1)S(1)}, bf16[32,7296]{1,0:T(8,128)(2,1)S(1)}, u32[]{:S(2)}, u32[]{:S(2)}) collective-permute-start(bf16[32,7296]{1,0:T(8,128)(2,1)S(1)} %collective-permute-done.6), channel_id=1, source_target_pairs={{0,224},{32,0},{64,32},{96,64},{128,96},{160,128},{192,160},{224,1... | collective-permute-start | bytes 1400840 | tf_op jit(solution)/shard_map/ppermute | solution.py:134
  70.8 15.4 %copy-start.8 = (bf16[32,7296]{1,0:T(8,128)(2,1)}, bf16[32,7296]{1,0:T(8,128)(2,1)S(1)}, u32[]{:S(2)}) copy-start(bf16[32,7296]{1,0:T(8,128)(2,1)S(1)} %collective-permute-done.2) | copy-start | bytes 1400836
  70.8 12.3 %collective-permute-start.3 = (bf16[32,7296]{1,0:T(8,128)(2,1)S(1)}, bf16[32,7296]{1,0:T(8,128)(2,1)S(1)}, u32[]{:S(2)}, u32[]{:S(2)}) collective-permute-start(bf16[32,7296]{1,0:T(8,128)(2,1)S(1)} %collective-permute-done.2), channel_id=1, source_target_pairs={{0,32},{32,64},{64,96},{96,128},{128,160},{160,192},{192,224},{224... | collective-permute-start | bytes 1400840 | tf_op jit(solution)/shard_map/ppermute | solution.py:133
  78.0 7.1 %copy-start.2 = (bf16[32,7296]{1,0:T(8,128)(2,1)}, bf16[32,7296]{1,0:T(8,128)(2,1)S(1)}, u32[]{:S(2)}) copy-start(bf16[32,7296]{1,0:T(8,128)(2,1)S(1)} %collective-permute-done.7) | copy-start | bytes 1400836
  78.0 8.6 %collective-permute-start.8 = (bf16[16,7296]{1,0:T(8,128)(2,1)S(1)}, bf16[16,7296]{1,0:T(8,128)(2,1)S(1)}, u32[]{:S(2)}, u32[]{:S(2)}) collective-permute-start(bf16[16,7296]{1,0:T(8,128)(2,1)S(1)} %slice.46), channel_id=1, source_target_pairs={{0,224},{32,0},{64,32},{96,64},{128,96},{160,128},{192,160},{224,1... | collective-permute-start | bytes 700424 | tf_op jit(solution)/shard_map/ppermute | solution.py:138
  83.1 2.0 %copy-start.3 = (bf16[32,7296]{1,0:T(8,128)(2,1)}, bf16[32,7296]{1,0:T(8,128)(2,1)S(1)}, u32[]{:S(2)}) copy-start(bf16[32,7296]{1,0:T(8,128)(2,1)S(1)} %collective-permute-done.3) | copy-start | bytes 1400836
  83.1 9.2 %collective-permute-start.4 = (bf16[16,7296]{1,0:T(8,128)(2,1)S(1)}, bf16[16,7296]{1,0:T(8,128)(2,1)S(1)}, u32[]{:S(2)}, u32[]{:S(2)}) collective-permute-start(bf16[16,7296]{1,0:T(8,128)(2,1)S(1)} %slice.45), channel_id=1, source_target_pairs={{0,32},{32,64},{64,96},{96,128},{128,160},{160,192},{192,224},{224... | collective-permute-start | bytes 700424 | tf_op jit(solution)/shard_map/ppermute | solution.py:138
  86.2 15.1 %copy-start = (bf16[1,2048,448]{1,2,0:T(8,128)(2,1)S(1)}, bf16[1,2048,448]{1,2,0:T(8,128)(2,1)}, u32[]{:S(2)}) copy-start(bf16[1,2048,448]{1,2,0:T(8,128)(2,1)} %param.9) | copy-start | bytes 5505028
  94.1 29.0 %all-to-all-start.1 = ((bf16[8,256,256]{2,1,0:T(8,128)(2,1)}), bf16[8,256,256]{2,1,0:T(8,128)(2,1)S(1)}, u32[]{:S(2)}, u32[]{:S(2)}) async-start(bf16[8,256,256]{2,1,0:T(8,128)(2,1)} %shard_map.56), calls=%async_computation.1 | async-start | bytes 2097152 | tf_op jit(solution)/shard_map/all_to_all | solution.py:152
  101.4 21.7 %collective-permute-start.9 = (bf16[448,2048]{1,0:T(8,128)(2,1)S(1)}, bf16[448,2048]{1,0:T(8,128)(2,1)}, u32[]{:S(2)}, u32[]{:S(2)}) collective-permute-start(bf16[448,2048]{1,0:T(8,128)(2,1)S(1)} %bitcast.19), channel_id=1, source_target_pairs={{0,256},{256,0},{1,257},{257,1},{2,258},{258,2},{3,259},{259,3},{4... | collective-permute-start | bytes 5505032 | tf_op jit(solution)/shard_map/ppermute | solution.py:36
